TPU v7x, 32 devices: a whole 2x2x4 slice. The times are simulated.
32 devices in a mesh: member: 2 (over x), dom: 16 (over z, y, core).
Axes of the slice: x: 2, y: 2, z: 4, core: 2. Of those that a mesh axis runs over, the one named last changes fastest.
Arguments:
- node_latent: bfloat16 [16384, 512], P(('member', 'dom')), parts along dimension 0, may hold values from -6 to 6
- edge_latent: bfloat16 [81920, 512], P(('member', 'dom')), parts along dimension 0, may hold values from -6 to 6
- node_cotan: bfloat16 [16384, 512], P(('member', 'dom')), parts along dimension 0, may hold values from -6 to 6
- edge_cotan: bfloat16 [81920, 512], P(('member', 'dom')), parts along dimension 0, may hold values from -6 to 6
- edge_w1: bfloat16 [1536, 512], replicated, may hold values from -0.15625 to 0.15625
- edge_w2: bfloat16 [512, 512], replicated, may hold values from -0.25 to 0.25
- node_w1: bfloat16 [1024, 512], replicated, may hold values from -0.1875 to 0.1875
- node_w2: bfloat16 [512, 512], replicated, may hold values from -0.25 to 0.25
- send_rows: int32 [16, 16, 16], P('dom'), may hold values from 0 to 511, as said below
- senders: int32 [40960], P('dom'), may hold values from 0 to 767, as said below
- receivers: int32 [40960], P('dom'), may hold values from 0 to 511, as said below
- edge_count: int32 [16], P('dom'), may hold values from 640 to 2560, as said below
Outputs:
- grad_node: float32 [16384, 512], P(('member', 'dom')), parts along dimension 0
- grad_edge: bfloat16 [81920, 512], P(('member', 'dom')), parts along dimension 0
- edge_weight_grads: float32 [4096, 512], P(('member', 'dom')), parts along dimension 0
- node_weight_grads: float32 [3072, 512], P(('member', 'dom')), parts along dimension 0
There are 2 independent parts, one for each index of `member`. A program takes and returns all parts, laid end to end along the dimension named above; an argument that names none is the same for every part. Nothing has to cross between parts.
Inputs may be any that keep to these rules, and one draw needn't show every extreme that they name: `send_rows`: row of the sending partition's 512 nodes. `senders`: below 512: a node of the edge's own partition; else k - 512 names slot (k - 512) % 16 received from partition (k - 512) // 16. `receivers`: a node of the edge's own partition; non-decreasing within the rows of one partition. A partition's live edges are its first edge_count slots; some partition has all 2560 live.
All inputs are finite; a program needn't handle non-finite values.
Results may differ from a plain program's by a relative error of at most 0.0075.
Values may be sent and summed in bfloat16 or wider, within the bound.
No kernel may reach another device: no remote copies, remote signals or barrier semaphores. Data moves between devices by JAX's collectives and lax.ppermute only.
A program may use at most 128 MiB of HBM per device.

v0:
```python
import jax
import jax.numpy as jnp
from jax import lax
from jax.sharding import PartitionSpec as P


def swish_value(value):
    return value * jax.nn.sigmoid(value)


def swish_slope(value):
    sig = jax.nn.sigmoid(value)
    return sig * (1.0 + value * (1.0 - sig))


def normalize(mixed):
    centre = mixed - jnp.mean(mixed, -1, keepdims=True)
    inverse = lax.rsqrt(jnp.mean(centre * centre, -1, keepdims=True) + 1e-05)
    return (centre * inverse, inverse)


def norm_back(grad, normed, inverse):
    return inverse * (
        grad
        - jnp.mean(grad, -1, keepdims=True)
        - normed * jnp.mean(grad * normed, -1, keepdims=True)
    )


def product(left, right):
    return jnp.dot(left, right, preferred_element_type=jnp.float32)


def contract_rows(left, right):
    return lax.dot_general(
        left, right, (((0,), (0,)), ((), ())), preferred_element_type=jnp.float32
    )


def times_transpose(left, weight):
    return lax.dot_general(
        left, weight, (((1,), (1,)), ((), ())), preferred_element_type=jnp.float32
    )


def local(
    node_latent,
    edge_latent,
    node_cotan,
    edge_cotan,
    edge_w1,
    edge_w2,
    node_w1,
    node_w2,
    send_rows,
    senders,
    receivers,
    edge_count,
):
    node_count, latent_width = node_latent.shape
    edge_total = edge_latent.shape[0]
    rows_out = send_rows[0]
    peer_count, slot_count = rows_out.shape
    flat_rows = rows_out.reshape(-1)
    outgoing = jnp.take(node_latent, flat_rows, axis=0).reshape(
        peer_count, slot_count, latent_width
    )
    incoming = lax.all_to_all(outgoing, "dom", split_axis=0, concat_axis=0, tiled=True)
    node_table = jnp.concatenate(
        [node_latent, incoming.reshape(peer_count * slot_count, latent_width)], 0
    )
    table_rows = node_table.shape[0]
    w_send = edge_w1[:latent_width]
    w_recv = edge_w1[latent_width : 2 * latent_width]
    w_edge = edge_w1[2 * latent_width :]
    w_node = node_w1[:latent_width]
    w_agg = node_w1[latent_width:]
    block_rows = min(512, edge_total)
    total_blocks = edge_total // block_rows
    live_count = edge_count[0]
    node_iota = jnp.arange(node_count, dtype=jnp.int32)
    table_iota = jnp.arange(table_rows, dtype=jnp.int32)
    block_iota = jnp.arange(block_rows, dtype=jnp.int32)

    def edge_inputs(first_row):
        send_index = lax.dynamic_slice_in_dim(senders, first_row, block_rows)
        recv_index = lax.dynamic_slice_in_dim(receivers, first_row, block_rows)
        edge_block = lax.dynamic_slice_in_dim(edge_latent, first_row, block_rows, 0)
        send_x = jnp.take(node_table, send_index, axis=0)
        recv_x = jnp.take(node_latent, recv_index, axis=0)
        pick_recv = (recv_index[:, None] == node_iota[None, :]).astype(jnp.bfloat16)
        live_mask = (first_row + block_iota < live_count).astype(jnp.float32)[:, None]
        return (send_index, send_x, recv_x, edge_block, pick_recv, live_mask)

    def forward_block(turn_index, carry):
        gathered, preact_all, mixed_all = carry
        first_row = turn_index * block_rows
        send_index, send_x, recv_x, edge_block, pick_recv, live_mask = edge_inputs(first_row)
        preact = product(send_x, w_send) + product(recv_x, w_recv) + product(edge_block, w_edge)
        hidden = swish_value(preact).astype(jnp.bfloat16)
        mixed = product(hidden, edge_w2)
        normed, inverse = normalize(mixed)
        message = (live_mask * normed).astype(jnp.bfloat16)
        gathered = gathered + contract_rows(pick_recv, message)
        preact_all = lax.dynamic_update_slice_in_dim(preact_all, preact, first_row, 0)
        mixed_all = lax.dynamic_update_slice_in_dim(mixed_all, mixed, first_row, 0)
        return (gathered, preact_all, mixed_all)

    start_carry = (
        jnp.zeros((node_count, latent_width), jnp.float32),
        jnp.zeros((edge_total, latent_width), jnp.float32),
        jnp.zeros((edge_total, latent_width), jnp.float32),
    )
    gathered, preact_all, mixed_all = lax.fori_loop(0, total_blocks, forward_block, start_carry)
    gathered_low = gathered.astype(jnp.bfloat16)
    node_pre = product(node_latent, w_node) + product(gathered_low, w_agg)
    node_hidden = swish_value(node_pre).astype(jnp.bfloat16)
    node_normed, node_inv = normalize(product(node_hidden, node_w2))
    node_grad_out = norm_back(node_cotan.astype(jnp.float32), node_normed, node_inv).astype(
        jnp.bfloat16
    )
    node_grad_pre = (times_transpose(node_grad_out, node_w2) * swish_slope(node_pre)).astype(
        jnp.bfloat16
    )
    node_stack = jnp.concatenate(
        [
            contract_rows(node_latent, node_grad_pre),
            contract_rows(gathered_low, node_grad_pre),
            contract_rows(node_hidden, node_grad_out),
        ],
        0,
    )
    agg_grad = times_transpose(node_grad_pre, w_agg).astype(jnp.bfloat16)
    node_grad = node_cotan.astype(jnp.float32) + times_transpose(node_grad_pre, w_node)

    def backward_block(turn_index, carry):
        node_accum, table_accum, weight_accum, edge_result = carry
        first_row = turn_index * block_rows
        send_index, send_x, recv_x, edge_block, pick_recv, live_mask = edge_inputs(first_row)
        preact = lax.dynamic_slice_in_dim(preact_all, first_row, block_rows, 0)
        mixed = lax.dynamic_slice_in_dim(mixed_all, first_row, block_rows, 0)
        hidden = swish_value(preact).astype(jnp.bfloat16)
        normed, inverse = normalize(mixed)
        edge_cot_block = lax.dynamic_slice_in_dim(edge_cotan, first_row, block_rows, 0).astype(
            jnp.float32
        )
        grad_msg = live_mask * (edge_cot_block + product(pick_recv, agg_grad))
        grad_mixed = norm_back(grad_msg, normed, inverse).astype(jnp.bfloat16)
        grad_preact = (times_transpose(grad_mixed, edge_w2) * swish_slope(preact)).astype(
            jnp.bfloat16
        )
        weight_accum = weight_accum + jnp.concatenate(
            [
                contract_rows(send_x, grad_preact),
                contract_rows(recv_x, grad_preact),
                contract_rows(edge_block, grad_preact),
                contract_rows(hidden, grad_mixed),
            ],
            0,
        )
        new_edge = (edge_cot_block + times_transpose(grad_preact, w_edge)).astype(jnp.bfloat16)
        edge_result = lax.dynamic_update_slice_in_dim(edge_result, new_edge, first_row, 0)
        grad_send = times_transpose(grad_preact, w_send).astype(jnp.bfloat16)
        grad_recv = times_transpose(grad_preact, w_recv).astype(jnp.bfloat16)
        pick_send = (send_index[:, None] == table_iota[None, :]).astype(jnp.bfloat16)
        table_accum = table_accum + contract_rows(pick_send, grad_send)
        node_accum = node_accum + contract_rows(pick_recv, grad_recv)
        return (node_accum, table_accum, weight_accum, edge_result)

    back_carry = (
        node_grad,
        jnp.zeros((table_rows, latent_width), jnp.float32),
        jnp.zeros((4 * latent_width, latent_width), jnp.float32),
        edge_cotan,
    )
    node_accum, table_accum, edge_stack, grad_edge = lax.fori_loop(
        0, total_blocks, backward_block, back_carry
    )
    returned = lax.all_to_all(
        table_accum[node_count:].reshape(peer_count, slot_count, latent_width).astype(jnp.bfloat16),
        "dom",
        split_axis=0,
        concat_axis=0,
        tiled=True,
    ).astype(jnp.float32)
    grad_node = (
        node_accum
        + table_accum[:node_count]
        + jax.ops.segment_sum(
            returned.reshape(peer_count * slot_count, latent_width),
            flat_rows,
            num_segments=node_count,
        )
    )
    edge_share, node_share = (
        lax.psum_scatter(edge_stack, "dom", scatter_dimension=0, tiled=True),
        lax.psum_scatter(node_stack, "dom", scatter_dimension=0, tiled=True),
    )
    return (grad_node, grad_edge, edge_share, node_share)


def solution(mesh):
    placed = (
        P(("member", "dom"), None),
        P(("member", "dom"), None),
        P(("member", "dom"), None),
        P(("member", "dom"), None),
        P(),
        P(),
        P(),
        P(),
        P("dom", None, None),
        P("dom"),
        P("dom"),
        P("dom"),
    )
    return jax.shard_map(
        local,
        mesh=mesh,
        in_specs=placed,
        out_specs=(
            P(("member", "dom"), None),
            P(("member", "dom"), None),
            P(("member", "dom"), None),
            P(("member", "dom"), None),
        ),
        check_vma=False,
    )
```

profile of v0, /device:TPU:0, one launch (start us, length us, event | category | flops | bytes accessed | tf_op | source)
XLA Modules:
  0.0 414.2 jit_solution(18176680409211886845)
XLA Ops:
  11.9 7.4 %all-to-all-start = ((bf16[16,16,512]{2,1,0:T(8,128)(2,1)}), bf16[16,16,512]{2,1,0:T(8,128)(2,1)S(1)}, u32[]{:S(2)}, u32[]{:S(2)}) async-start(bf16[16,16,512]{2,1,0:T(8,128)(2,1)} %broadcast_select_fusion), calls=%async_computation | async-start | bytes 524288 | tf_op jit(solution)/shard_map/all_to_all | solution.py:68
  20.4 3.6 copy.64
  26.5 2.9 all-to-all-done
  29.4 3.0 broadcast.230
  32.4 3.0 broadcast.230.clone
  35.3 89.3 %while.42 = (s32[]{:T(128)}, f32[512,512]{1,0:T(8,128)}, f32[2560,512]{1,0:T(8,128)}, f32[2560,512]{0,1:T(8,128)}, s32[2560]{0:T(1024)}, /*index=5*/s32[]{:T(128...) while((s32[]{:T(128)}, f32[512,512]{1,0:T(8,128)}, ...), condition=%wide.region_3.6_spmd.clone.clone, body=%wide.region_0.5_spmd.clone.clone.sunk | while | flops 1347694080 | bytes 21552396 | solution.py:114
  36.1 2.6 gather_fusion
  41.9 2.6 gather_fusion.1
  53.0 2.6 gather_fusion
  58.7 2.6 gather_fusion.1
  63.1 2.5 constant_dynamic-update-slice_fusion.6
  67.5 2.9 convolution_add_fusion.11
  71.1 2.6 gather_fusion
  76.9 2.6 gather_fusion.1
  81.3 2.5 constant_dynamic-update-slice_fusion.6
  85.6 2.9 convolution_add_fusion.11
  89.2 2.6 gather_fusion
  95.0 2.6 gather_fusion.1
  99.3 2.5 constant_dynamic-update-slice_fusion.6
  103.6 2.9 convolution_add_fusion.11
  107.3 2.6 gather_fusion
  113.0 2.6 gather_fusion.1
  121.8 2.9 convolution_add_fusion.11
  136.4 200.3 %while.43 = (s32[]{:T(128)}, f32[512,512]{1,0:T(8,128)}, f32[768,512]{1,0:T(8,128)}, f32[2048,512]{1,0:T(8,128)}, bf16[2560,512]{1,0:T(8,128)(2,1)}, /*index=5*/...) while((s32[]{:T(128)}, f32[512,512]{1,0:T(8,128)}, ...), condition=%wide.region_13.16_spmd.clone.clone, body=%wide.region_8.15_spmd.clone.clone.sunk | while | flops 3104715776 | bytes 66669108 | solution.py:176
  157.7 2.8 fusion.160
  160.5 5.4 %maximum_add_fusion.2 = f32[2048,512]{1,0:T(8,128)} fusion(f32[512,512]{1,0:T(8,128)} %fusion.160, f32[512,512]{1,0:T(8,128)S(1)} %fusion.161, f32[512,512]{1,0:T(8,128)} %fusion.162, f32[512,512]{1,0:T(8,128)} %fusion.163, f32[2048,512]{1,0:T(8,128)} %get-tuple-element.1369, pred[]{:T(512)S(6)} %compare.7), kind=kLoop, calls=%fused_computation.47.clone.1 | loop fusion | flops 5242880 | bytes 12582913 | tf_op jit(solution)/shard_map/while/body/eval_jaxpr/add | solution.py:152
  169.3 3.2 select_add_fusion.2
  172.5 3.0 convolution_add_fusion.12
  196.7 2.8 fusion.160
  199.5 6.3 %maximum_add_fusion.2 = f32[2048,512]{1,0:T(8,128)} fusion(f32[512,512]{1,0:T(8,128)} %fusion.160, f32[512,512]{1,0:T(8,128)S(1)} %fusion.161, f32[512,512]{1,0:T(8,128)} %fusion.162, f32[512,512]{1,0:T(8,128)} %fusion.163, f32[2048,512]{1,0:T(8,128)} %get-tuple-element.1369, pred[]{:T(512)S(6)} %compare.7), kind=kLoop, calls=%fused_computation.47.clone.1 | loop fusion | flops 5242880 | bytes 12582913 | tf_op jit(solution)/shard_map/while/body/eval_jaxpr/add | solution.py:152
  209.2 3.8 select_add_fusion.2
  212.9 3.0 convolution_add_fusion.12
  237.0 2.8 fusion.160
  239.8 6.3 %maximum_add_fusion.2 = f32[2048,512]{1,0:T(8,128)} fusion(f32[512,512]{1,0:T(8,128)} %fusion.160, f32[512,512]{1,0:T(8,128)S(1)} %fusion.161, f32[512,512]{1,0:T(8,128)} %fusion.162, f32[512,512]{1,0:T(8,128)} %fusion.163, f32[2048,512]{1,0:T(8,128)} %get-tuple-element.1369, pred[]{:T(512)S(6)} %compare.7), kind=kLoop, calls=%fused_computation.47.clone.1 | loop fusion | flops 5242880 | bytes 12582913 | tf_op jit(solution)/shard_map/while/body/eval_jaxpr/add | solution.py:152
  249.5 3.8 select_add_fusion.2
  253.2 3.0 convolution_add_fusion.12
  277.3 2.8 fusion.160
  280.0 6.3 %maximum_add_fusion.2 = f32[2048,512]{1,0:T(8,128)} fusion(f32[512,512]{1,0:T(8,128)} %fusion.160, f32[512,512]{1,0:T(8,128)S(1)} %fusion.161, f32[512,512]{1,0:T(8,128)} %fusion.162, f32[512,512]{1,0:T(8,128)} %fusion.163, f32[2048,512]{1,0:T(8,128)} %get-tuple-element.1369, pred[]{:T(512)S(6)} %compare.7), kind=kLoop, calls=%fused_computation.47.clone.1 | loop fusion | flops 5242880 | bytes 12582913 | tf_op jit(solution)/shard_map/while/body/eval_jaxpr/add | solution.py:152
  289.7 3.8 select_add_fusion.2
  293.5 3.0 convolution_add_fusion.12
  317.5 2.8 fusion.160
  320.3 6.3 %maximum_add_fusion.2 = f32[2048,512]{1,0:T(8,128)} fusion(f32[512,512]{1,0:T(8,128)} %fusion.160, f32[512,512]{1,0:T(8,128)S(1)} %fusion.161, f32[512,512]{1,0:T(8,128)} %fusion.162, f32[512,512]{1,0:T(8,128)} %fusion.163, f32[2048,512]{1,0:T(8,128)} %get-tuple-element.1369, pred[]{:T(512)S(6)} %compare.7), kind=kLoop, calls=%fused_computation.47.clone.1 | loop fusion | flops 5242880 | bytes 12582913 | tf_op jit(solution)/shard_map/while/body/eval_jaxpr/add | solution.py:152
  330.0 3.8 select_add_fusion.2
  333.8 3.0 convolution_add_fusion.12
  338.7 3.5 all-to-all-start.1
  343.8 8.4 %all-to-all-done.1 = bf16[16,16,512]{2,1,0:T(8,128)(2,1)S(1)} async-done(((bf16[16,16,512]{2,1,0:T(8,128)(2,1)}), bf16[16,16,512]{2,1,0:T(8,128)(2,1)S(1)}, u32[]{:S(2)}, u32[]{:S(2)}) %all-to-all-start.1) | async-done | bytes 262176 | tf_op jit(solution)/shard_map/all_to_all | solution.py:179
  352.2 2.5 scatter_custom_fusion
  354.8 52.6 %reduce-scatter.3.cloned.1.call-done = f32[128,512]{1,0:T(8,128)} async-done(((f32[2048,512]{1,0:T(8,128)}), f32[128,512]{1,0:T(8,128)}) %reduce-scatter.3.cloned.1.call-update) | async-done | bytes 262160 | tf_op jit(solution)/shard_map/reduce_scatter | solution.py:196
  (342 shorter events, 189.1 us)
Async XLA Ops:
  7.2 119.8 %copy-start = (bf16[512,512]{1,0:T(8,128)(2,1)S(1)}, bf16[512,512]{1,0:T(8,128)(2,1)}, u32[]{:S(2)}) copy-start(bf16[512,512]{1,0:T(8,128)(2,1)} %param.27) | copy-start | bytes 1572868
  7.2 12.2 %copy-start.17 = (bf16[512,512]{1,0:T(8,128)(2,1)S(1)}, bf16[512,512]{1,0:T(8,128)(2,1)}, u32[]{:S(2)}) copy-start(bf16[512,512]{1,0:T(8,128)(2,1)} %param.22) | copy-start | bytes 1572868
  11.9 17.4 %all-to-all-start = ((bf16[16,16,512]{2,1,0:T(8,128)(2,1)}), bf16[16,16,512]{2,1,0:T(8,128)(2,1)S(1)}, u32[]{:S(2)}, u32[]{:S(2)}) async-start(bf16[16,16,512]{2,1,0:T(8,128)(2,1)} %broadcast_select_fusion), calls=%async_computation | async-start | bytes 524288 | tf_op jit(solution)/shard_map/all_to_all | solution.py:68
  19.3 335.5 %reduce-scatter.5.cloned.1.call-start = ((), (), s32[]{:S(2)}) async-start(), calls=%async_computation.5 | async-start | bytes 3342336 | tf_op jit(solution)/shard_map/reduce_scatter | solution.py:197
  20.4 3.6 copy-start.13
  20.4 4.7 %copy-start.1 = (bf16[512,512]{1,0:T(8,128)(2,1)S(1)}, bf16[512,512]{1,0:T(8,128)(2,1)}, u32[]{:S(2)}) copy-start(bf16[512,512]{1,0:T(8,128)(2,1)} %param.20) | copy-start | bytes 1572868
  20.4 4.7 %copy-start.15 = (bf16[1024,512]{1,0:T(8,128)(2,1)S(1)}, bf16[1024,512]{1,0:T(8,128)(2,1)}, u32[]{:S(2)}) copy-start(bf16[1024,512]{1,0:T(8,128)(2,1)} %param.26) | copy-start | bytes 3145732
  44.5 4.2 %copy-start.19 = (bf16[512,512]{1,0:T(8,128)(2,1)S(1)}, bf16[512,512]{1,0:T(8,128)(2,1)}, u32[]{:S(2)}) copy-start(bf16[512,512]{1,0:T(8,128)(2,1)} %get-tuple-element.1338) | copy-start | bytes 1572868 | tf_op jit(solution)/shard_map/while
  61.3 4.3 %copy-start.19 = (bf16[512,512]{1,0:T(8,128)(2,1)S(1)}, bf16[512,512]{1,0:T(8,128)(2,1)}, u32[]{:S(2)}) copy-start(bf16[512,512]{1,0:T(8,128)(2,1)} %get-tuple-element.1338) | copy-start | bytes 1572868 | tf_op jit(solution)/shard_map/while
  79.5 4.2 %copy-start.19 = (bf16[512,512]{1,0:T(8,128)(2,1)S(1)}, bf16[512,512]{1,0:T(8,128)(2,1)}, u32[]{:S(2)}) copy-start(bf16[512,512]{1,0:T(8,128)(2,1)} %get-tuple-element.1338) | copy-start | bytes 1572868 | tf_op jit(solution)/shard_map/while
  97.6 4.2 %copy-start.19 = (bf16[512,512]{1,0:T(8,128)(2,1)S(1)}, bf16[512,512]{1,0:T(8,128)(2,1)}, u32[]{:S(2)}) copy-start(bf16[512,512]{1,0:T(8,128)(2,1)} %get-tuple-element.1338) | copy-start | bytes 1572868 | tf_op jit(solution)/shard_map/while
  115.6 4.2 %copy-start.19 = (bf16[512,512]{1,0:T(8,128)(2,1)S(1)}, bf16[512,512]{1,0:T(8,128)(2,1)}, u32[]{:S(2)}) copy-start(bf16[512,512]{1,0:T(8,128)(2,1)} %get-tuple-element.1338) | copy-start | bytes 1572868 | tf_op jit(solution)/shard_map/while
  134.9 272.4 %reduce-scatter.3.cloned.1.call-start = ((), (), s32[]{:S(2)}) async-start(), calls=%async_computation.4 | async-start | bytes 4456448 | tf_op jit(solution)/shard_map/reduce_scatter | solution.py:196
  141.9 6.2 %copy-start.5 = (bf16[512,512]{0,1:T(8,128)(2,1)}, bf16[512,512]{0,1:T(8,128)(2,1)S(1)}, u32[]{:S(2)}) copy-start(bf16[512,512]{0,1:T(8,128)(2,1)S(1)} %copy.43) | copy-start | bytes 1572868 | tf_op jit(solution)/shard_map/while
  141.9 4.0 copy-start.20
  148.1 6.3 %copy-start.2 = (bf16[512,512]{1,0:T(8,128)(2,1)}, bf16[512,512]{1,0:T(8,128)(2,1)S(1)}, u32[]{:S(2)}) copy-start(bf16[512,512]{1,0:T(8,128)(2,1)S(1)} %fusion.159) | copy-start | bytes 1572868 | tf_op jit(solution)/shard_map/while
  160.5 5.4 %copy-start.3 = (bf16[512,512]{1,0:T(8,128)(2,1)S(1)}, bf16[512,512]{1,0:T(8,128)(2,1)}, u32[]{:S(2)}) copy-start(bf16[512,512]{1,0:T(8,128)(2,1)} %copy-done.2) | copy-start | bytes 1572868 | tf_op jit(solution)/shard_map/while
  160.5 5.4 %copy-start.6 = (bf16[512,512]{0,1:T(8,128)(2,1)S(1)}, bf16[512,512]{0,1:T(8,128)(2,1)}, u32[]{:S(2)}) copy-start(bf16[512,512]{0,1:T(8,128)(2,1)} %copy-done.5) | copy-start | bytes 1572868 | tf_op jit(solution)/shard_map/while
  165.9 3.4 copy-start.4
  181.0 6.1 %copy-start.5 = (bf16[512,512]{0,1:T(8,128)(2,1)}, bf16[512,512]{0,1:T(8,128)(2,1)S(1)}, u32[]{:S(2)}) copy-start(bf16[512,512]{0,1:T(8,128)(2,1)S(1)} %copy.43) | copy-start | bytes 1572868 | tf_op jit(solution)/shard_map/while
  181.0 4.0 copy-start.20
  187.2 6.3 %copy-start.2 = (bf16[512,512]{1,0:T(8,128)(2,1)}, bf16[512,512]{1,0:T(8,128)(2,1)S(1)}, u32[]{:S(2)}) copy-start(bf16[512,512]{1,0:T(8,128)(2,1)S(1)} %fusion.159) | copy-start | bytes 1572868 | tf_op jit(solution)/shard_map/while
  199.5 6.3 %copy-start.3 = (bf16[512,512]{1,0:T(8,128)(2,1)S(1)}, bf16[512,512]{1,0:T(8,128)(2,1)}, u32[]{:S(2)}) copy-start(bf16[512,512]{1,0:T(8,128)(2,1)} %copy-done.2) | copy-start | bytes 1572868 | tf_op jit(solution)/shard_map/while
  199.5 6.3 %copy-start.6 = (bf16[512,512]{0,1:T(8,128)(2,1)S(1)}, bf16[512,512]{0,1:T(8,128)(2,1)}, u32[]{:S(2)}) copy-start(bf16[512,512]{0,1:T(8,128)(2,1)} %copy-done.5) | copy-start | bytes 1572868 | tf_op jit(solution)/shard_map/while
  205.8 3.4 copy-start.4
  209.2 3.8 copy-start.8
  221.4 6.0 %copy-start.5 = (bf16[512,512]{0,1:T(8,128)(2,1)}, bf16[512,512]{0,1:T(8,128)(2,1)S(1)}, u32[]{:S(2)}) copy-start(bf16[512,512]{0,1:T(8,128)(2,1)S(1)} %copy.43) | copy-start | bytes 1572868 | tf_op jit(solution)/shard_map/while
  221.4 3.9 copy-start.20
  227.4 6.3 %copy-start.2 = (bf16[512,512]{1,0:T(8,128)(2,1)}, bf16[512,512]{1,0:T(8,128)(2,1)S(1)}, u32[]{:S(2)}) copy-start(bf16[512,512]{1,0:T(8,128)(2,1)S(1)} %fusion.159) | copy-start | bytes 1572868 | tf_op jit(solution)/shard_map/while
  239.7 6.3 %copy-start.3 = (bf16[512,512]{1,0:T(8,128)(2,1)S(1)}, bf16[512,512]{1,0:T(8,128)(2,1)}, u32[]{:S(2)}) copy-start(bf16[512,512]{1,0:T(8,128)(2,1)} %copy-done.2) | copy-start | bytes 1572868 | tf_op jit(solution)/shard_map/while
  239.8 6.3 %copy-start.6 = (bf16[512,512]{0,1:T(8,128)(2,1)S(1)}, bf16[512,512]{0,1:T(8,128)(2,1)}, u32[]{:S(2)}) copy-start(bf16[512,512]{0,1:T(8,128)(2,1)} %copy-done.5) | copy-start | bytes 1572868 | tf_op jit(solution)/shard_map/while
  249.4 3.8 copy-start.8
  261.7 6.0 %copy-start.5 = (bf16[512,512]{0,1:T(8,128)(2,1)}, bf16[512,512]{0,1:T(8,128)(2,1)S(1)}, u32[]{:S(2)}) copy-start(bf16[512,512]{0,1:T(8,128)(2,1)S(1)} %copy.43) | copy-start | bytes 1572868 | tf_op jit(solution)/shard_map/while
  261.7 3.9 copy-start.20
  267.7 6.3 %copy-start.2 = (bf16[512,512]{1,0:T(8,128)(2,1)}, bf16[512,512]{1,0:T(8,128)(2,1)S(1)}, u32[]{:S(2)}) copy-start(bf16[512,512]{1,0:T(8,128)(2,1)S(1)} %fusion.159) | copy-start | bytes 1572868 | tf_op jit(solution)/shard_map/while
  280.0 6.3 %copy-start.3 = (bf16[512,512]{1,0:T(8,128)(2,1)S(1)}, bf16[512,512]{1,0:T(8,128)(2,1)}, u32[]{:S(2)}) copy-start(bf16[512,512]{1,0:T(8,128)(2,1)} %copy-done.2) | copy-start | bytes 1572868 | tf_op jit(solution)/shard_map/while
  280.0 6.3 %copy-start.6 = (bf16[512,512]{0,1:T(8,128)(2,1)S(1)}, bf16[512,512]{0,1:T(8,128)(2,1)}, u32[]{:S(2)}) copy-start(bf16[512,512]{0,1:T(8,128)(2,1)} %copy-done.5) | copy-start | bytes 1572868 | tf_op jit(solution)/shard_map/while
  289.7 3.8 copy-start.8
  301.9 6.0 %copy-start.5 = (bf16[512,512]{0,1:T(8,128)(2,1)}, bf16[512,512]{0,1:T(8,128)(2,1)S(1)}, u32[]{:S(2)}) copy-start(bf16[512,512]{0,1:T(8,128)(2,1)S(1)} %copy.43) | copy-start | bytes 1572868 | tf_op jit(solution)/shard_map/while
  301.9 3.9 copy-start.20
  308.0 6.3 %copy-start.2 = (bf16[512,512]{1,0:T(8,128)(2,1)}, bf16[512,512]{1,0:T(8,128)(2,1)S(1)}, u32[]{:S(2)}) copy-start(bf16[512,512]{1,0:T(8,128)(2,1)S(1)} %fusion.159) | copy-start | bytes 1572868 | tf_op jit(solution)/shard_map/while
  320.3 6.3 %copy-start.3 = (bf16[512,512]{1,0:T(8,128)(2,1)S(1)}, bf16[512,512]{1,0:T(8,128)(2,1)}, u32[]{:S(2)}) copy-start(bf16[512,512]{1,0:T(8,128)(2,1)} %copy-done.2) | copy-start | bytes 1572868 | tf_op jit(solution)/shard_map/while
  320.3 6.3 %copy-start.6 = (bf16[512,512]{0,1:T(8,128)(2,1)S(1)}, bf16[512,512]{0,1:T(8,128)(2,1)}, u32[]{:S(2)}) copy-start(bf16[512,512]{0,1:T(8,128)(2,1)} %copy-done.5) | copy-start | bytes 1572868 | tf_op jit(solution)/shard_map/while
  330.0 3.8 copy-start.8
  336.8 5.4 %copy-start.18 = (s32[1,16,16]{2,1,0:T(8,128)S(1)}, s32[1,16,16]{2,1,0:T(8,128)}, u32[]{:S(2)}) copy-start(s32[1,16,16]{2,1,0:T(8,128)} %param.28) | copy-start | bytes 3076
  336.8 5.5 %copy-start.12 = (f32[512,512]{1,0:T(8,128)S(1)}, f32[512,512]{1,0:T(8,128)}, u32[]{:S(2)}) copy-start(f32[512,512]{1,0:T(8,128)} %get-tuple-element.686) | copy-start | bytes 3145732
  338.7 13.5 %all-to-all-start.1 = ((bf16[16,16,512]{2,1,0:T(8,128)(2,1)}), bf16[16,16,512]{2,1,0:T(8,128)(2,1)S(1)}, u32[]{:S(2)}, u32[]{:S(2)}) async-start(bf16[16,16,512]{2,1,0:T(8,128)(2,1)} %bitcast.5), calls=%async_computation.1 | async-start | bytes 524288 | tf_op jit(solution)/shard_map/all_to_all | solution.py:179
  354.7 52.6 %copy-start.14 = (f32[512,512]{1,0:T(8,128)}, f32[512,512]{1,0:T(8,128)S(1)}, u32[]{:S(2)}) copy-start(f32[512,512]{1,0:T(8,128)S(1)} %scatter_custom_fusion) | copy-start | bytes 3145732
  (17 other events, 45.8 us)
Sparse Core Ops, SparseCore 0:
  135.0 64.6 reduce-scatter.4
  336.9 70.3 reduce-scatter.2
where the time goes:
time: 418 us; the launch traced here: 414 us
  matrix products  153 us (37%)
  other arithmetic  88.5 us (21%)
  local copies, waits for them, and re-layouts  82.1 us (20%)
  waiting for transfers between devices  63.9 us (15%)
  between operations  14.2 us (3%)
  starting transfers between devices  11.2 us (3%)
    dot_general x38, matrix products, contract_rows(): lax.dot_general(left, right, (((0,), (0,)), ((), ())), preferred_element_...  85.4 us
    reduce_scatter x1, waiting for transfers between devices, local(): lax.psum_scatter(edge_stack, 'dom', scatter_dimension=0, tiled=True)  52.6 us
    dot_general x28, matrix products, product(): return jnp.dot(left, right, preferred_element_type=jnp.float32)  48.6 us
    add x5, other arithmetic, backward_block(): weight_accum + jnp.concatenate([contract_rows(send_x, grad_preact), contr...  30.7 us
    gather x10, local copies, waits for them, and re-layouts, edge_inputs(): send_x = jnp.take(node_table, send_index, axis=0)  23 us
    gather x10, local copies, waits for them, and re-layouts, edge_inputs(): recv_x = jnp.take(node_latent, recv_index, axis=0)  23 us
    dot_general x13, matrix products, times_transpose(): lax.dot_general(left, weight, (((1,), (1,)), ((), ())), preferred_element...  19.3 us
    and x10, other arithmetic, edge_inputs(): recv_x = jnp.take(node_latent, recv_index, axis=0)  14.2 us
  transfers between devices with their start and end apart: 4, of which 3 were waited for; matrix products, arithmetic and copies ran while one was open for 52% of the time, Pallas kernels for 0%

commit v1 on v0

v1 whole, which is shorter than its diff:
```python
import functools

import jax
import jax.numpy as jnp
from jax import lax
from jax.experimental import pallas as pl
from jax.experimental.pallas import tpu as pltpu
from jax.sharding import PartitionSpec as P

BF = jnp.bfloat16
F32 = jnp.float32
VMEM_BYTES = 56 * 1024 * 1024


def dot(left, right):
    return jnp.dot(left, right, preferred_element_type=F32)


def dot_rows(left, right):
    return lax.dot_general(left, right, (((0,), (0,)), ((), ())), preferred_element_type=F32)


def dot_last(left, right):
    return lax.dot_general(left, right, (((1,), (1,)), ((), ())), preferred_element_type=F32)


def split(value):
    high = value.astype(BF)
    return high, (value - high.astype(F32)).astype(BF)


def pick(row, base, count):
    size = row.shape[1]
    column = jnp.broadcast_to(row, (128, size)).T
    wide = jnp.concatenate([column] * (count // 128), 1)
    place = lax.broadcasted_iota(jnp.int32, (size, count), 1) + base
    return jnp.where(wide == place, 1.0, 0.0).astype(BF)


def pick_t(row, base, count):
    size = row.shape[1]
    place = lax.broadcasted_iota(jnp.int32, (count, size), 0) + base
    return jnp.where(jnp.broadcast_to(row, (count, size)) == place, 1.0, 0.0).astype(BF)


def normalize(mixed):
    centre = mixed - jnp.mean(mixed, -1, keepdims=True)
    inverse = lax.rsqrt(jnp.mean(centre * centre, -1, keepdims=True) + 1e-05)
    return centre * inverse, inverse


def norm_back(grad, normed, inverse):
    return inverse * (
        grad
        - jnp.mean(grad, -1, keepdims=True)
        - normed * jnp.mean(grad * normed, -1, keepdims=True)
    )


def swish_both(value):
    sig = jax.nn.sigmoid(value)
    hidden = value * sig
    return hidden.astype(BF), sig * (1.0 + value * (1.0 - sig))


def rows_kernel(rows_ref, latent_ref, out_ref):
    out_ref[...] = dot(pick(rows_ref[...], 0, latent_ref.shape[0]), latent_ref[...]).astype(BF)


def early_kernel(send_ref, recv_ref, edge_ref, latent_ref, w1_ref, pre_ref, high, low):
    nodes, width = latent_ref.shape

    @pl.when(pl.program_id(0) == 0)
    def _():
        latent = latent_ref[...]
        for part in range(2):
            table_high, table_low = split(dot(latent, w1_ref[pl.ds(part * width, width), :]))
            high[pl.ds(part * nodes, nodes), :] = table_high
            low[pl.ds(part * nodes, nodes), :] = table_low

    both = jnp.concatenate([pick(send_ref[0], 0, nodes), pick(recv_ref[0], 0, nodes)], 1)
    pre_ref[...] = (
        dot(edge_ref[...], w1_ref[pl.ds(2 * width, width), :])
        + dot(both, high[...])
        + dot(both, low[...])
    )


def stash(acc, row0, keep_ref, send_ref, core):
    groups, rows, _ = keep_ref.shape
    for group in range(groups):
        mine = pl.multiple_of(row0 + (2 * group + core) * rows, 16)
        other = pl.multiple_of(row0 + (2 * group + 1 - core) * rows, 16)
        keep_ref[group] = acc[pl.ds(mine, rows), :]
        send_ref[group] = acc[pl.ds(other, rows), :].astype(BF)


def forward_kernel(
    scalar_ref, send_ref, recv_ref, pre_ref, halo_ref, wsend_ref, w2_ref,
    latent_ref, cotan_ref, nw1_ref, nw2_ref,
    hidden_ref, slope_ref, normed_ref, inverse_ref, agg_ref, grad_ref, keep_ref, away_ref,
    table, gathered, acc,
):
    turn = pl.program_id(0)
    nodes, width = latent_ref.shape
    halo = halo_ref.shape[0]
    size = pre_ref.shape[0]

    @pl.when(turn == 0)
    def _():
        high, low = split(dot(halo_ref[...], wsend_ref[...]))
        table[pl.ds(0, halo), :] = high
        table[pl.ds(halo, halo), :] = low
        gathered[...] = jnp.zeros_like(gathered)

    far = pick(send_ref[0], nodes, halo)
    pre = pre_ref[...] + dot(far, table[pl.ds(0, halo), :]) + dot(far, table[pl.ds(halo, halo), :])
    hidden, slope = swish_both(pre)
    hidden_ref[...] = hidden
    slope_ref[...] = slope
    normed, inverse = normalize(dot(hidden, w2_ref[...]))
    normed_ref[...] = normed
    inverse_ref[...] = inverse
    place = turn * size + lax.broadcasted_iota(jnp.int32, (size, 1), 0)
    message = jnp.where(place < scalar_ref[0], normed, 0.0).astype(BF)
    gathered[...] += dot(pick_t(recv_ref[0], 0, nodes), message)

    @pl.when(turn == pl.num_programs(0) - 1)
    def _():
        latent = latent_ref[...]
        sums = gathered[...].astype(BF)
        w_node = nw1_ref[pl.ds(0, width), :]
        w_agg = nw1_ref[pl.ds(width, width), :]
        node_hidden, node_slope = swish_both(dot(latent, w_node) + dot(sums, w_agg))
        node_normed, node_inverse = normalize(dot(node_hidden, nw2_ref[...]))
        cotan = cotan_ref[...].astype(F32)
        grad_out = norm_back(cotan, node_normed, node_inverse).astype(BF)
        grad_pre = (dot_last(grad_out, nw2_ref[...]) * node_slope).astype(BF)
        agg_ref[...] = dot_last(grad_pre, w_agg).astype(BF)
        grad_ref[...] = cotan + dot_last(grad_pre, w_node)
        acc[pl.ds(0, width), :] = dot_rows(latent, grad_pre)
        acc[pl.ds(width, width), :] = dot_rows(sums, grad_pre)
        acc[pl.ds(2 * width, width), :] = dot_rows(node_hidden, grad_out)
        stash(acc, 0, keep_ref, away_ref, scalar_ref[1])


def backward_kernel(
    scalar_ref, send_ref, recv_ref, edge_ref, cotan_ref, hidden_ref, slope_ref, normed_ref, inverse_ref,
    agg_ref, grad_ref, latent_ref, halo_ref, w1_ref, w2_ref,
    edge_out, node_out, far_out, keep_ref, away_ref,
    sent, received, acc,
):
    turn = pl.program_id(0)
    nodes, width = latent_ref.shape
    halo = halo_ref.shape[0]
    size = edge_ref.shape[0]

    @pl.when(turn == 0)
    def _():
        sent[...] = jnp.zeros_like(sent)
        received[...] = jnp.zeros_like(received)
        acc[...] = jnp.zeros_like(acc)

    recv_row = recv_ref[0]
    cotan = cotan_ref[...].astype(F32)
    place = turn * size + lax.broadcasted_iota(jnp.int32, (size, 1), 0)
    grad_msg = jnp.where(
        place < scalar_ref[0], cotan + dot(pick(recv_row, 0, nodes), agg_ref[...]), 0.0
    )
    grad_mixed = norm_back(grad_msg, normed_ref[...], inverse_ref[...]).astype(BF)
    grad_pre = (dot_last(grad_mixed, w2_ref[...]) * slope_ref[...]).astype(BF)
    acc[pl.ds(3 * width, width), :] += dot_rows(hidden_ref[...], grad_mixed)
    acc[pl.ds(2 * width, width), :] += dot_rows(edge_ref[...], grad_pre)
    sent[...] += dot(pick_t(send_ref[0], 0, nodes + halo), grad_pre)
    received[...] += dot(pick_t(recv_row, 0, nodes), grad_pre)
    edge_out[...] = (cotan + dot_last(grad_pre, w1_ref[pl.ds(2 * width, width), :])).astype(BF)

    @pl.when(turn == pl.num_programs(0) - 1)
    def _():
        w_send = w1_ref[pl.ds(0, width), :]
        latent = latent_ref[...]
        near = sent[pl.ds(0, nodes), :].astype(BF)
        far = sent[pl.ds(nodes, halo), :].astype(BF)
        into = received[...].astype(BF)
        far_out[...] = dot_last(far, w_send).astype(BF)
        node_out[...] = (
            grad_ref[...] + dot_last(near, w_send) + dot_last(into, w1_ref[pl.ds(width, width), :])
        )
        acc[pl.ds(0, width), :] = dot_rows(latent, near) + dot_rows(halo_ref[...], far)
        acc[pl.ds(width, width), :] = dot_rows(latent, into)
        stash(acc, 0, keep_ref, away_ref, scalar_ref[1])


def return_kernel(rows_ref, back_ref, part_ref, out_ref):
    out_ref[...] = part_ref[...] + dot(pick_t(rows_ref[...], 0, out_ref.shape[0]), back_ref[...])


def whole(shape):
    return pl.BlockSpec(shape, lambda i: (0,) * len(shape))


def by_rows(size, width):
    return pl.BlockSpec((size, width), lambda i: (i, 0))


def reduce_scatter(keep, away, count):
    place = lax.axis_index("dom")
    _, rows, width = keep.shape
    total = keep + lax.ppermute(away, "dom", [(i, i ^ 1) for i in range(count)]).astype(F32)
    groups = count // 4
    total = total.reshape(groups, 2, rows, width)
    side = (place // 2) % 2
    mine = lax.dynamic_index_in_dim(total, side, 1, keepdims=False)
    other = lax.dynamic_index_in_dim(total, 1 - side, 1, keepdims=False).astype(BF)
    total = mine + lax.ppermute(other, "dom", [(i, i ^ 2) for i in range(count)]).astype(F32)
    group = place // 4
    result = lax.dynamic_index_in_dim(total, group, 0, keepdims=False)
    for step in range(1, groups):
        piece = lax.dynamic_index_in_dim(total, (group + step) % groups, 0, keepdims=False).astype(BF)
        result = result + lax.ppermute(
            piece, "dom", [(i, (i + 4 * step) % count) for i in range(count)]
        ).astype(F32)
    return result


def local(
    count,
    node_latent,
    edge_latent,
    node_cotan,
    edge_cotan,
    edge_w1,
    edge_w2,
    node_w1,
    node_w2,
    send_rows,
    senders,
    receivers,
    edge_count,
):
    nodes, width = node_latent.shape
    edges = edge_latent.shape[0]
    peers, slots = send_rows.shape[1:]
    halo = peers * slots
    size = 512
    turns = edges // size
    place = lax.axis_index("dom")
    scalars = jnp.stack([edge_count[0], (place % 2).astype(jnp.int32)])
    flat_rows = send_rows.reshape(1, halo)
    send_row = senders.reshape(turns, 1, size)
    recv_row = receivers.reshape(turns, 1, size)
    row_spec = pl.BlockSpec((1, 1, size), lambda i: (i, 0, 0))
    smem = pl.BlockSpec(memory_space=pltpu.SMEM)
    params = pltpu.CompilerParams(vmem_limit_bytes=VMEM_BYTES)
    unit = 2 * edges * width * width

    def cost(units, bytes_accessed):
        return pl.CostEstimate(flops=int(units * unit), bytes_accessed=bytes_accessed, transcendentals=0)

    outgoing = pl.pallas_call(
        rows_kernel,
        out_shape=jax.ShapeDtypeStruct((halo, width), BF),
        compiler_params=params,
        cost_estimate=cost(0.1, 3 * halo * width * 2),
        name="halo_rows",
    )(flat_rows, node_latent)
    incoming = lax.all_to_all(
        outgoing.reshape(peers, slots, width), "dom", split_axis=0, concat_axis=0, tiled=True
    ).reshape(halo, width)

    pre = pl.pallas_call(
        early_kernel,
        grid=(turns,),
        in_specs=[row_spec, row_spec, by_rows(size, width), whole((nodes, width)), whole(edge_w1.shape)],
        out_specs=by_rows(size, width),
        out_shape=jax.ShapeDtypeStruct((edges, width), F32),
        scratch_shapes=[pltpu.VMEM((2 * nodes, width), BF)] * 2,
        compiler_params=params,
        cost_estimate=cost(5.5, edges * width * 6),
        name="edge_early",
    )(send_row, recv_row, edge_latent, node_latent, edge_w1)

    node_rows = 3 * width // count
    edge_rows = 4 * width // count
    hidden, slope, normed, inverse, agg_grad, grad_part, node_keep, node_away = pl.pallas_call(
        forward_kernel,
        grid=(turns,),
        in_specs=[
            smem, row_spec, row_spec, by_rows(size, width), whole((halo, width)), whole((width, width)),
            whole((width, width)), whole((nodes, width)), whole((nodes, width)),
            whole(node_w1.shape), whole(node_w2.shape),
        ],
        out_specs=[
            by_rows(size, width), by_rows(size, width), by_rows(size, width), by_rows(size, 1),
            whole((nodes, width)), whole((nodes, width)),
            whole((count // 2, node_rows, width)), whole((count // 2, node_rows, width)),
        ],
        out_shape=[
            jax.ShapeDtypeStruct((edges, width), BF),
            jax.ShapeDtypeStruct((edges, width), F32),
            jax.ShapeDtypeStruct((edges, width), F32),
            jax.ShapeDtypeStruct((edges, 1), F32),
            jax.ShapeDtypeStruct((nodes, width), BF),
            jax.ShapeDtypeStruct((nodes, width), F32),
            jax.ShapeDtypeStruct((count // 2, node_rows, width), F32),
            jax.ShapeDtypeStruct((count // 2, node_rows, width), BF),
        ],
        scratch_shapes=[
            pltpu.VMEM((2 * halo, width), BF),
            pltpu.VMEM((nodes, width), F32),
            pltpu.VMEM((3 * width, width), F32),
        ],
        compiler_params=params,
        cost_estimate=cost(6, edges * width * 20),
        name="edge_forward",
    )(
        scalars, send_row, recv_row, pre, incoming, edge_w1, edge_w2,
        node_latent, node_cotan, node_w1, node_w2,
    )

    node_share = reduce_scatter(node_keep, node_away, count)

    grad_edge, node_part, far_grad, edge_keep, edge_away = pl.pallas_call(
        backward_kernel,
        grid=(turns,),
        in_specs=[
            smem, row_spec, row_spec, by_rows(size, width), by_rows(size, width), by_rows(size, width),
            by_rows(size, width), by_rows(size, width), by_rows(size, 1),
            whole((nodes, width)), whole((nodes, width)), whole((nodes, width)), whole((halo, width)),
            whole(edge_w1.shape), whole(edge_w2.shape),
        ],
        out_specs=[
            by_rows(size, width), whole((nodes, width)), whole((halo, width)),
            whole((count // 2, edge_rows, width)), whole((count // 2, edge_rows, width)),
        ],
        out_shape=[
            jax.ShapeDtypeStruct((edges, width), BF),
            jax.ShapeDtypeStruct((nodes, width), F32),
            jax.ShapeDtypeStruct((halo, width), BF),
            jax.ShapeDtypeStruct((count // 2, edge_rows, width), F32),
            jax.ShapeDtypeStruct((count // 2, edge_rows, width), BF),
        ],
        scratch_shapes=[
            pltpu.VMEM((nodes + halo, width), F32),
            pltpu.VMEM((nodes, width), F32),
            pltpu.VMEM((4 * width, width), F32),
        ],
        compiler_params=params,
        cost_estimate=cost(10, edges * width * 20),
        name="edge_backward",
    )(
        scalars, send_row, recv_row, edge_latent, edge_cotan, hidden, slope, normed, inverse,
        agg_grad, grad_part, node_latent, incoming, edge_w1, edge_w2,
    )

    returned = lax.all_to_all(
        far_grad.reshape(peers, slots, width), "dom", split_axis=0, concat_axis=0, tiled=True
    ).reshape(halo, width)
    edge_share = reduce_scatter(edge_keep, edge_away, count)
    grad_node = pl.pallas_call(
        return_kernel,
        out_shape=jax.ShapeDtypeStruct((nodes, width), F32),
        compiler_params=params,
        cost_estimate=cost(0.1, nodes * width * 8),
        name="halo_return",
    )(flat_rows, returned, node_part)
    return (grad_node, grad_edge, edge_share, node_share)


def solution(mesh):
    rows = P(("member", "dom"), None)
    placed = (
        rows, rows, rows, rows, P(), P(), P(), P(), P("dom", None, None), P("dom"), P("dom"), P("dom"),
    )
    return jax.shard_map(
        functools.partial(local, mesh.shape["dom"]),
        mesh=mesh,
        in_specs=placed,
        out_specs=(rows, rows, rows, rows),
        check_vma=False,
    )
```

time: 418 us -> 116 us (0.28)
  matrix products: 153 us -> 0 us
  other arithmetic: 88.5 us -> 5.32 us
  local copies, waits for them, and re-layouts: 82.1 us -> 6.49 us
  Pallas kernels: 0 us -> 56.2 us
  waiting for transfers between devices: 63.9 us -> 17.5 us
  starting transfers between devices: 11.2 us -> 27.6 us
  between operations: 14.2 us -> 1.43 us
    dot_general x79 -> x0, matrix products: 153 us -> none  [the longest x38 85.4 us: contract_rows(): lax.dot_general(left, right, (((0,), (0,)), ((), ())), preferred_element_...]
    pallas_call x0 -> x5, Pallas kernels: none -> 56.2 us  [the longest x1 22.1 us: local(): pl.pallas_call(backward_kernel, grid=(turns,), in_specs=[smem, row_spec,...]
    reduce_scatter x2 -> x0, waiting for transfers between devices: 52.6 us -> none  [the longest x1 52.6 us: local(): lax.psum_scatter(edge_stack, 'dom', scatter_dimension=0, tiled=True)]
    gather x21 -> x0, local copies, waits for them, and re-layouts: 48.4 us -> none  [the longest x10 23 us: edge_inputs(): send_x = jnp.take(node_table, send_index, axis=0)]
    add x6, other arithmetic: 32.2 us -> 4.67 us  [the longest x2 1.85 us: reduce_scatter(): keep + lax.ppermute(away, 'dom', [(i, i ^ 1) for i in range(count)]).asty...]
    and x21 -> x0, other arithmetic: 22.5 us -> none  [the longest x10 14.2 us: edge_inputs(): recv_x = jnp.take(node_latent, recv_index, axis=0)]
    ppermute x0 -> x10, starting transfers between devices: none -> 14.2 us  [the longest x6 11.2 us: reduce_scatter(): lax.ppermute(piece, 'dom', [(i, (i + 4 * step) % count) for i in range(co...]
    reduce_sum x12 -> x0, other arithmetic: 14 us -> none  [the longest x6 7.1 us: normalize(): inverse = lax.rsqrt(jnp.mean(centre * centre, -1, keepdims=True) + 1e-05)]
  transfers between devices with their start and end apart: 4 -> 12, of which waited for: 3 -> 5; matrix products, arithmetic and copies ran while one was open for 52% -> 7% of each run, Pallas kernels for 0% -> 32%
where the time goes in v1:
time: 116 us; the launch traced here: 115 us
  Pallas kernels  56.2 us (48%)
  starting transfers between devices  27.6 us (24%)
  waiting for transfers between devices  17.5 us (15%)
  local copies, waits for them, and re-layouts  6.49 us (6%)
  other arithmetic  5.32 us (5%)
  between operations  1.43 us (1%)
    pallas_call x1, Pallas kernels, local(): pl.pallas_call(backward_kernel, grid=(turns,), in_specs=[smem, row_spec,...  22.1 us
    pallas_call x1, Pallas kernels, local(): pl.pallas_call(forward_kernel, grid=(turns,), in_specs=[smem, row_spec, r...  18 us
    pallas_call x1, Pallas kernels, local(): pl.pallas_call(early_kernel, grid=(turns,), in_specs=[row_spec, row_spec,...  11.4 us
    ppermute x6, starting transfers between devices, reduce_scatter(): lax.ppermute(piece, 'dom', [(i, (i + 4 * step) % count) for i in range(co...  11.2 us
    all_to_all x1, starting transfers between devices, local(): lax.all_to_all(outgoing.reshape(peers, slots, width), 'dom', split_axis=0...  7.39 us
    ppermute x6, waiting for transfers between devices, reduce_scatter(): lax.ppermute(piece, 'dom', [(i, (i + 4 * step) % count) for i in range(co...  6.45 us
    ppermute x2, waiting for transfers between devices, reduce_scatter(): lax.ppermute(other, 'dom', [(i, i ^ 2) for i in range(count)]).astype(F32)  6.24 us
    all_to_all x1, starting transfers between devices, local(): lax.all_to_all(far_grad.reshape(peers, slots, width), 'dom', split_axis=0...  6.01 us
  transfers between devices with their start and end apart: 12, of which 5 were waited for; matrix products, arithmetic and copies ran while one was open for 7% of the time, Pallas kernels for 32%

profile of v1, /device:TPU:0, one launch (start us, length us, event | category | flops | bytes accessed | tf_op | source)
XLA Modules:
  0.0 114.6 jit_solution(625743367233340261)
XLA Ops:
  0.6 1.4 %reshape.43.rows_ref = s32[1,256]{1,0:T(1,128)} reshape(s32[1,16,16]{2,1,0:T(8,128)} %param.20) | data formatting | bytes 2048 | tf_op jit(solution)/shard_map/reshape | solution.py:249
  2.0 2.1 %halo_rows.1 = bf16[256,512]{1,0:T(8,128)(2,1)} custom-call(s32[1,256]{1,0:T(1,128)} %reshape.43.rows_ref, bf16[512,512]{1,0:T(8,128)(2,1)} %latent_ref.7), custom_call_target="tpu_custom_call" | custom-call | flops 134217728 | bytes 786432 | tf_op jit(solution)/shard_map/halo_rows/pallas_call | solution.py:260
  4.1 7.4 %all-to-all-start = ((bf16[16,16,512]{2,1,0:T(8,128)(2,1)}), bf16[16,16,512]{2,1,0:T(8,128)(2,1)S(1)}, u32[]{:S(2)}, u32[]{:S(2)}) async-start(bf16[16,16,512]{2,1,0:T(8,128)(2,1)} %bitcast.52), calls=%async_computation | async-start | bytes 524288 | tf_op jit(solution)/shard_map/all_to_all | solution.py:267
  12.1 1.3 %reshape.44.send_ref = s32[5,1,512]{2,1,0:T(1,128)} reshape(s32[2560]{0:T(1024)} %param.21) | data formatting | bytes 20480 | tf_op jit(solution)/shard_map/reshape | solution.py:250
  13.5 1.3 %reshape.45.recv_ref = s32[5,1,512]{2,1,0:T(1,128)} reshape(s32[2560]{0:T(1024)} %param.22) | data formatting | bytes 20480 | tf_op jit(solution)/shard_map/reshape | solution.py:251
  14.8 0.6 pad_add_fusion.scalar_ref
  15.4 11.4 %edge_early.1.pre_ref = f32[2560,512]{1,0:T(8,128)} custom-call(s32[5,1,512]{2,1,0:T(1,128)} %reshape.44.send_ref, s32[5,1,512]{2,1,0:T(1,128)} %reshape.45.recv_ref, bf16[2560,512]{1,0:T(8,128)(2,1)} %edge_ref.3, bf16[512,512]{1,0:T(8,128)(2,1)} %latent_ref.7, bf16[1536,512]{1,0:T(8,128)(2,1)} %w1_ref.3), custom_call_target="tpu_custom_call" | custom-call | flops 7381975040 | bytes 7864320 | tf_op jit(solution)/shard_map/edge_early/pallas_call | solution.py:271
  26.8 0.0 all-to-all-done
  26.8 0.7 copy-done.5
  27.5 18.0 %edge_forward.1 = (bf16[2560,512]{1,0:T(8,128)(2,1)}, f32[2560,512]{1,0:T(8,128)}, f32[2560,512]{1,0:T(8,128)}, f32[2560,1]{1,0:T(8,128)}, bf16[512,512]{1,0:T(8...) custom-call(s32[2]{0:T(128)} %pad_add_fusion.scalar_ref, ...), custom_call_target="tpu_custom_call" | custom-call | flops 8053063680 | bytes 26214400 | tf_op jit(solution)/shard_map/edge_forward/pallas_call | solution.py:285
  45.6 0.5 collective-permute-start.5
  46.0 22.1 %edge_backward.1 = (bf16[2560,512]{1,0:T(8,128)(2,1)}, f32[512,512]{1,0:T(8,128)}, bf16[256,512]{1,0:T(8,128)(2,1)}, f32[8,128,512]{2,1,0:T(8,128)}, bf16[8,128,512]{2,1,0:T(8,128)(2,1)}) custom-call(s32[2]{0:T(128)} %pad_add_fusion.scalar_ref, s32[5,1,512]{2,1,0:T(1,128)} %reshape.44.send_ref, s32[5,1,512]{2,1,0:T(1,128)} %reshape.45.recv_ref, ...), custom_call_target="tpu_custom_call" | custom-call | flops 13421772800 | bytes 26214400 | tf_op jit(solution)/shard_map/edge_backward/pallas_call | solution.py:323
  68.2 0.2 collective-permute-start
  68.4 6.0 %all-to-all-start.1 = ((bf16[16,16,512]{2,1,0:T(8,128)(2,1)}), bf16[16,16,512]{2,1,0:T(8,128)(2,1)S(1)}, u32[]{:S(2)}, u32[]{:S(2)}) async-start(bf16[16,16,512]{2,1,0:T(8,128)(2,1)} %bitcast.53), calls=%async_computation.1 | async-start | bytes 524288 | tf_op jit(solution)/shard_map/all_to_all | solution.py:356
  74.4 0.0 collective-permute-done.5
  74.4 0.0 copy-done.3
  74.4 0.0 copy-start.2
  74.4 1.5 %convert_add_fusion.1 = f32[8,96,512]{2,1,0:T(8,128)S(1)} fusion(f32[8,96,512]{2,1,0:T(8,128)S(1)} %copy-done.3, bf16[8,96,512]{2,1,0:T(8,128)(2,1)} %collective-permute-done.5), kind=kLoop, calls=%fused_computation.1 | loop fusion | flops 786432 | bytes 3932160 | tf_op jit(solution)/shard_map/add | solution.py:209
  75.9 0.0 copy-start
  75.9 0.9 fusion.1
  76.8 1.9 %collective-permute-start.6 = (bf16[4,96,512]{2,1,0:T(8,128)(2,1)}, bf16[4,96,512]{2,1,0:T(8,128)(2,1)}, u32[]{:S(2)}, u32[]{:S(2)}) collective-permute-start(bf16[4,96,512]{2,1,0:T(8,128)(2,1)} %fusion.1), channel_id=1, source_target_pairs={{0,2},{1,3},{2,0},{3,1},{4,6},{5,7},{6,4},{7,5},{8,10},{9,11},{10,... | collective-permute-start | bytes 1179656 | tf_op jit(solution)/shard_map/ppermute | solution.py:215
  78.8 0.0 collective-permute-done
  78.8 0.0 copy-done
  78.8 0.3 convert_add_fusion
  79.1 0.1 fusion
  79.2 0.4 collective-permute-start.1
  79.6 4.8 %all-to-all-done.1 = bf16[16,16,512]{2,1,0:T(8,128)(2,1)S(1)} async-done(((bf16[16,16,512]{2,1,0:T(8,128)(2,1)}), bf16[16,16,512]{2,1,0:T(8,128)(2,1)S(1)}, u32[]{:S(2)}, u32[]{:S(2)}) %all-to-all-start.1) | async-done | bytes 262176 | tf_op jit(solution)/shard_map/all_to_all | solution.py:356
  84.4 0.7 copy-done.4
  85.1 2.6 %halo_return.1 = f32[512,512]{1,0:T(8,128)} custom-call(s32[1,256]{1,0:T(1,128)} %reshape.43.rows_ref, bf16[256,512]{1,0:T(8,128)(2,1)} %bitcast.51, f32[512,512]{1,0:T(8,128)} %get-tuple-element.24.part_ref), custom_call_target="tpu_custom_call" | custom-call | flops 134217728 | bytes 2097152 | tf_op jit(solution)/shard_map/halo_return/pallas_call | solution.py:360
  87.7 2.4 %collective-permute-done.6 = bf16[4,96,512]{2,1,0:T(8,128)(2,1)} collective-permute-done((bf16[4,96,512]{2,1,0:T(8,128)(2,1)}, bf16[4,96,512]{2,1,0:T(8,128)(2,1)}, u32[]{:S(2)}, u32[]{:S(2)}) %collective-permute-start.6) | collective-permute-done | bytes 393248 | tf_op jit(solution)/shard_map/ppermute | solution.py:215
  90.1 1.1 bitcast_add_fusion.1
  91.3 2.0 %collective-permute-start.7 = (bf16[96,512]{1,0:T(8,128)(2,1)S(1)}, bf16[96,512]{1,0:T(8,128)(2,1)S(1)}, u32[]{:S(2)}, u32[]{:S(2)}) collective-permute-start(bf16[96,512]{1,0:T(8,128)(2,1)S(1)} %get-tuple-element.33), channel_id=1, source_target_pairs={{0,4},{1,5},{2,6},{3,7},{4,8},{5,9},{6,10},{7,11},{8,12},{9,13},{1... | collective-permute-start | bytes 294920 | tf_op jit(solution)/shard_map/ppermute | solution.py:220
  93.3 1.9 %collective-permute-start.8 = (bf16[96,512]{1,0:T(8,128)(2,1)S(1)}, bf16[96,512]{1,0:T(8,128)(2,1)S(1)}, u32[]{:S(2)}, u32[]{:S(2)}) collective-permute-start(bf16[96,512]{1,0:T(8,128)(2,1)S(1)} %get-tuple-element.35), channel_id=1, source_target_pairs={{0,8},{1,9},{2,10},{3,11},{4,12},{5,13},{6,14},{7,15},{8,0},{9,1},... | collective-permute-start | bytes 294920 | tf_op jit(solution)/shard_map/ppermute | solution.py:220
  95.2 1.8 %collective-permute-start.9 = (bf16[96,512]{1,0:T(8,128)(2,1)S(1)}, bf16[96,512]{1,0:T(8,128)(2,1)S(1)}, u32[]{:S(2)}, u32[]{:S(2)}) collective-permute-start(bf16[96,512]{1,0:T(8,128)(2,1)S(1)} %get-tuple-element.34), channel_id=1, source_target_pairs={{0,12},{1,13},{2,14},{3,15},{4,0},{5,1},{6,2},{7,3},{8,4},{9,5},{1... | collective-permute-start | bytes 294920 | tf_op jit(solution)/shard_map/ppermute | solution.py:220
  97.0 3.9 %collective-permute-done.1 = bf16[4,128,512]{2,1,0:T(8,128)(2,1)S(1)} collective-permute-done((bf16[4,128,512]{2,1,0:T(8,128)(2,1)S(1)}, bf16[4,128,512]{2,1,0:T(8,128)(2,1)S(1)}, u32[]{:S(2)}, u32[]{:S(2)}) %collective-permute-start.1) | collective-permute-done | bytes 524320 | tf_op jit(solution)/shard_map/ppermute | solution.py:215
  100.9 0.2 bitcast_add_fusion
  101.1 0.1 fusion.6
  101.1 1.9 %collective-permute-start.2 = (bf16[128,512]{1,0:T(8,128)(2,1)S(1)}, bf16[128,512]{1,0:T(8,128)(2,1)S(1)}, u32[]{:S(2)}, u32[]{:S(2)}) collective-permute-start(bf16[128,512]{1,0:T(8,128)(2,1)S(1)} %get-tuple-element.30), channel_id=1, source_target_pairs={{0,4},{1,5},{2,6},{3,7},{4,8},{5,9},{6,10},{7,11},{8,12},{9,13},{1... | collective-permute-start | bytes 393224 | tf_op jit(solution)/shard_map/ppermute | solution.py:220
  103.0 1.7 %collective-permute-start.3 = (bf16[128,512]{1,0:T(8,128)(2,1)S(1)}, bf16[128,512]{1,0:T(8,128)(2,1)S(1)}, u32[]{:S(2)}, u32[]{:S(2)}) collective-permute-start(bf16[128,512]{1,0:T(8,128)(2,1)S(1)} %get-tuple-element.32), channel_id=1, source_target_pairs={{0,8},{1,9},{2,10},{3,11},{4,12},{5,13},{6,14},{7,15},{8,0},{9,1},... | collective-permute-start | bytes 393224 | tf_op jit(solution)/shard_map/ppermute | solution.py:220
  104.7 0.0 collective-permute-done.7
  104.7 1.9 %collective-permute-start.4 = (bf16[128,512]{1,0:T(8,128)(2,1)S(1)}, bf16[128,512]{1,0:T(8,128)(2,1)S(1)}, u32[]{:S(2)}, u32[]{:S(2)}) collective-permute-start(bf16[128,512]{1,0:T(8,128)(2,1)S(1)} %get-tuple-element.31), channel_id=1, source_target_pairs={{0,12},{1,13},{2,14},{3,15},{4,0},{5,1},{6,2},{7,3},{8,4},{9,5},{1... | collective-permute-start | bytes 393224 | tf_op jit(solution)/shard_map/ppermute | solution.py:220
  106.7 0.0 collective-permute-done.8
  106.7 0.0 collective-permute-done.9
  106.7 0.7 fusion.5
  107.4 2.1 %collective-permute-done.2 = bf16[128,512]{1,0:T(8,128)(2,1)S(1)} collective-permute-done((bf16[128,512]{1,0:T(8,128)(2,1)S(1)}, bf16[128,512]{1,0:T(8,128)(2,1)S(1)}, u32[]{:S(2)}, u32[]{:S(2)}) %collective-permute-start.2) | collective-permute-done | bytes 131104 | tf_op jit(solution)/shard_map/ppermute | solution.py:220
  109.5 4.4 %collective-permute-done.3 = bf16[128,512]{1,0:T(8,128)(2,1)S(1)} collective-permute-done((bf16[128,512]{1,0:T(8,128)(2,1)S(1)}, bf16[128,512]{1,0:T(8,128)(2,1)S(1)}, u32[]{:S(2)}, u32[]{:S(2)}) %collective-permute-start.3) | collective-permute-done | bytes 131104 | tf_op jit(solution)/shard_map/ppermute | solution.py:220
  113.9 0.0 collective-permute-done.4
  113.9 0.8 fusion.3
  (7 shorter events, 0.1 us)
Async XLA Ops:
  4.1 22.8 %all-to-all-start = ((bf16[16,16,512]{2,1,0:T(8,128)(2,1)}), bf16[16,16,512]{2,1,0:T(8,128)(2,1)S(1)}, u32[]{:S(2)}, u32[]{:S(2)}) async-start(bf16[16,16,512]{2,1,0:T(8,128)(2,1)} %bitcast.52), calls=%async_computation | async-start | bytes 524288 | tf_op jit(solution)/shard_map/all_to_all | solution.py:267
  26.8 0.7 copy-start.5
  45.6 28.8 %collective-permute-start.5 = (bf16[8,96,512]{2,1,0:T(8,128)(2,1)}, bf16[8,96,512]{2,1,0:T(8,128)(2,1)}, u32[]{:S(2)}, u32[]{:S(2)}) collective-permute-start(bf16[8,96,512]{2,1,0:T(8,128)(2,1)} %get-tuple-element.29), channel_id=1, source_target_pairs={{0,1},{1,0},{2,3},{3,2},{4,5},{5,4},{6,7},{7,6},{8,9},{9,8},{10,11... | collective-permute-start | bytes 2359304 | tf_op jit(solution)/shard_map/ppermute | solution.py:209
  46.0 28.3 %copy-start.3 = (f32[8,96,512]{2,1,0:T(8,128)S(1)}, f32[8,96,512]{2,1,0:T(8,128)}, u32[]{:S(2)}) copy-start(f32[8,96,512]{2,1,0:T(8,128)} %get-tuple-element.28) | copy-start | bytes 4718596
  68.2 10.6 %collective-permute-start = (bf16[8,128,512]{2,1,0:T(8,128)(2,1)}, bf16[8,128,512]{2,1,0:T(8,128)(2,1)S(1)}, u32[]{:S(2)}, u32[]{:S(2)}) collective-permute-start(bf16[8,128,512]{2,1,0:T(8,128)(2,1)} %get-tuple-element.27), channel_id=1, source_target_pairs={{0,1},{1,0},{2,3},{3,2},{4,5},{5,4},{6,7},{7,6},{8,9},{9,8},{10,11... | collective-permute-start | bytes 3145736 | tf_op jit(solution)/shard_map/ppermute | solution.py:209
  68.4 16.1 %all-to-all-start.1 = ((bf16[16,16,512]{2,1,0:T(8,128)(2,1)}), bf16[16,16,512]{2,1,0:T(8,128)(2,1)S(1)}, u32[]{:S(2)}, u32[]{:S(2)}) async-start(bf16[16,16,512]{2,1,0:T(8,128)(2,1)} %bitcast.53), calls=%async_computation.1 | async-start | bytes 524288 | tf_op jit(solution)/shard_map/all_to_all | solution.py:356
  74.4 4.4 %copy-start.2 = (f32[8,128,512]{2,1,0:T(8,128)S(1)}, f32[8,128,512]{2,1,0:T(8,128)}, u32[]{:S(2)}) copy-start(f32[8,128,512]{2,1,0:T(8,128)} %get-tuple-element.26) | copy-start | bytes 6291460
  75.9 2.8 %copy-start = (f32[8,96,512]{2,1,0:T(8,128)}, f32[8,96,512]{2,1,0:T(8,128)S(1)}, u32[]{:S(2)}) copy-start(f32[8,96,512]{2,1,0:T(8,128)S(1)} %convert_add_fusion.1) | copy-start | bytes 4718596
  76.8 13.3 %collective-permute-start.6 = (bf16[4,96,512]{2,1,0:T(8,128)(2,1)}, bf16[4,96,512]{2,1,0:T(8,128)(2,1)}, u32[]{:S(2)}, u32[]{:S(2)}) collective-permute-start(bf16[4,96,512]{2,1,0:T(8,128)(2,1)} %fusion.1), channel_id=1, source_target_pairs={{0,2},{1,3},{2,0},{3,1},{4,6},{5,7},{6,4},{7,5},{8,10},{9,11},{10,... | collective-permute-start | bytes 1179656 | tf_op jit(solution)/shard_map/ppermute | solution.py:215
  79.2 21.7 %collective-permute-start.1 = (bf16[4,128,512]{2,1,0:T(8,128)(2,1)S(1)}, bf16[4,128,512]{2,1,0:T(8,128)(2,1)S(1)}, u32[]{:S(2)}, u32[]{:S(2)}) collective-permute-start(bf16[4,128,512]{2,1,0:T(8,128)(2,1)S(1)} %fusion), channel_id=1, source_target_pairs={{0,2},{1,3},{2,0},{3,1},{4,6},{5,7},{6,4},{7,5},{8,10},{9,11},{10,... | collective-permute-start | bytes 1572872 | tf_op jit(solution)/shard_map/ppermute | solution.py:215
  84.4 0.7 copy-start.4
  84.4 5.7 %copy-start.1 = (f32[8,96,512]{2,1,0:T(8,128)S(1)}, f32[8,96,512]{2,1,0:T(8,128)}, u32[]{:S(2)}) copy-start(f32[8,96,512]{2,1,0:T(8,128)} %copy-done) | copy-start | bytes 4718596
  91.3 13.4 %collective-permute-start.7 = (bf16[96,512]{1,0:T(8,128)(2,1)S(1)}, bf16[96,512]{1,0:T(8,128)(2,1)S(1)}, u32[]{:S(2)}, u32[]{:S(2)}) collective-permute-start(bf16[96,512]{1,0:T(8,128)(2,1)S(1)} %get-tuple-element.33), channel_id=1, source_target_pairs={{0,4},{1,5},{2,6},{3,7},{4,8},{5,9},{6,10},{7,11},{8,12},{9,13},{1... | collective-permute-start | bytes 294920 | tf_op jit(solution)/shard_map/ppermute | solution.py:220
  93.3 13.4 %collective-permute-start.8 = (bf16[96,512]{1,0:T(8,128)(2,1)S(1)}, bf16[96,512]{1,0:T(8,128)(2,1)S(1)}, u32[]{:S(2)}, u32[]{:S(2)}) collective-permute-start(bf16[96,512]{1,0:T(8,128)(2,1)S(1)} %get-tuple-element.35), channel_id=1, source_target_pairs={{0,8},{1,9},{2,10},{3,11},{4,12},{5,13},{6,14},{7,15},{8,0},{9,1},... | collective-permute-start | bytes 294920 | tf_op jit(solution)/shard_map/ppermute | solution.py:220
  95.2 11.5 %collective-permute-start.9 = (bf16[96,512]{1,0:T(8,128)(2,1)S(1)}, bf16[96,512]{1,0:T(8,128)(2,1)S(1)}, u32[]{:S(2)}, u32[]{:S(2)}) collective-permute-start(bf16[96,512]{1,0:T(8,128)(2,1)S(1)} %get-tuple-element.34), channel_id=1, source_target_pairs={{0,12},{1,13},{2,14},{3,15},{4,0},{5,1},{6,2},{7,3},{8,4},{9,5},{1... | collective-permute-start | bytes 294920 | tf_op jit(solution)/shard_map/ppermute | solution.py:220
  101.1 8.3 %collective-permute-start.2 = (bf16[128,512]{1,0:T(8,128)(2,1)S(1)}, bf16[128,512]{1,0:T(8,128)(2,1)S(1)}, u32[]{:S(2)}, u32[]{:S(2)}) collective-permute-start(bf16[128,512]{1,0:T(8,128)(2,1)S(1)} %get-tuple-element.30), channel_id=1, source_target_pairs={{0,4},{1,5},{2,6},{3,7},{4,8},{5,9},{6,10},{7,11},{8,12},{9,13},{1... | collective-permute-start | bytes 393224 | tf_op jit(solution)/shard_map/ppermute | solution.py:220
  103.0 10.8 %collective-permute-start.3 = (bf16[128,512]{1,0:T(8,128)(2,1)S(1)}, bf16[128,512]{1,0:T(8,128)(2,1)S(1)}, u32[]{:S(2)}, u32[]{:S(2)}) collective-permute-start(bf16[128,512]{1,0:T(8,128)(2,1)S(1)} %get-tuple-element.32), channel_id=1, source_target_pairs={{0,8},{1,9},{2,10},{3,11},{4,12},{5,13},{6,14},{7,15},{8,0},{9,1},... | collective-permute-start | bytes 393224 | tf_op jit(solution)/shard_map/ppermute | solution.py:220
  104.7 9.1 %collective-permute-start.4 = (bf16[128,512]{1,0:T(8,128)(2,1)S(1)}, bf16[128,512]{1,0:T(8,128)(2,1)S(1)}, u32[]{:S(2)}, u32[]{:S(2)}) collective-permute-start(bf16[128,512]{1,0:T(8,128)(2,1)S(1)} %get-tuple-element.31), channel_id=1, source_target_pairs={{0,12},{1,13},{2,14},{3,15},{4,0},{5,1},{6,2},{7,3},{8,4},{9,5},{1... | collective-permute-start | bytes 393224 | tf_op jit(solution)/shard_map/ppermute | solution.py:220

commit v2 on v1

--- a/solution.py
+++ b/solution.py
@@ -78,12 +78,29 @@
             high[pl.ds(part * nodes, nodes), :] = table_high
             low[pl.ds(part * nodes, nodes), :] = table_low
 
-    both = jnp.concatenate([pick(send_ref[0], 0, nodes), pick(recv_ref[0], 0, nodes)], 1)
+    size = edge_ref.shape[0]
+    both = jnp.concatenate(
+        [pick(block_row(send_ref, size), 0, nodes), pick(block_row(recv_ref, size), 0, nodes)], 1
+    )
     pre_ref[...] = (
         dot(edge_ref[...], w1_ref[pl.ds(2 * width, width), :])
         + dot(both, high[...])
         + dot(both, low[...])
     )
+
+
+def block_row(ref, size):
+    return ref[pl.ds(pl.multiple_of(pl.program_id(0) * size, size), size)].reshape(1, size)
+
+
+def accumulate(acc, value):
+    @pl.when(pl.program_id(0) == 0)
+    def _():
+        acc[...] = value
+
+    @pl.when(pl.program_id(0) > 0)
+    def _():
+        acc[...] += value
 
 
 def stash(acc, row0, keep_ref, send_ref, core):
@@ -111,9 +128,8 @@
         high, low = split(dot(halo_ref[...], wsend_ref[...]))
         table[pl.ds(0, halo), :] = high
         table[pl.ds(halo, halo), :] = low
-        gathered[...] = jnp.zeros_like(gathered)
-
-    far = pick(send_ref[0], nodes, halo)
+
+    far = pick(block_row(send_ref, size), nodes, halo)
     pre = pre_ref[...] + dot(far, table[pl.ds(0, halo), :]) + dot(far, table[pl.ds(halo, halo), :])
     hidden, slope = swish_both(pre)
     hidden_ref[...] = hidden
@@ -123,7 +139,7 @@
     inverse_ref[...] = inverse
     place = turn * size + lax.broadcasted_iota(jnp.int32, (size, 1), 0)
     message = jnp.where(place < scalar_ref[0], normed, 0.0).astype(BF)
-    gathered[...] += dot(pick_t(recv_ref[0], 0, nodes), message)
+    accumulate(gathered, dot(pick_t(block_row(recv_ref, size), 0, nodes), message))
 
     @pl.when(turn == pl.num_programs(0) - 1)
     def _():
@@ -144,51 +160,68 @@
         stash(acc, 0, keep_ref, away_ref, scalar_ref[1])
 
 
-def backward_kernel(
-    scalar_ref, send_ref, recv_ref, edge_ref, cotan_ref, hidden_ref, slope_ref, normed_ref, inverse_ref,
-    agg_ref, grad_ref, latent_ref, halo_ref, w1_ref, w2_ref,
-    edge_out, node_out, far_out, keep_ref, away_ref,
-    sent, received, acc,
+def mixed_kernel(
+    scalar_ref, recv_ref, cotan_ref, hidden_ref, normed_ref, inverse_ref, agg_ref,
+    mixed_out, keep_ref, away_ref, acc,
+):
+    turn = pl.program_id(0)
+    size = cotan_ref.shape[0]
+    place = turn * size + lax.broadcasted_iota(jnp.int32, (size, 1), 0)
+    grad_msg = jnp.where(
+        place < scalar_ref[0],
+        cotan_ref[...].astype(F32) + dot(pick(block_row(recv_ref, size), 0, agg_ref.shape[0]), agg_ref[...]),
+        0.0,
+    )
+    grad_mixed = norm_back(grad_msg, normed_ref[...], inverse_ref[...]).astype(BF)
+    mixed_out[...] = grad_mixed
+    accumulate(acc, dot_rows(hidden_ref[...], grad_mixed))
+
+    @pl.when(turn == pl.num_programs(0) - 1)
+    def _():
+        stash(acc, 0, keep_ref, away_ref, scalar_ref[1])
+
+
+def sender_kernel(
+    scalar_ref, send_ref, mixed_ref, slope_ref, w2_ref, w1_ref, grad_ref, latent_ref, halo_ref,
+    pre_out, node_out, far_out, keep_ref, away_ref, sent, acc,
 ):
     turn = pl.program_id(0)
     nodes, width = latent_ref.shape
     halo = halo_ref.shape[0]
-    size = edge_ref.shape[0]
-
-    @pl.when(turn == 0)
-    def _():
-        sent[...] = jnp.zeros_like(sent)
-        received[...] = jnp.zeros_like(received)
-        acc[...] = jnp.zeros_like(acc)
-
-    recv_row = recv_ref[0]
-    cotan = cotan_ref[...].astype(F32)
-    place = turn * size + lax.broadcasted_iota(jnp.int32, (size, 1), 0)
-    grad_msg = jnp.where(
-        place < scalar_ref[0], cotan + dot(pick(recv_row, 0, nodes), agg_ref[...]), 0.0
-    )
-    grad_mixed = norm_back(grad_msg, normed_ref[...], inverse_ref[...]).astype(BF)
-    grad_pre = (dot_last(grad_mixed, w2_ref[...]) * slope_ref[...]).astype(BF)
-    acc[pl.ds(3 * width, width), :] += dot_rows(hidden_ref[...], grad_mixed)
-    acc[pl.ds(2 * width, width), :] += dot_rows(edge_ref[...], grad_pre)
-    sent[...] += dot(pick_t(send_ref[0], 0, nodes + halo), grad_pre)
-    received[...] += dot(pick_t(recv_row, 0, nodes), grad_pre)
-    edge_out[...] = (cotan + dot_last(grad_pre, w1_ref[pl.ds(2 * width, width), :])).astype(BF)
+    grad_pre = (dot_last(mixed_ref[...], w2_ref[...]) * slope_ref[...]).astype(BF)
+    pre_out[...] = grad_pre
+    accumulate(sent, dot(pick_t(block_row(send_ref, mixed_ref.shape[0]), 0, nodes + halo), grad_pre))
 
     @pl.when(turn == pl.num_programs(0) - 1)
     def _():
-        w_send = w1_ref[pl.ds(0, width), :]
-        latent = latent_ref[...]
         near = sent[pl.ds(0, nodes), :].astype(BF)
         far = sent[pl.ds(nodes, halo), :].astype(BF)
+        far_out[...] = dot_last(far, w1_ref[...]).astype(BF)
+        acc[...] = dot_rows(latent_ref[...], near) + dot_rows(halo_ref[...], far)
+        stash(acc, 0, keep_ref, away_ref, scalar_ref[1])
+        node_out[...] = grad_ref[...] + dot_last(near, w1_ref[...])
+
+
+def receiver_kernel(
+    scalar_ref, recv_ref, pre_ref, edge_ref, w1_ref, part_ref, latent_ref,
+    node_out, keep_ref, away_ref, received, acc,
+):
+    turn = pl.program_id(0)
+    nodes, width = latent_ref.shape
+    grad_pre = pre_ref[...]
+    accumulate(acc.at[pl.ds(width, width), :], dot_rows(edge_ref[...], grad_pre))
+    accumulate(received, dot(pick_t(block_row(recv_ref, pre_ref.shape[0]), 0, nodes), grad_pre))
+
+    @pl.when(turn == pl.num_programs(0) - 1)
+    def _():
         into = received[...].astype(BF)
-        far_out[...] = dot_last(far, w_send).astype(BF)
-        node_out[...] = (
-            grad_ref[...] + dot_last(near, w_send) + dot_last(into, w1_ref[pl.ds(width, width), :])
-        )
-        acc[pl.ds(0, width), :] = dot_rows(latent, near) + dot_rows(halo_ref[...], far)
-        acc[pl.ds(width, width), :] = dot_rows(latent, into)
+        acc[pl.ds(0, width), :] = dot_rows(latent_ref[...], into)
         stash(acc, 0, keep_ref, away_ref, scalar_ref[1])
+        node_out[...] = part_ref[...] + dot_last(into, w1_ref[...])
+
+
+def edge_kernel(cotan_ref, pre_ref, w1_ref, out_ref):
+    out_ref[...] = (cotan_ref[...].astype(F32) + dot_last(pre_ref[...], w1_ref[...])).astype(BF)
 
 
 def return_kernel(rows_ref, back_ref, part_ref, out_ref):
@@ -203,23 +236,36 @@
     return pl.BlockSpec((size, width), lambda i: (i, 0))
 
 
-def reduce_scatter(keep, away, count):
-    place = lax.axis_index("dom")
-    _, rows, width = keep.shape
-    total = keep + lax.ppermute(away, "dom", [(i, i ^ 1) for i in range(count)]).astype(F32)
-    groups = count // 4
-    total = total.reshape(groups, 2, rows, width)
-    side = (place // 2) % 2
+def permute(value, pairs):
+    return lax.ppermute(value, "dom", pairs).astype(F32)
+
+
+def core_hop(keep, away, count):
+    return keep + permute(away, [(i, i ^ 1) for i in range(count)])
+
+
+def side_hop(total, count):
+    groups, rows, width = total.shape
+    total = total.reshape(groups // 2, 2, rows, width)
+    side = (lax.axis_index("dom") // 2) % 2
     mine = lax.dynamic_index_in_dim(total, side, 1, keepdims=False)
     other = lax.dynamic_index_in_dim(total, 1 - side, 1, keepdims=False).astype(BF)
-    total = mine + lax.ppermute(other, "dom", [(i, i ^ 2) for i in range(count)]).astype(F32)
-    group = place // 4
-    result = lax.dynamic_index_in_dim(total, group, 0, keepdims=False)
+    return mine + permute(other, [(i, i ^ 2) for i in range(count)])
+
+
+def group_hop(total, where, count):
+    groups = count // 4
+    slot = [where.index(g) if g in where else 0 for g in range(groups)]
+    group = lax.axis_index("dom") // 4
+    table = jnp.array(slot, jnp.int32)
+
+    def entry(step):
+        return lax.dynamic_index_in_dim(total, table[(group + step) % groups], 0, keepdims=False)
+
+    result = entry(0)
     for step in range(1, groups):
-        piece = lax.dynamic_index_in_dim(total, (group + step) % groups, 0, keepdims=False).astype(BF)
-        result = result + lax.ppermute(
-            piece, "dom", [(i, (i + 4 * step) % count) for i in range(count)]
-        ).astype(F32)
+        pairs = [(i, (i + 4 * step) % count) for i in range(count) if (i // 4 + step) % groups in where]
+        result = result + permute(entry(step).astype(BF), pairs)
     return result
 
 
@@ -247,9 +293,7 @@
     place = lax.axis_index("dom")
     scalars = jnp.stack([edge_count[0], (place % 2).astype(jnp.int32)])
     flat_rows = send_rows.reshape(1, halo)
-    send_row = senders.reshape(turns, 1, size)
-    recv_row = receivers.reshape(turns, 1, size)
-    row_spec = pl.BlockSpec((1, 1, size), lambda i: (i, 0, 0))
+    row_spec = whole((edges,))
     smem = pl.BlockSpec(memory_space=pltpu.SMEM)
     params = pltpu.CompilerParams(vmem_limit_bytes=VMEM_BYTES)
     unit = 2 * edges * width * width
@@ -278,7 +322,7 @@
         compiler_params=params,
         cost_estimate=cost(5.5, edges * width * 6),
         name="edge_early",
-    )(send_row, recv_row, edge_latent, node_latent, edge_w1)
+    )(senders, receivers, edge_latent, node_latent, edge_w1)
 
     node_rows = 3 * width // count
     edge_rows = 4 * width // count
@@ -314,49 +358,100 @@
         cost_estimate=cost(6, edges * width * 20),
         name="edge_forward",
     )(
-        scalars, send_row, recv_row, pre, incoming, edge_w1, edge_w2,
+        scalars, senders, receivers, pre, incoming, edge_w1, edge_w2,
         node_latent, node_cotan, node_w1, node_w2,
     )
 
-    node_share = reduce_scatter(node_keep, node_away, count)
-
-    grad_edge, node_part, far_grad, edge_keep, edge_away = pl.pallas_call(
-        backward_kernel,
+    half = count // 8
+    kept = [jax.ShapeDtypeStruct((half, edge_rows, width), F32), jax.ShapeDtypeStruct((half, edge_rows, width), BF)]
+    kept_spec = [whole((half, edge_rows, width))] * 2
+    square = whole((width, width))
+    per_edge = by_rows(size, width)
+    node_total = core_hop(node_keep, node_away, count)
+
+    grad_mixed, mix_keep, mix_away = pl.pallas_call(
+        mixed_kernel,
+        grid=(turns,),
+        in_specs=[smem, row_spec, per_edge, per_edge, per_edge, by_rows(size, 1), whole((nodes, width))],
+        out_specs=[per_edge] + kept_spec,
+        out_shape=[jax.ShapeDtypeStruct((edges, width), BF)] + kept,
+        scratch_shapes=[pltpu.VMEM((width, width), F32)],
+        compiler_params=params,
+        cost_estimate=cost(3, edges * width * 10),
+        name="grad_mixed",
+    )(scalars, receivers, edge_cotan, hidden, normed, inverse, agg_grad)
+
+    node_total = side_hop(node_total, count)
+    mix_total = core_hop(mix_keep, mix_away, count)
+
+    grad_pre, node_part, far_grad, send_keep, send_away = pl.pallas_call(
+        sender_kernel,
         grid=(turns,),
         in_specs=[
-            smem, row_spec, row_spec, by_rows(size, width), by_rows(size, width), by_rows(size, width),
-            by_rows(size, width), by_rows(size, width), by_rows(size, 1),
-            whole((nodes, width)), whole((nodes, width)), whole((nodes, width)), whole((halo, width)),
-            whole(edge_w1.shape), whole(edge_w2.shape),
-        ],
-        out_specs=[
-            by_rows(size, width), whole((nodes, width)), whole((halo, width)),
-            whole((count // 2, edge_rows, width)), whole((count // 2, edge_rows, width)),
-        ],
+            smem, row_spec, per_edge, per_edge, square, pl.BlockSpec((width, width), lambda i: (0, 0)),
+            whole((nodes, width)), whole((nodes, width)), whole((halo, width)),
+        ],
+        out_specs=[per_edge, whole((nodes, width)), whole((halo, width))] + kept_spec,
         out_shape=[
             jax.ShapeDtypeStruct((edges, width), BF),
             jax.ShapeDtypeStruct((nodes, width), F32),
             jax.ShapeDtypeStruct((halo, width), BF),
-            jax.ShapeDtypeStruct((count // 2, edge_rows, width), F32),
-            jax.ShapeDtypeStruct((count // 2, edge_rows, width), BF),
-        ],
-        scratch_shapes=[
-            pltpu.VMEM((nodes + halo, width), F32),
-            pltpu.VMEM((nodes, width), F32),
-            pltpu.VMEM((4 * width, width), F32),
-        ],
-        compiler_params=params,
-        cost_estimate=cost(10, edges * width * 20),
-        name="edge_backward",
-    )(
-        scalars, send_row, recv_row, edge_latent, edge_cotan, hidden, slope, normed, inverse,
-        agg_grad, grad_part, node_latent, incoming, edge_w1, edge_w2,
-    )
+        ] + kept,
+        scratch_shapes=[pltpu.VMEM((nodes + halo, width), F32), pltpu.VMEM((width, width), F32)],
+        compiler_params=params,
+        cost_estimate=cost(4, edges * width * 8),
+        name="grad_pre",
+    )(scalars, senders, grad_mixed, slope, edge_w2, edge_w1, grad_part, node_latent, incoming)
 
     returned = lax.all_to_all(
         far_grad.reshape(peers, slots, width), "dom", split_axis=0, concat_axis=0, tiled=True
     ).reshape(halo, width)
-    edge_share = reduce_scatter(edge_keep, edge_away, count)
+    mix_total = side_hop(mix_total, count)
+    send_total = core_hop(send_keep, send_away, count)
+
+    node_part, recv_keep, recv_away = pl.pallas_call(
+        receiver_kernel,
+        grid=(turns,),
+        in_specs=[
+            smem, row_spec, per_edge, per_edge, pl.BlockSpec((width, width), lambda i: (1, 0)),
+            whole((nodes, width)), whole((nodes, width)),
+        ],
+        out_specs=[whole((nodes, width))] + [whole((2 * half, edge_rows, width))] * 2,
+        out_shape=[
+            jax.ShapeDtypeStruct((nodes, width), F32),
+            jax.ShapeDtypeStruct((2 * half, edge_rows, width), F32),
+            jax.ShapeDtypeStruct((2 * half, edge_rows, width), BF),
+        ],
+        scratch_shapes=[pltpu.VMEM((nodes, width), F32), pltpu.VMEM((2 * width, width), F32)],
+        compiler_params=params,
+        cost_estimate=cost(3, edges * width * 4),
+        name="grad_recv",
+    )(scalars, receivers, grad_pre, edge_latent, edge_w1, node_part, node_latent)
+
+    send_total = side_hop(send_total, count)
+    recv_total = core_hop(recv_keep, recv_away, count)
+
+    grad_edge = pl.pallas_call(
+        edge_kernel,
+        grid=(turns,),
+        in_specs=[per_edge, per_edge, pl.BlockSpec((width, width), lambda i: (2, 0))],
+        out_specs=per_edge,
+        out_shape=jax.ShapeDtypeStruct((edges, width), BF),
+        compiler_params=params,
+        cost_estimate=cost(1, edges * width * 6),
+        name="grad_edge",
+    )(edge_cotan, grad_pre, edge_w1)
+
+    recv_total = side_hop(recv_total, count)
+    groups = count // 4
+    each = groups // 4
+    inner = list(range(each, 3 * each))
+    outer = list(range(each)) + list(range(3 * each, groups))
+    node_share = group_hop(node_total, list(range(groups)), count)
+    outer_share = group_hop(jnp.concatenate([send_total, mix_total], 0), outer, count)
+    inner_share = group_hop(recv_total, inner, count)
+    group = place // 4
+    edge_share = jnp.where((group >= each) & (group < 3 * each), inner_share, outer_share)
     grad_node = pl.pallas_call(
         return_kernel,
         out_shape=jax.ShapeDtypeStruct((nodes, width), F32),

time: 116 us -> 154 us (1.33)
  Pallas kernels: 56.2 us -> 72.3 us
  between operations: 1.43 us -> 16.8 us
  starting transfers between devices: 27.6 us -> 37.7 us
  waiting for transfers between devices: 17.5 us -> 12.1 us
  other arithmetic: 5.32 us -> 7.98 us
    pallas_call x1 -> x4, Pallas kernels: 22.1 us -> 38.1 us  [the longest x1 11.2 us: local(): pl.pallas_call(sender_kernel, grid=(turns,), in_specs=[smem, row_spec, pe...]
    ppermute x10 -> x17, starting transfers between devices: 14.2 us -> 24.5 us  [permute(): return lax.ppermute(value, 'dom', pairs).astype(F32)]
    all_to_all x1, waiting for transfers between devices: 4.82 us -> 0.01 us  [local(): lax.all_to_all(far_grad.reshape(peers, slots, width), 'dom', split_axis=0...]
    reshape x2 -> x0, local copies, waits for them, and re-layouts: 2.63 us -> none  [the longest x1 1.32 us: local(): send_row = senders.reshape(turns, 1, size)]
    select_n x0 -> x1, other arithmetic: none -> 1.9 us  [local(): jnp.where((group >= each) & (group < 3 * each), inner_share, outer_share)]
    ppermute x10 -> x17, waiting for transfers between devices: 12.7 us -> 12.1 us  [permute(): return lax.ppermute(value, 'dom', pairs).astype(F32)]
    add x6 -> x9, other arithmetic: 4.67 us -> 4.67 us  [the longest x4 2.22 us: side_hop(): return mine + permute(other, [(i, i ^ 2) for i in range(count)])]
  transfers between devices with their start and end apart: 12 -> 19, of which waited for: 5 -> 4; matrix products, arithmetic and copies ran while one was open for 7% -> 7% of each run, Pallas kernels for 32% -> 34%
where the time goes in v2:
time: 154 us; the launch traced here: 153 us
  Pallas kernels  72.3 us (47%)
  starting transfers between devices  37.7 us (24%)
  between operations  16.8 us (11%)
  waiting for transfers between devices  12.1 us (8%)
  other arithmetic  7.98 us (5%)
  local copies, waits for them, and re-layouts  5.98 us (4%)
    ppermute x17, starting transfers between devices, permute(): return lax.ppermute(value, 'dom', pairs).astype(F32)  24.5 us
    pallas_call x1, Pallas kernels, local(): pl.pallas_call(forward_kernel, grid=(turns,), in_specs=[smem, row_spec, r...  18.1 us
    ppermute x17, waiting for transfers between devices, permute(): return lax.ppermute(value, 'dom', pairs).astype(F32)  12.1 us
    pallas_call x1, Pallas kernels, local(): pl.pallas_call(early_kernel, grid=(turns,), in_specs=[row_spec, row_spec,...  11.4 us
    pallas_call x1, Pallas kernels, local(): pl.pallas_call(sender_kernel, grid=(turns,), in_specs=[smem, row_spec, pe...  11.2 us
    pallas_call x1, Pallas kernels, local(): pl.pallas_call(mixed_kernel, grid=(turns,), in_specs=[smem, row_spec, per...  10.4 us
    pallas_call x1, Pallas kernels, local(): pl.pallas_call(receiver_kernel, grid=(turns,), in_specs=[smem, row_spec,...  9.94 us
    all_to_all x1, starting transfers between devices, local(): lax.all_to_all(outgoing.reshape(peers, slots, width), 'dom', split_axis=0...  7.39 us
  transfers between devices with their start and end apart: 19, of which 4 were waited for; matrix products, arithmetic and copies ran while one was open for 7% of the time, Pallas kernels for 34%

profile of v2, /device:TPU:0, one launch (start us, length us, event | category | flops | bytes accessed | tf_op | source)
XLA Modules:
  0.0 152.8 jit_solution(15824894982333088602)
XLA Ops:
  0.6 1.4 reshape.54.rows_ref
  2.0 2.1 %halo_rows.1 = bf16[256,512]{1,0:T(8,128)(2,1)} custom-call(s32[1,256]{1,0:T(1,128)} %reshape.54.rows_ref, bf16[512,512]{1,0:T(8,128)(2,1)} %latent_ref.9), custom_call_target="tpu_custom_call" | custom-call | flops 134217728 | bytes 786432 | tf_op jit(solution)/shard_map/halo_rows/pallas_call | solution.py:304
  4.1 7.4 %all-to-all-start = ((bf16[16,16,512]{2,1,0:T(8,128)(2,1)}), bf16[16,16,512]{2,1,0:T(8,128)(2,1)S(1)}, u32[]{:S(2)}, u32[]{:S(2)}) async-start(bf16[16,16,512]{2,1,0:T(8,128)(2,1)} %bitcast.78), calls=%async_computation | async-start | bytes 524288 | tf_op jit(solution)/shard_map/all_to_all | solution.py:311
  11.6 1.5 fusion.27
  23.8 0.6 pad_add_fusion.scalar_ref
  29.4 11.4 %edge_early.1.pre_ref = f32[2560,512]{1,0:T(8,128)} custom-call(s32[2560]{0:T(1024)} %send_ref.5, s32[2560]{0:T(1024)} %recv_ref.7, bf16[2560,512]{1,0:T(8,128)(2,1)} %edge_ref.3, bf16[512,512]{1,0:T(8,128)(2,1)} %latent_ref.9, bf16[1536,512]{1,0:T(8,128)(2,1)} %w1_ref.7), custom_call_target="tpu_custom_call" | custom-call | flops 7381975040 | bytes 7864320 | tf_op jit(solution)/shard_map/edge_early/pallas_call | solution.py:315
  40.8 0.7 copy-done.5
  41.5 18.1 %edge_forward.1 = (bf16[2560,512]{1,0:T(8,128)(2,1)}, f32[2560,512]{1,0:T(8,128)}, f32[2560,512]{1,0:T(8,128)}, f32[2560,1]{1,0:T(8,128)}, bf16[512,512]{1,0:T(8...) custom-call(s32[2]{0:T(128)} %pad_add_fusion.scalar_ref, s32[2560]{0:T(1024)} %send_ref.5, ...), custom_call_target="tpu_custom_call" | custom-call | flops 8053063680 | bytes 26214400 | tf_op jit(solution)/shard_map/edge_forward/pallas_call | solution.py:329
  59.7 0.3 collective-permute-start.12
  60.0 10.4 %grad_mixed.1 = (bf16[2560,512]{1,0:T(8,128)(2,1)}, f32[2,128,512]{2,1,0:T(8,128)}, bf16[2,128,512]{2,1,0:T(8,128)(2,1)}) custom-call(s32[2]{0:T(128)} %pad_add_fusion.scalar_ref, s32[2560]{0:T(1024)} %recv_ref.7, bf16[2560,512]{1,0:T(8,128)(2,1)} %cotan_ref.5, bf16[2560,512]{1,0:T(8,128)(2,1)} %get-tuple-element.23.hidden_ref, ...), custom_call_target="tpu_custom_call" | custom-call | flops 4026531840 | bytes 13107200 | tf_op jit(solution)/shard_map/grad_mixed/pallas_call | solution.py:372
  70.4 0.3 collective-permute-start.7
  70.7 11.2 %grad_pre.1 = (bf16[2560,512]{1,0:T(8,128)(2,1)}, f32[512,512]{1,0:T(8,128)}, bf16[256,512]{1,0:T(8,128)(2,1)}, f32[2,128,512]{2,1,0:T(8,128)}, bf16[2,128,512]{2,1,0:T(8,128)(2,1)}) custom-call(s32[2]{0:T(128)} %pad_add_fusion.scalar_ref, s32[2560]{0:T(1024)} %send_ref.5, bf16[2560,512]{1,0:T(8,128)(2,1)} %get-tuple-element.27.mixed_ref, ...), custom_call_target="tpu_custom_call" | custom-call | flops 5368709120 | bytes 10485760 | tf_op jit(solution)/shard_map/grad_pre/pallas_call | solution.py:387
  81.9 9.9 %grad_recv.1 = (f32[512,512]{1,0:T(8,128)}, f32[4,128,512]{2,1,0:T(8,128)}, bf16[4,128,512]{2,1,0:T(8,128)(2,1)}) custom-call(s32[2]{0:T(128)} %pad_add_fusion.scalar_ref, s32[2560]{0:T(1024)} %recv_ref.7, bf16[2560,512]{1,0:T(8,128)(2,1)} %get-tuple-element.31.pre_ref, bf16[2560,512]{1,0:T(8,128)(2,1)} %edge_ref.3, bf16[1536,512]{1,0:T(8,128)(2,1)} %w1_ref.7, ...), custom_call_target="tpu_custom_call" | custom-call | flops 4026531840 | bytes 5242880 | tf_op jit(solution)/shard_map/grad_recv/pallas_call | solution.py:412
  91.9 0.3 collective-permute-start
  92.1 0.2 collective-permute-start.5
  92.4 5.9 %all-to-all-start.1 = ((bf16[16,16,512]{2,1,0:T(8,128)(2,1)}), bf16[16,16,512]{2,1,0:T(8,128)(2,1)S(1)}, u32[]{:S(2)}, u32[]{:S(2)}) async-start(bf16[16,16,512]{2,1,0:T(8,128)(2,1)} %bitcast.3), calls=%async_computation.1 | async-start | bytes 524288 | tf_op jit(solution)/shard_map/all_to_all | solution.py:406
  98.3 6.5 %grad_edge.1 = bf16[2560,512]{1,0:T(8,128)(2,1)} custom-call(bf16[2560,512]{1,0:T(8,128)(2,1)} %cotan_ref.5, bf16[2560,512]{1,0:T(8,128)(2,1)} %get-tuple-element.31.pre_ref, bf16[1536,512]{1,0:T(8,128)(2,1)} %w1_ref.7), custom_call_target="tpu_custom_call" | custom-call | flops 1342177280 | bytes 7864320 | tf_op jit(solution)/shard_map/grad_edge/pallas_call | solution.py:434
  104.8 0.1 convert_add_fusion.2
  104.9 2.0 %collective-permute-start.8 = (bf16[1,128,512]{2,1,0:T(8,128)(2,1)S(1)}, bf16[1,128,512]{2,1,0:T(8,128)(2,1)S(1)}, u32[]{:S(2)}, u32[]{:S(2)}) collective-permute-start(bf16[1,128,512]{2,1,0:T(8,128)(2,1)S(1)} %dynamic-slice_convert_fusion), channel_id=1, source_target_pairs={{0,2},{1,3},{2,0},{3,1},{4,6},{5,7},{6,4},{7,5},{8,10},{9,11},{10,... | collective-permute-start | bytes 393224 | tf_op jit(solution)/shard_map/ppermute | solution.py:240
  106.9 0.1 convert_add_fusion.3
  107.0 0.2 collective-permute-start.6
  107.2 4.1 %collective-permute-done.8 = bf16[1,128,512]{2,1,0:T(8,128)(2,1)S(1)} collective-permute-done((bf16[1,128,512]{2,1,0:T(8,128)(2,1)S(1)}, bf16[1,128,512]{2,1,0:T(8,128)(2,1)S(1)}, u32[]{:S(2)}, u32[]{:S(2)}) %collective-permute-start.8) | collective-permute-done | bytes 131104 | tf_op jit(solution)/shard_map/ppermute | solution.py:240
  111.3 2.5 %collective-permute-done.6 = bf16[1,128,512]{2,1,0:T(8,128)(2,1)S(1)} collective-permute-done((bf16[1,128,512]{2,1,0:T(8,128)(2,1)S(1)}, bf16[1,128,512]{2,1,0:T(8,128)(2,1)S(1)}, u32[]{:S(2)}, u32[]{:S(2)}) %collective-permute-start.6) | collective-permute-done | bytes 131104 | tf_op jit(solution)/shard_map/ppermute | solution.py:240
  113.9 0.2 convert_add_fusion.1
  114.1 0.7 fusion.1
  114.8 1.4 collective-permute-start.1
  116.2 1.4 convert_add_fusion
  117.7 0.8 fusion
  118.5 0.6 collective-permute-start.13
  119.1 0.8 fusion.22
  119.9 1.3 collective-permute-start.10
  121.2 5.2 %collective-permute-start.11 = (bf16[128,512]{1,0:T(8,128)(2,1)}, bf16[128,512]{1,0:T(8,128)(2,1)}, u32[]{:S(2)}, u32[]{:S(2)}) collective-permute-start(bf16[128,512]{1,0:T(8,128)(2,1)} %get-tuple-element.50), channel_id=1, source_target_pairs={{0,12},{1,13},{2,14},{3,15},{4,0},{5,1},{6,2},{7,3},{16,28},{17,29... | collective-permute-start | bytes 393224 | tf_op jit(solution)/shard_map/ppermute | solution.py:240
  126.3 1.3 collective-permute-start.9
  127.7 0.7 copy-done.1
  128.3 2.6 %halo_return.1 = f32[512,512]{1,0:T(8,128)} custom-call(s32[1,256]{1,0:T(1,128)} %reshape.54.rows_ref, bf16[256,512]{1,0:T(8,128)(2,1)} %bitcast.77, f32[512,512]{1,0:T(8,128)} %get-tuple-element.33.part_ref), custom_call_target="tpu_custom_call" | custom-call | flops 134217728 | bytes 2097152 | tf_op jit(solution)/shard_map/halo_return/pallas_call | solution.py:455
  130.9 1.0 bitcast_add_fusion.1
  132.0 0.1 fusion.18
  132.0 3.8 %collective-permute-start.2 = (bf16[128,512]{1,0:T(8,128)(2,1)S(1)}, bf16[128,512]{1,0:T(8,128)(2,1)S(1)}, u32[]{:S(2)}, u32[]{:S(2)}) collective-permute-start(bf16[128,512]{1,0:T(8,128)(2,1)S(1)} %get-tuple-element.45), channel_id=1, source_target_pairs={{0,4},{1,5},{2,6},{3,7},{4,8},{5,9},{6,10},{7,11},{16,20},{17,21},... | collective-permute-start | bytes 393224 | tf_op jit(solution)/shard_map/ppermute | solution.py:240
  135.8 1.3 collective-permute-start.3
  137.1 0.7 collective-permute-start.4
  137.8 1.1 bitcast_add_fusion
  139.0 0.7 collective-permute-start.14
  139.7 3.5 %collective-permute-start.15 = (bf16[96,512]{1,0:T(8,128)(2,1)S(1)}, bf16[96,512]{1,0:T(8,128)(2,1)S(1)}, u32[]{:S(2)}, u32[]{:S(2)}) collective-permute-start(bf16[96,512]{1,0:T(8,128)(2,1)S(1)} %get-tuple-element.44), channel_id=1, source_target_pairs={{0,8},{1,9},{2,10},{3,11},{4,12},{5,13},{6,14},{7,15},{8,0},{9,1},... | collective-permute-start | bytes 294920 | tf_op jit(solution)/shard_map/ppermute | solution.py:240
  143.2 1.5 collective-permute-start.16
  144.7 1.9 %fusion.9 = f32[128,512]{1,0:T(8,128)} fusion(s32[]{:T(128)S(6)} %select_n.162, f32[1,128,512]{2,1,0:T(8,128)S(1)} %convert_add_fusion.5, f32[1,128,512]{2,1,0:T(8,128)S(1)} %convert_add_fusion.4, bf16[128,512]{1,0:T(8,128)(2,1)} %collective-permute-done.11, bf16[128,512]{1,0:T(8,128)(2,1)} %collective-permute-done.10, ...), kind=kLoop, calls=%fused_computation.25 | loop fusion | flops 917504 | bytes 1835017 | tf_op jit(solution)/shard_map/jit(_where)/select_n | solution.py:454
  146.6 2.5 %collective-permute-done.14 = bf16[96,512]{1,0:T(8,128)(2,1)S(1)} collective-permute-done((bf16[96,512]{1,0:T(8,128)(2,1)S(1)}, bf16[96,512]{1,0:T(8,128)(2,1)S(1)}, u32[]{:S(2)}, u32[]{:S(2)}) %collective-permute-start.14) | collective-permute-done | bytes 98336 | tf_op jit(solution)/shard_map/ppermute | solution.py:240
  149.1 3.0 %collective-permute-done.15 = bf16[96,512]{1,0:T(8,128)(2,1)S(1)} collective-permute-done((bf16[96,512]{1,0:T(8,128)(2,1)S(1)}, bf16[96,512]{1,0:T(8,128)(2,1)S(1)}, u32[]{:S(2)}, u32[]{:S(2)}) %collective-permute-start.15) | collective-permute-done | bytes 98336 | tf_op jit(solution)/shard_map/ppermute | solution.py:240
  152.1 0.7 fusion.17
  (32 shorter events, 0.2 us)
Async XLA Ops:
  4.1 36.7 %all-to-all-start = ((bf16[16,16,512]{2,1,0:T(8,128)(2,1)}), bf16[16,16,512]{2,1,0:T(8,128)(2,1)S(1)}, u32[]{:S(2)}, u32[]{:S(2)}) async-start(bf16[16,16,512]{2,1,0:T(8,128)(2,1)} %bitcast.78), calls=%async_computation | async-start | bytes 524288 | tf_op jit(solution)/shard_map/all_to_all | solution.py:311
  40.8 0.7 copy-start.5
  59.7 56.6 %collective-permute-start.12 = (bf16[8,96,512]{2,1,0:T(8,128)(2,1)}, bf16[8,96,512]{2,1,0:T(8,128)(2,1)}, u32[]{:S(2)}, u32[]{:S(2)}) collective-permute-start(bf16[8,96,512]{2,1,0:T(8,128)(2,1)} %get-tuple-element.41), channel_id=1, source_target_pairs={{0,1},{1,0},{2,3},{3,2},{4,5},{5,4},{6,7},{7,6},{8,9},{9,8},{10,11... | collective-permute-start | bytes 2359304 | tf_op jit(solution)/shard_map/ppermute | solution.py:240
  70.4 34.4 %collective-permute-start.7 = (bf16[2,128,512]{2,1,0:T(8,128)(2,1)}, bf16[2,128,512]{2,1,0:T(8,128)(2,1)S(1)}, u32[]{:S(2)}, u32[]{:S(2)}) collective-permute-start(bf16[2,128,512]{2,1,0:T(8,128)(2,1)} %get-tuple-element.39), channel_id=1, source_target_pairs={{0,1},{1,0},{2,3},{3,2},{4,5},{5,4},{6,7},{7,6},{8,9},{9,8},{10,11... | collective-permute-start | bytes 786440 | tf_op jit(solution)/shard_map/ppermute | solution.py:240
  81.9 10.2 %copy-start.6 = (bf16[2,128,512]{2,1,0:T(8,128)(2,1)S(1)}, bf16[2,128,512]{2,1,0:T(8,128)(2,1)}, u32[]{:S(2)}) copy-start(bf16[2,128,512]{2,1,0:T(8,128)(2,1)} %get-tuple-element.37) | copy-start | bytes 786436
  91.9 22.0 %collective-permute-start = (bf16[4,128,512]{2,1,0:T(8,128)(2,1)}, bf16[4,128,512]{2,1,0:T(8,128)(2,1)S(1)}, u32[]{:S(2)}, u32[]{:S(2)}) collective-permute-start(bf16[4,128,512]{2,1,0:T(8,128)(2,1)} %get-tuple-element.35), channel_id=1, source_target_pairs={{0,1},{1,0},{2,3},{3,2},{4,5},{5,4},{6,7},{7,6},{8,9},{9,8},{10,11... | collective-permute-start | bytes 1572872 | tf_op jit(solution)/shard_map/ppermute | solution.py:240
  92.1 14.8 %collective-permute-start.5 = (bf16[2,128,512]{2,1,0:T(8,128)(2,1)S(1)}, bf16[2,128,512]{2,1,0:T(8,128)(2,1)S(1)}, u32[]{:S(2)}, u32[]{:S(2)}) collective-permute-start(bf16[2,128,512]{2,1,0:T(8,128)(2,1)S(1)} %copy-done.6), channel_id=1, source_target_pairs={{0,1},{1,0},{2,3},{3,2},{4,5},{5,4},{6,7},{7,6},{8,9},{9,8},{10,11... | collective-permute-start | bytes 786440 | tf_op jit(solution)/shard_map/ppermute | solution.py:240
  92.4 35.3 %all-to-all-start.1 = ((bf16[16,16,512]{2,1,0:T(8,128)(2,1)}), bf16[16,16,512]{2,1,0:T(8,128)(2,1)S(1)}, u32[]{:S(2)}, u32[]{:S(2)}) async-start(bf16[16,16,512]{2,1,0:T(8,128)(2,1)} %bitcast.3), calls=%async_computation.1 | async-start | bytes 524288 | tf_op jit(solution)/shard_map/all_to_all | solution.py:406
  98.2 6.6 %copy-start.3 = (f32[2,128,512]{2,1,0:T(8,128)S(1)}, f32[2,128,512]{2,1,0:T(8,128)}, u32[]{:S(2)}) copy-start(f32[2,128,512]{2,1,0:T(8,128)} %get-tuple-element.38) | copy-start | bytes 1572868
  98.3 8.7 %copy-start.4 = (f32[2,128,512]{2,1,0:T(8,128)S(1)}, f32[2,128,512]{2,1,0:T(8,128)}, u32[]{:S(2)}) copy-start(f32[2,128,512]{2,1,0:T(8,128)} %get-tuple-element.36) | copy-start | bytes 1572868
  104.8 9.1 %copy-start.2 = (f32[4,128,512]{2,1,0:T(8,128)S(1)}, f32[4,128,512]{2,1,0:T(8,128)}, u32[]{:S(2)}) copy-start(f32[4,128,512]{2,1,0:T(8,128)} %get-tuple-element.34) | copy-start | bytes 3145732
  104.9 6.4 %collective-permute-start.8 = (bf16[1,128,512]{2,1,0:T(8,128)(2,1)S(1)}, bf16[1,128,512]{2,1,0:T(8,128)(2,1)S(1)}, u32[]{:S(2)}, u32[]{:S(2)}) collective-permute-start(bf16[1,128,512]{2,1,0:T(8,128)(2,1)S(1)} %dynamic-slice_convert_fusion), channel_id=1, source_target_pairs={{0,2},{1,3},{2,0},{3,1},{4,6},{5,7},{6,4},{7,5},{8,10},{9,11},{10,... | collective-permute-start | bytes 393224 | tf_op jit(solution)/shard_map/ppermute | solution.py:240
  107.0 9.3 %copy-start = (f32[8,96,512]{2,1,0:T(8,128)S(1)}, f32[8,96,512]{2,1,0:T(8,128)}, u32[]{:S(2)}) copy-start(f32[8,96,512]{2,1,0:T(8,128)} %get-tuple-element.40) | copy-start | bytes 4718596
  107.0 6.8 %collective-permute-start.6 = (bf16[1,128,512]{2,1,0:T(8,128)(2,1)S(1)}, bf16[1,128,512]{2,1,0:T(8,128)(2,1)S(1)}, u32[]{:S(2)}, u32[]{:S(2)}) collective-permute-start(bf16[1,128,512]{2,1,0:T(8,128)(2,1)S(1)} %dynamic-slice_convert_fusion.1), channel_id=1, source_target_pairs={{0,2},{1,3},{2,0},{3,1},{4,6},{5,7},{6,4},{7,5},{8,10},{9,11},{10,... | collective-permute-start | bytes 393224 | tf_op jit(solution)/shard_map/ppermute | solution.py:240
  114.8 16.1 %collective-permute-start.1 = (bf16[2,128,512]{2,1,0:T(8,128)(2,1)}, bf16[2,128,512]{2,1,0:T(8,128)(2,1)}, u32[]{:S(2)}, u32[]{:S(2)}) collective-permute-start(bf16[2,128,512]{2,1,0:T(8,128)(2,1)} %fusion.1), channel_id=1, source_target_pairs={{0,2},{1,3},{2,0},{3,1},{4,6},{5,7},{6,4},{7,5},{8,10},{9,11},{10,... | collective-permute-start | bytes 786440 | tf_op jit(solution)/shard_map/ppermute | solution.py:240
  118.5 18.6 %collective-permute-start.13 = (bf16[4,96,512]{2,1,0:T(8,128)(2,1)}, bf16[4,96,512]{2,1,0:T(8,128)(2,1)}, u32[]{:S(2)}, u32[]{:S(2)}) collective-permute-start(bf16[4,96,512]{2,1,0:T(8,128)(2,1)} %fusion), channel_id=1, source_target_pairs={{0,2},{1,3},{2,0},{3,1},{4,6},{5,7},{6,4},{7,5},{8,10},{9,11},{10,... | collective-permute-start | bytes 1179656 | tf_op jit(solution)/shard_map/ppermute | solution.py:240
  119.9 15.9 %collective-permute-start.10 = (bf16[128,512]{1,0:T(8,128)(2,1)}, bf16[128,512]{1,0:T(8,128)(2,1)}, u32[]{:S(2)}, u32[]{:S(2)}) collective-permute-start(bf16[128,512]{1,0:T(8,128)(2,1)} %get-tuple-element.49), channel_id=1, source_target_pairs={{4,12},{5,13},{6,14},{7,15},{8,0},{9,1},{10,2},{11,3},{20,28},{21,... | collective-permute-start | bytes 393224 | tf_op jit(solution)/shard_map/ppermute | solution.py:240
  121.2 17.8 %collective-permute-start.11 = (bf16[128,512]{1,0:T(8,128)(2,1)}, bf16[128,512]{1,0:T(8,128)(2,1)}, u32[]{:S(2)}, u32[]{:S(2)}) collective-permute-start(bf16[128,512]{1,0:T(8,128)(2,1)} %get-tuple-element.50), channel_id=1, source_target_pairs={{0,12},{1,13},{2,14},{3,15},{4,0},{5,1},{6,2},{7,3},{16,28},{17,29... | collective-permute-start | bytes 393224 | tf_op jit(solution)/shard_map/ppermute | solution.py:240
  126.3 13.4 %collective-permute-start.9 = (bf16[128,512]{1,0:T(8,128)(2,1)S(1)}, bf16[128,512]{1,0:T(8,128)(2,1)}, u32[]{:S(2)}, u32[]{:S(2)}) collective-permute-start(bf16[128,512]{1,0:T(8,128)(2,1)S(1)} %get-tuple-element.48), channel_id=1, source_target_pairs={{8,12},{9,13},{10,14},{11,15},{12,0},{13,1},{14,2},{15,3},{24,28},... | collective-permute-start | bytes 393224 | tf_op jit(solution)/shard_map/ppermute | solution.py:240
  127.6 0.7 copy-start.1
  132.0 11.2 %collective-permute-start.2 = (bf16[128,512]{1,0:T(8,128)(2,1)S(1)}, bf16[128,512]{1,0:T(8,128)(2,1)S(1)}, u32[]{:S(2)}, u32[]{:S(2)}) collective-permute-start(bf16[128,512]{1,0:T(8,128)(2,1)S(1)} %get-tuple-element.45), channel_id=1, source_target_pairs={{0,4},{1,5},{2,6},{3,7},{4,8},{5,9},{6,10},{7,11},{16,20},{17,21},... | collective-permute-start | bytes 393224 | tf_op jit(solution)/shard_map/ppermute | solution.py:240
  135.8 8.9 %collective-permute-start.3 = (bf16[128,512]{1,0:T(8,128)(2,1)S(1)}, bf16[128,512]{1,0:T(8,128)(2,1)S(1)}, u32[]{:S(2)}, u32[]{:S(2)}) collective-permute-start(bf16[128,512]{1,0:T(8,128)(2,1)S(1)} %get-tuple-element.47), channel_id=1, source_target_pairs={{0,8},{1,9},{2,10},{3,11},{12,4},{13,5},{14,6},{15,7},{16,24},{17,... | collective-permute-start | bytes 393224 | tf_op jit(solution)/shard_map/ppermute | solution.py:240
  137.1 7.6 %collective-permute-start.4 = (bf16[128,512]{1,0:T(8,128)(2,1)S(1)}, bf16[128,512]{1,0:T(8,128)(2,1)S(1)}, u32[]{:S(2)}, u32[]{:S(2)}) collective-permute-start(bf16[128,512]{1,0:T(8,128)(2,1)S(1)} %get-tuple-element.46), channel_id=1, source_target_pairs={{8,4},{9,5},{10,6},{11,7},{12,8},{13,9},{14,10},{15,11},{24,20},{2... | collective-permute-start | bytes 393224 | tf_op jit(solution)/shard_map/ppermute | solution.py:240
  139.0 10.1 %collective-permute-start.14 = (bf16[96,512]{1,0:T(8,128)(2,1)S(1)}, bf16[96,512]{1,0:T(8,128)(2,1)S(1)}, u32[]{:S(2)}, u32[]{:S(2)}) collective-permute-start(bf16[96,512]{1,0:T(8,128)(2,1)S(1)} %get-tuple-element.42), channel_id=1, source_target_pairs={{0,4},{1,5},{2,6},{3,7},{4,8},{5,9},{6,10},{7,11},{8,12},{9,13},{1... | collective-permute-start | bytes 294920 | tf_op jit(solution)/shard_map/ppermute | solution.py:240
  139.7 12.4 %collective-permute-start.15 = (bf16[96,512]{1,0:T(8,128)(2,1)S(1)}, bf16[96,512]{1,0:T(8,128)(2,1)S(1)}, u32[]{:S(2)}, u32[]{:S(2)}) collective-permute-start(bf16[96,512]{1,0:T(8,128)(2,1)S(1)} %get-tuple-element.44), channel_id=1, source_target_pairs={{0,8},{1,9},{2,10},{3,11},{4,12},{5,13},{6,14},{7,15},{8,0},{9,1},... | collective-permute-start | bytes 294920 | tf_op jit(solution)/shard_map/ppermute | solution.py:240
  143.2 8.9 %collective-permute-start.16 = (bf16[96,512]{1,0:T(8,128)(2,1)S(1)}, bf16[96,512]{1,0:T(8,128)(2,1)S(1)}, u32[]{:S(2)}, u32[]{:S(2)}) collective-permute-start(bf16[96,512]{1,0:T(8,128)(2,1)S(1)} %get-tuple-element.43), channel_id=1, source_target_pairs={{0,12},{1,13},{2,14},{3,15},{4,0},{5,1},{6,2},{7,3},{8,4},{9,5},{1... | collective-permute-start | bytes 294920 | tf_op jit(solution)/shard_map/ppermute | solution.py:240

commit v3 on v1

v3 whole, which is shorter than its diff:
```python
import functools

import jax
import jax.numpy as jnp
from jax import lax
from jax.experimental import pallas as pl
from jax.experimental.pallas import tpu as pltpu
from jax.sharding import PartitionSpec as P

BF = jnp.bfloat16
F32 = jnp.float32
VMEM_BYTES = 58 * 1024 * 1024
ANY = pl.BlockSpec(memory_space=pl.ANY)
VMEM = pl.BlockSpec(memory_space=pltpu.VMEM)
SMEM = pl.BlockSpec(memory_space=pltpu.SMEM)
DMA = pltpu.SemaphoreType.DMA


def dot(left, right):
    return jnp.dot(left, right, preferred_element_type=F32)


def dot_rows(left, right):
    return lax.dot_general(left, right, (((0,), (0,)), ((), ())), preferred_element_type=F32)


def dot_last(left, right):
    return lax.dot_general(left, right, (((1,), (1,)), ((), ())), preferred_element_type=F32)


def pick(row, base, count):
    size = row.shape[1]
    column = jnp.broadcast_to(row, (128, size)).T
    wide = jnp.concatenate([column] * (count // 128), 1)
    place = lax.broadcasted_iota(jnp.int32, (size, count), 1) + base
    return jnp.where(wide == place, 1.0, 0.0).astype(BF)


def pick_t(row, base, count):
    size = row.shape[1]
    place = lax.broadcasted_iota(jnp.int32, (count, size), 0) + base
    return jnp.where(jnp.broadcast_to(row, (count, size)) == place, 1.0, 0.0).astype(BF)


def pick_slots(rows_ref, count):
    _, peers, slots = rows_ref.shape
    same = lax.broadcasted_iota(jnp.int32, (slots, slots), 0) == lax.broadcasted_iota(
        jnp.int32, (slots, slots), 1
    )
    place = lax.broadcasted_iota(jnp.int32, (slots, count), 1)
    parts = []
    for peer in range(peers):
        row = jnp.broadcast_to(rows_ref[0, peer : peer + 1, :], (slots, slots)).astype(F32)
        column = jnp.sum(jnp.where(same, row, 0.0), 1, keepdims=True).astype(jnp.int32)
        parts.append(jnp.where(column == place, 1.0, 0.0).astype(BF))
    return jnp.concatenate(parts, 0)


def normalize(mixed):
    centre = mixed - jnp.mean(mixed, -1, keepdims=True)
    inverse = lax.rsqrt(jnp.mean(centre * centre, -1, keepdims=True) + 1e-05)
    return centre * inverse, inverse


def norm_back(grad, normed, inverse):
    return inverse * (
        grad
        - jnp.mean(grad, -1, keepdims=True)
        - normed * jnp.mean(grad * normed, -1, keepdims=True)
    )


def swish_both(value):
    sig = jax.nn.sigmoid(value)
    hidden = value * sig
    return hidden.astype(BF), sig * (1.0 + value * (1.0 - sig))


def begin(source, target, sem):
    copy = pltpu.make_async_copy(source, target, sem)
    copy.start()
    return copy


class Blocks:
    def __init__(self, source, target, sems, size):
        self.source, self.target, self.sems, self.size = source, target, sems, size
        self.turns = source.shape[0] // size

    def copy(self, turn):
        rows = pl.ds(pl.multiple_of(turn * self.size, self.size), self.size)
        return pltpu.make_async_copy(self.source.at[rows, :], self.target.at[rows, :], self.sems.at[turn])

    def start(self, turn):
        self.copy(turn).start()

    def start_all(self):
        for turn in range(self.turns):
            self.start(turn)

    def wait(self, turn):
        self.copy(turn).wait()

    def wait_all(self):
        for turn in range(self.turns):
            self.wait(turn)


def to_row(column):
    return jnp.broadcast_to(column, (column.shape[0], 128)).T[0:1, :]


def to_column(row):
    return jnp.broadcast_to(row, (128, row.shape[1])).T[:, 0:1]


def block_row(ref, turn, size):
    return ref[pl.ds(pl.multiple_of(turn * size, size), size)].reshape(1, size)


def each_block(turns, body):
    def step(turn, carry):
        body(turn)
        return carry

    lax.fori_loop(0, turns, step, 0)


def rows_kernel(rows_ref, latent_ref, out_ref):
    out_ref[...] = dot(pick_slots(rows_ref, latent_ref.shape[0]), latent_ref[...]).astype(BF)


def return_kernel(rows_ref, back_ref, part_ref, out_ref):
    out_ref[...] = part_ref[...] + dot_rows(pick_slots(rows_ref, out_ref.shape[0]), back_ref[...])


def early_kernel(
    size, send_ref, recv_ref, edge_h, latent_h, w1_h, pre_h,
    edge, latent, w1, pre, table, edge_sem, out_sem, one_sem,
):
    nodes, width = latent.shape
    first = [
        begin(latent_h, latent, one_sem.at[0]),
        begin(w1_h.at[pl.ds(0, 2 * width), :], w1, one_sem.at[1]),
        begin(w1_h.at[pl.ds(2 * width, width), :], table.at[pl.ds(2 * nodes, width), :], one_sem.at[2]),
    ]
    edges = Blocks(edge_h, edge, edge_sem, size)
    outs = Blocks(pre, pre_h, out_sem, size)
    edges.start_all()
    for copy in first:
        copy.wait()
    for part in range(2):
        table[pl.ds(part * nodes, nodes), :] = dot(latent[...], w1[pl.ds(part * width, width), :]).astype(BF)

    def body(turn):
        rows = pl.ds(pl.multiple_of(turn * size, size), size)
        sender = pick(block_row(send_ref, turn, size), 0, nodes)
        receiver = pick(block_row(recv_ref, turn, size), 0, nodes)
        edges.wait(turn)
        pre[rows, :] = dot(jnp.concatenate([sender, receiver, edge[rows, :]], 1), table[...])
        outs.start(turn)

    each_block(edges.turns, body)
    outs.wait_all()


def stash(acc, keep, away, core):
    groups, rows, _ = keep.shape
    for group in range(groups):
        mine = pl.multiple_of((2 * group + core) * rows, 16)
        other = pl.multiple_of((2 * group + 1 - core) * rows, 16)
        keep[group] = acc[pl.ds(mine, rows), :]
        away[group] = acc[pl.ds(other, rows), :].astype(BF)


def forward_kernel(
    size, scalar_ref, send_ref, recv_ref, pre_h, halo_h, w1_h, w2_h, latent_h, cotan_h, nw1_h, nw2_h,
    hidden_h, slope_h, normed_h, inverse_ref, agg_h, grad_h, keep_h, away_h,
    pre, halo, wsend, w2, latent, cotan, nw1, nw2, hidden, slope, normed, agg, grad, keep, away,
    table, gathered, acc, pre_sem, out_sem, one_sem, end_sem,
):
    nodes, width = latent.shape
    far_rows = halo.shape[0]
    first = [
        begin(halo_h, halo, one_sem.at[0]),
        begin(w1_h.at[pl.ds(0, width), :], wsend, one_sem.at[1]),
    ]
    pres = Blocks(pre_h, pre, pre_sem, size)
    pres.start_all()
    second = begin(w2_h, w2, one_sem.at[2])
    later = [
        begin(source, target, one_sem.at[3 + place])
        for place, (source, target) in enumerate(
            [(latent_h, latent), (cotan_h, cotan), (nw1_h, nw1), (nw2_h, nw2)]
        )
    ]
    outs = [
        Blocks(hidden, hidden_h, out_sem.at[0], size),
        Blocks(slope, slope_h, out_sem.at[1], size),
        Blocks(normed, normed_h, out_sem.at[2], size),
    ]
    gathered[...] = jnp.zeros_like(gathered)
    for copy in first:
        copy.wait()
    table[...] = dot(halo[...], wsend[...]).astype(BF)
    second.wait()

    def body(turn):
        pres.wait(turn)
        rows = pl.ds(pl.multiple_of(turn * size, size), size)
        far = pick(block_row(send_ref, turn, size), nodes, far_rows)
        value = pre[rows, :] + dot(far, table[...])
        low_hidden, slopes = swish_both(value)
        hidden[rows, :] = low_hidden
        slope[rows, :] = slopes.astype(BF)
        unit, scale = normalize(dot(low_hidden, w2[...]))
        normed[rows, :] = unit
        inverse_ref[turn] = to_row(scale)
        for out in outs:
            out.start(turn)
        place = turn * size + lax.broadcasted_iota(jnp.int32, (size, 1), 0)
        message = jnp.where(place < scalar_ref[0], unit, 0.0).astype(BF)
        gathered[...] += dot(pick_t(block_row(recv_ref, turn, size), 0, nodes), message)

    each_block(pres.turns, body)
    for copy in later:
        copy.wait()
    sums = gathered[...].astype(BF)
    w_node = nw1[pl.ds(0, width), :]
    w_agg = nw1[pl.ds(width, width), :]
    node_hidden, node_slope = swish_both(dot(latent[...], w_node) + dot(sums, w_agg))
    node_normed, node_inverse = normalize(dot(node_hidden, nw2[...]))
    node_cotan = cotan[...].astype(F32)
    grad_out = norm_back(node_cotan, node_normed, node_inverse).astype(BF)
    acc[pl.ds(2 * width, width), :] = dot_rows(node_hidden, grad_out)
    grad_pre = (dot_last(grad_out, nw2[...]) * node_slope).astype(BF)
    agg[...] = dot_last(grad_pre, w_agg).astype(BF)
    acc[pl.ds(0, width), :] = dot_rows(latent[...], grad_pre)
    acc[pl.ds(width, width), :] = dot_rows(sums, grad_pre)
    stash(acc, keep, away, scalar_ref[1])
    grad[...] = node_cotan + dot_last(grad_pre, w_node)
    last = [
        begin(source, target, end_sem.at[place])
        for place, (source, target) in enumerate(
            [(agg, agg_h), (grad, grad_h), (keep, keep_h), (away, away_h)]
        )
    ]
    for out in outs:
        out.wait_all()
    for copy in last:
        copy.wait()


def edge_back_kernel(
    size, scalar_ref, recv_ref, inverse_ref, cotan_h, normed_h, slope_h, hidden_h, edge_h, agg_h, w2_h,
    pre_h, keep_h, away_h,
    cotan, normed, slope, hidden, edge, agg, w2, pre, keep, away,
    acc, in_sem, out_sem, one_sem, end_sem,
):
    nodes, width = agg.shape
    first = [begin(agg_h, agg, one_sem.at[0])]
    ins = [
        Blocks(source, target, in_sem.at[place], size)
        for place, (source, target) in enumerate(
            [
                (cotan_h, cotan), (normed_h, normed),
                (slope_h, slope), (hidden_h, hidden), (edge_h, edge),
            ]
        )
    ]
    turns = ins[0].turns
    for block in ins[:2]:
        block.start(0)
    first.append(begin(w2_h, w2, one_sem.at[1]))
    for block in ins[2:]:
        block.start(0)
    for turn in range(1, turns):
        for block in ins:
            block.start(turn)
    outs = Blocks(pre, pre_h, out_sem, size)
    acc[...] = jnp.zeros_like(acc)
    for copy in first:
        copy.wait()

    def body(turn):
        rows = pl.ds(pl.multiple_of(turn * size, size), size)
        place = turn * size + lax.broadcasted_iota(jnp.int32, (size, 1), 0)
        near = dot(pick(block_row(recv_ref, turn, size), 0, nodes), agg[...])
        for block in ins[:2]:
            block.wait(turn)
        grad_msg = jnp.where(place < scalar_ref[0], cotan[rows, :].astype(F32) + near, 0.0)
        grad_mixed = norm_back(grad_msg, normed[rows, :], to_column(inverse_ref[turn])).astype(BF)
        for block in ins[2:]:
            block.wait(turn)
        grad_pre = (dot_last(grad_mixed, w2[...]) * slope[rows, :].astype(F32)).astype(BF)
        pre[rows, :] = grad_pre
        outs.start(turn)
        acc[pl.ds(width, width), :] += dot_rows(hidden[rows, :], grad_mixed)
        acc[pl.ds(0, width), :] += dot_rows(edge[rows, :], grad_pre)

    each_block(turns, body)
    stash(acc, keep, away, scalar_ref[1])
    last = [begin(keep, keep_h, end_sem.at[0]), begin(away, away_h, end_sem.at[1])]
    outs.wait_all()
    for copy in last:
        copy.wait()


def scatter_kernel(
    size, scalar_ref, send_ref, recv_ref, pre_h, w1_h, part_h, latent_h, halo_h, order_h,
    node_h, far_h, keep_h, away_h,
    pre, w1, part, latent, halo, far_grad, keep, away, sent, received, acc, in_sem, one_sem, end_sem,
):
    del order_h
    nodes, width = latent.shape
    far_rows = halo.shape[0]
    ins = Blocks(pre_h, pre, in_sem, size)
    ins.start_all()
    later = [
        begin(source, target, one_sem.at[place])
        for place, (source, target) in enumerate(
            [(w1_h.at[pl.ds(0, 2 * width), :], w1), (part_h, part), (latent_h, latent), (halo_h, halo)]
        )
    ]
    sent[...] = jnp.zeros_like(sent)
    received[...] = jnp.zeros_like(received)

    def body(turn):
        ins.wait(turn)
        rows = pl.ds(pl.multiple_of(turn * size, size), size)
        sent[...] += dot(pick_t(block_row(send_ref, turn, size), 0, nodes + far_rows), pre[rows, :])
        received[...] += dot(pick_t(block_row(recv_ref, turn, size), 0, nodes), pre[rows, :])

    each_block(ins.turns, body)
    for copy in later:
        copy.wait()
    w_send = w1[pl.ds(0, width), :]
    near = sent[pl.ds(0, nodes), :].astype(BF)
    far = sent[pl.ds(nodes, far_rows), :].astype(BF)
    into = received[...].astype(BF)
    acc[pl.ds(0, width), :] = dot_rows(latent[...], near) + dot_rows(halo[...], far)
    acc[pl.ds(width, width), :] = dot_rows(latent[...], into)
    stash(acc, keep, away, scalar_ref[1])
    last = [begin(keep, keep_h, end_sem.at[0]), begin(away, away_h, end_sem.at[1])]
    far_grad[...] = dot_last(far, w_send).astype(BF)
    last.append(begin(far_grad, far_h, end_sem.at[2]))
    part[...] += dot_last(near, w_send) + dot_last(into, w1[pl.ds(width, width), :])
    last.append(begin(part, node_h, end_sem.at[3]))
    for copy in last:
        copy.wait()


def edge_kernel(size, cotan_h, pre_h, w1_h, ready0_h, ready1_h, out_h, cotan, pre, wedge, out, in_sem, out_sem, one_sem):
    del ready0_h, ready1_h
    width = wedge.shape[0]
    weight = begin(w1_h.at[pl.ds(2 * width, width), :], wedge, one_sem.at[0])
    ins = [Blocks(pre_h, pre, in_sem.at[0], size), Blocks(cotan_h, cotan, in_sem.at[1], size)]
    for turn in range(ins[0].turns):
        for block in ins:
            block.start(turn)
    outs = Blocks(out, out_h, out_sem, size)
    weight.wait()

    def body(turn):
        for block in ins:
            block.wait(turn)
        rows = pl.ds(pl.multiple_of(turn * size, size), size)
        out[rows, :] = (cotan[rows, :].astype(F32) + dot_last(pre[rows, :], wedge[...])).astype(BF)
        outs.start(turn)

    each_block(outs.turns, body)
    outs.wait_all()


def permute(value, pairs):
    return lax.ppermute(value, "dom", pairs)


class Share:
    def __init__(self, keep, away, count):
        self.count = count
        self.terms = [keep, permute(away, [(i, i ^ 1) for i in range(count)])]

    def prepare_side(self):
        side = (lax.axis_index("dom") >> 1) & 1
        paired = [t.reshape(t.shape[0] // 2, 2, *t.shape[1:]) for t in self.terms]
        mine = [lax.dynamic_index_in_dim(t, side, 1, keepdims=False) for t in paired]
        other = [lax.dynamic_index_in_dim(t, 1 - side, 1, keepdims=False) for t in paired]
        self.other = (other[0] + other[1].astype(F32)).astype(BF)
        self.terms = mine
        return self.other

    def send_side(self):
        self.terms.append(permute(self.other, [(i, i ^ 2) for i in range(self.count)]))

    def total(self):
        return sum(term.astype(F32) for term in self.terms[1:]) + self.terms[0].astype(F32)


def finish(total, count):
    groups = count // 4
    group = lax.axis_index("dom") >> 2
    result = lax.dynamic_index_in_dim(total, group, 0, keepdims=False)
    pieces = []
    for step in range(1, groups):
        piece = lax.dynamic_index_in_dim(total, (group + step) & (groups - 1), 0, keepdims=False)
        pieces.append(permute(piece.astype(BF), [(i, (i + 4 * step) % count) for i in range(count)]))
    for piece in pieces:
        result = result + piece.astype(F32)
    return result


def local(
    count,
    node_latent,
    edge_latent,
    node_cotan,
    edge_cotan,
    edge_w1,
    edge_w2,
    node_w1,
    node_w2,
    send_rows,
    senders,
    receivers,
    edge_count,
):
    nodes, width = node_latent.shape
    edges = edge_latent.shape[0]
    peers, slots = send_rows.shape[1:]
    halo = peers * slots
    size = edges // 2
    turns = edges // size
    place = lax.axis_index("dom")
    scalars = jnp.stack([edge_count[0], (place & 1).astype(jnp.int32)])
    params = pltpu.CompilerParams(vmem_limit_bytes=VMEM_BYTES)
    unit = 2 * edges * width * width

    def cost(units, bytes_accessed):
        return pl.CostEstimate(flops=int(units * unit), bytes_accessed=bytes_accessed, transcendentals=0)

    def shape(rows, dtype, columns=width):
        return jax.ShapeDtypeStruct((rows, columns), dtype)

    def stack(groups, rows, dtype):
        return jax.ShapeDtypeStruct((groups, rows, width), dtype)

    def buffer(*arrays):
        return [pltpu.VMEM(a.shape, a.dtype) for a in arrays]

    outgoing = pl.pallas_call(
        rows_kernel,
        in_specs=[VMEM, VMEM],
        out_specs=VMEM,
        out_shape=shape(halo, BF),
        compiler_params=params,
        cost_estimate=cost(0.1, 3 * halo * width * 2),
        name="halo_rows",
    )(send_rows, node_latent)
    incoming = lax.all_to_all(
        outgoing.reshape(peers, slots, width), "dom", split_axis=0, concat_axis=0, tiled=True
    ).reshape(halo, width)

    pre_shape = shape(edges, F32)
    pre = pl.pallas_call(
        functools.partial(early_kernel, size),
        in_specs=[VMEM, VMEM, ANY, ANY, ANY],
        out_specs=ANY,
        out_shape=pre_shape,
        scratch_shapes=buffer(edge_latent, node_latent, shape(2 * width, BF), pre_shape)
        + buffer(shape(2 * nodes + width, BF))
        + [DMA((turns,)), DMA((turns,)), DMA((3,))],
        compiler_params=params,
        cost_estimate=cost(3.5, edges * width * 6),
        name="edge_early",
    )(senders, receivers, edge_latent, node_latent, edge_w1)

    node_rows = 3 * width // count
    edge_rows = 4 * width // count
    half = count // 8
    square = shape(width, BF)
    state = [shape(edges, BF), shape(edges, BF), shape(edges, F32)]
    inverse_shape = jax.ShapeDtypeStruct((turns, 1, size), F32)
    ends = [
        shape(nodes, BF), shape(nodes, F32),
        stack(count // 2, node_rows, F32), stack(count // 2, node_rows, BF),
    ]
    hidden, slope, normed, inverse, agg_grad, grad_part, node_keep, node_away = pl.pallas_call(
        functools.partial(forward_kernel, size),
        in_specs=[SMEM, VMEM, VMEM] + [ANY] * 8,
        out_specs=[ANY] * 3 + [VMEM] + [ANY] * 4,
        out_shape=state + [inverse_shape] + ends,
        scratch_shapes=buffer(pre, incoming, square, edge_w2, node_latent, node_cotan, node_w1, node_w2)
        + buffer(*state, *ends)
        + buffer(shape(halo, BF), shape(nodes, F32), shape(3 * width, F32))
        + [DMA((turns,)), DMA((3, turns)), DMA((7,)), DMA((4,))],
        compiler_params=params,
        cost_estimate=cost(6, edges * width * 20),
        name="edge_forward",
    )(
        scalars, senders, receivers, pre, incoming, edge_w1, edge_w2,
        node_latent, node_cotan, node_w1, node_w2,
    )
    node_way = Share(node_keep, node_away, count)

    pre_low = shape(edges, BF)
    far_shape = shape(halo, BF)
    kept = [stack(2 * half, edge_rows, F32), stack(2 * half, edge_rows, BF)]
    two = shape(2 * width, F32)
    grad_pre, outer_keep, outer_away = pl.pallas_call(
        functools.partial(edge_back_kernel, size),
        in_specs=[SMEM, VMEM, VMEM] + [ANY] * 7,
        out_specs=[ANY] * 3,
        out_shape=[pre_low] + kept,
        scratch_shapes=buffer(
            edge_cotan, normed, slope, hidden, edge_latent, agg_grad, edge_w2, pre_low, *kept, two
        )
        + [DMA((5, turns)), DMA((turns,)), DMA((2,)), DMA((2,))],
        compiler_params=params,
        cost_estimate=cost(6, edges * width * 20),
        name="edge_backward",
    )(scalars, receivers, inverse, edge_cotan, normed, slope, hidden, edge_latent, agg_grad, edge_w2)
    order = node_way.prepare_side()
    node_way.send_side()
    outer_way = Share(outer_keep, outer_away, count)

    node_part, far_grad, inner_keep, inner_away = pl.pallas_call(
        functools.partial(scatter_kernel, size),
        in_specs=[SMEM, VMEM, VMEM] + [ANY] * 6,
        out_specs=[ANY] * 4,
        out_shape=[shape(nodes, F32), far_shape] + kept,
        scratch_shapes=buffer(pre_low, shape(2 * width, BF), grad_part, node_latent, incoming, far_shape, *kept)
        + buffer(shape(nodes + halo, F32), shape(nodes, F32), two)
        + [DMA((turns,)), DMA((4,)), DMA((4,))],
        compiler_params=params,
        cost_estimate=cost(5, edges * width * 4),
        name="edge_scatter",
    )(scalars, senders, receivers, grad_pre, edge_w1, grad_part, node_latent, incoming, order)
    inner_way = Share(inner_keep, inner_away, count)
    returned = lax.all_to_all(
        far_grad.reshape(peers, slots, width), "dom", split_axis=0, concat_axis=0, tiled=True
    ).reshape(halo, width)

    ready = [outer_way.prepare_side(), inner_way.prepare_side()]
    outer_way.send_side()
    inner_way.send_side()
    node_share = finish(node_way.total(), count)
    grad_edge = pl.pallas_call(
        functools.partial(edge_kernel, size),
        in_specs=[ANY] * 5,
        out_specs=ANY,
        out_shape=pre_low,
        scratch_shapes=buffer(edge_cotan, grad_pre, square, pre_low)
        + [DMA((2, turns)), DMA((turns,)), DMA((1,))],
        compiler_params=params,
        cost_estimate=cost(1.5, edges * width * 6),
        name="grad_edge",
    )(edge_cotan, grad_pre, edge_w1, *ready)
    edge_share = finish(jnp.concatenate([inner_way.total(), outer_way.total()], 0), count)
    grad_node = pl.pallas_call(
        return_kernel,
        in_specs=[VMEM, VMEM, VMEM],
        out_specs=VMEM,
        out_shape=shape(nodes, F32),
        compiler_params=params,
        cost_estimate=cost(0.1, nodes * width * 8),
        name="halo_return",
    )(send_rows, returned, node_part)
    return (grad_node, grad_edge, edge_share, node_share)


def solution(mesh):
    rows = P(("member", "dom"), None)
    placed = (
        rows, rows, rows, rows, P(), P(), P(), P(), P("dom", None, None), P("dom"), P("dom"), P("dom"),
    )
    return jax.shard_map(
        functools.partial(local, mesh.shape["dom"]),
        mesh=mesh,
        in_specs=placed,
        out_specs=(rows, rows, rows, rows),
        check_vma=False,
    )
```

time: 116 us -> 109 us (0.940)
  waiting for transfers between devices: 17.5 us -> 9.91 us
  local copies, waits for them, and re-layouts: 6.49 us -> 1.47 us
  Pallas kernels: 56.2 us -> 61.1 us
  other arithmetic: 5.32 us -> 8.09 us
  starting transfers between devices: 27.6 us -> 25.7 us
    pallas_call x5 -> x7, Pallas kernels: 56.2 us -> 61.1 us  [the longest x1 16.7 us: local(): pl.pallas_call(functools.partial(edge_back_kernel, size), in_specs=[SMEM,...]
    ppermute x10 -> x12, waiting for transfers between devices: 12.7 us -> 8.66 us  [permute(): return lax.ppermute(value, 'dom', pairs)]
    reshape x3 -> x0, local copies, waits for them, and re-layouts: 3.99 us -> none  [the longest x1 1.37 us: local(): flat_rows = send_rows.reshape(1, halo)]
    all_to_all x1, waiting for transfers between devices: 4.82 us -> 1.25 us  [local(): lax.all_to_all(far_grad.reshape(peers, slots, width), 'dom', split_axis=0...]
    convert_element_type x0 -> x4, other arithmetic: none -> 2.24 us  [the longest x3 2.09 us: prepare_side(): self.other = (other[0] + other[1].astype(F32)).astype(BF)]
    ppermute x10 -> x12, starting transfers between devices: 14.2 us -> 12.4 us  [permute(): return lax.ppermute(value, 'dom', pairs)]
    add x6 -> x5, other arithmetic: 4.67 us -> 5.29 us  [the longest x3 3.78 us: total(): sum((term.astype(F32) for term in self.terms[1:]))]
  transfers between devices with their start and end apart: 12 -> 14, of which waited for: 5 -> 3; matrix products, arithmetic and copies ran while one was open for 7% -> 6% of each run, Pallas kernels for 32% -> 41%
where the time goes in v3:
time: 109 us; the launch traced here: 108 us
  Pallas kernels  61.1 us (56%)
  starting transfers between devices  25.7 us (24%)
  waiting for transfers between devices  9.91 us (9%)
  other arithmetic  8.09 us (7%)
  between operations  1.51 us (1%)
  local copies, waits for them, and re-layouts  1.47 us (1%)
    pallas_call x1, Pallas kernels, local(): pl.pallas_call(functools.partial(edge_back_kernel, size), in_specs=[SMEM,...  16.7 us
    pallas_call x1, Pallas kernels, local(): pl.pallas_call(functools.partial(forward_kernel, size), in_specs=[SMEM, V...  14.7 us
    ppermute x12, starting transfers between devices, permute(): return lax.ppermute(value, 'dom', pairs)  12.4 us
    pallas_call x1, Pallas kernels, local(): pl.pallas_call(functools.partial(early_kernel, size), in_specs=[VMEM, VME...  10.6 us
    pallas_call x1, Pallas kernels, local(): pl.pallas_call(functools.partial(scatter_kernel, size), in_specs=[SMEM, V...  9.13 us
    ppermute x12, waiting for transfers between devices, permute(): return lax.ppermute(value, 'dom', pairs)  8.66 us
    all_to_all x1, starting transfers between devices, local(): lax.all_to_all(outgoing.reshape(peers, slots, width), 'dom', split_axis=0...  7.39 us
    all_to_all x1, starting transfers between devices, local(): lax.all_to_all(far_grad.reshape(peers, slots, width), 'dom', split_axis=0...  5.91 us
  transfers between devices with their start and end apart: 14, of which 3 were waited for; matrix products, arithmetic and copies ran while one was open for 6% of the time, Pallas kernels for 41%

profile of v3, /device:TPU:0, one launch (start us, length us, event | category | flops | bytes accessed | tf_op | source)
XLA Modules:
  0.0 107.7 jit_solution(6311534936813882670)
XLA Ops:
  0.6 2.1 %halo_rows.1 = bf16[256,512]{1,0:T(8,128)(2,1)} custom-call(s32[1,16,16]{2,1,0:T(8,128)} %rows_ref.3, bf16[512,512]{1,0:T(8,128)(2,1)} %latent_h.5), custom_call_target="tpu_custom_call" | custom-call | flops 134217728 | bytes 786432 | tf_op jit(solution)/shard_map/halo_rows/pallas_call | solution.py:451
  2.7 7.4 %all-to-all-start = ((bf16[16,16,512]{2,1,0:T(8,128)(2,1)}), bf16[16,16,512]{2,1,0:T(8,128)(2,1)S(1)}, u32[]{:S(2)}, u32[]{:S(2)}) async-start(bf16[16,16,512]{2,1,0:T(8,128)(2,1)} %bitcast.91), calls=%async_computation | async-start | bytes 524288 | tf_op jit(solution)/shard_map/all_to_all | solution.py:460
  10.8 0.6 pad_add_fusion.scalar_ref
  11.3 10.6 %edge_early.1.pre_h = f32[2560,512]{1,0:T(8,128)} custom-call(s32[2560]{0:T(1024)} %send_ref.5, s32[2560]{0:T(1024)} %recv_ref.7, bf16[2560,512]{1,0:T(8,128)(2,1)} %edge_h.3, bf16[512,512]{1,0:T(8,128)(2,1)} %latent_h.5, bf16[1536,512]{1,0:T(8,128)(2,1)} %w1_h.7), custom_call_target="tpu_custom_call" | custom-call | flops 4697620480 | bytes 7864320 | tf_op jit(solution)/shard_map/edge_early/pallas_call | solution.py:465
  21.9 0.0 all-to-all-done
  21.9 0.0 copy-start.7
  21.9 0.7 copy-done.7
  22.6 14.7 %edge_forward.1 = (bf16[2560,512]{1,0:T(8,128)(2,1)}, bf16[2560,512]{1,0:T(8,128)(2,1)}, f32[2560,512]{1,0:T(8,128)}, f32[2,1,1280]{2,1,0:T(1,128)}, bf16[512,51...) custom-call(s32[2]{0:T(128)} %pad_add_fusion.scalar_ref, ...), custom_call_target="tpu_custom_call" | custom-call | flops 8053063680 | bytes 26214400 | tf_op jit(solution)/shard_map/edge_forward/pallas_call | solution.py:488
  37.4 0.5 collective-permute-start
  37.8 16.7 %edge_backward.1 = (bf16[2560,512]{1,0:T(8,128)(2,1)}, f32[4,128,512]{2,1,0:T(8,128)}, bf16[4,128,512]{2,1,0:T(8,128)(2,1)}) custom-call(s32[2]{0:T(128)} %pad_add_fusion.scalar_ref, s32[2560]{0:T(1024)} %recv_ref.7, f32[2,1,1280]{2,1,0:T(1,128)} %get-tuple-element.19.inverse_ref, bf16[2560,512]{1,0:T(8,128)(2,1)} %cotan_h.5, ...), custom_call_target="tpu_custom_call" | custom-call | flops 8053063680 | bytes 26214400 | tf_op jit(solution)/shard_map/edge_backward/pallas_call | solution.py:510
  54.6 0.2 collective-permute-start.1
  54.7 0.0 collective-permute-done
  54.7 1.0 fusion.6.order_h
  55.7 1.9 %collective-permute-start.8 = (bf16[4,96,512]{2,1,0:T(8,128)(2,1)}, bf16[4,96,512]{2,1,0:T(8,128)(2,1)}, u32[]{:S(2)}, u32[]{:S(2)}) collective-permute-start(bf16[4,96,512]{2,1,0:T(8,128)(2,1)} %fusion.6.order_h), channel_id=1, source_target_pairs={{0,2},{1,3},{2,0},{3,1},{4,6},{5,7},{6,4},{7,5},{8,10},{9,11},{10,... | collective-permute-start | bytes 1179656 | tf_op jit(solution)/shard_map/ppermute | solution.py:376
  57.7 9.1 %edge_scatter.1 = (f32[512,512]{1,0:T(8,128)}, bf16[256,512]{1,0:T(8,128)(2,1)}, f32[4,128,512]{2,1,0:T(8,128)}, bf16[4,128,512]{2,1,0:T(8,128)(2,1)}) custom-call(s32[2]{0:T(128)} %pad_add_fusion.scalar_ref, s32[2560]{0:T(1024)} %send_ref.5, s32[2560]{0:T(1024)} %recv_ref.7, bf16[2560,512]{1,0:T(8,128)(2,1)} %get-tuple-element.24.pre_h, ...), custom_call_target="tpu_custom_call" | custom-call | flops 6710886400 | bytes 5242880 | tf_op jit(solution)/shard_map/edge_scatter/pallas_call | solution.py:527
  66.8 0.1 collective-permute-start.2
  66.9 0.0 collective-permute-done.1
  66.9 1.0 fusion.7.ready0_h
  68.0 0.3 collective-permute-start.4
  68.2 5.9 %all-to-all-start.1 = ((bf16[16,16,512]{2,1,0:T(8,128)(2,1)}), bf16[16,16,512]{2,1,0:T(8,128)(2,1)S(1)}, u32[]{:S(2)}, u32[]{:S(2)}) async-start(bf16[16,16,512]{2,1,0:T(8,128)(2,1)} %bitcast.100), calls=%async_computation.1 | async-start | bytes 524288 | tf_op jit(solution)/shard_map/all_to_all | solution.py:540
  74.2 0.0 collective-permute-done.8
  74.2 1.4 %fusion.1 = f32[4,96,512]{2,1,0:T(8,128)S(1)} fusion(f32[4,2,96,512]{3,2,1,0:T(8,128)S(1)} %bitcast.89, s32[]{:T(128)S(6)} %select_n.39, bf16[4,96,512]{2,1,0:T(8,128)(2,1)} %collective-permute-done.8, bf16[4,2,96,512]{3,2,1,0:T(8,128)(2,1)} %bitcast.97), kind=kLoop, calls=%fused_computation.11 | loop fusion | flops 786432 | bytes 2359300 | tf_op jit(solution)/shard_map/add | solution.py:397
  75.6 3.8 %collective-permute-start.11 = (bf16[96,512]{1,0:T(8,128)(2,1)S(1)}, bf16[96,512]{1,0:T(8,128)(2,1)S(1)}, u32[]{:S(2)}, u32[]{:S(2)}) collective-permute-start(bf16[96,512]{1,0:T(8,128)(2,1)S(1)} %get-tuple-element.38), channel_id=1, source_target_pairs={{0,12},{1,13},{2,14},{3,15},{4,0},{5,1},{6,2},{7,3},{8,4},{9,5},{1... | collective-permute-start | bytes 294920 | tf_op jit(solution)/shard_map/ppermute | solution.py:376
  79.4 0.0 collective-permute-start.10
  79.4 1.1 %collective-permute-start.9 = (bf16[96,512]{1,0:T(8,128)(2,1)S(1)}, bf16[96,512]{1,0:T(8,128)(2,1)S(1)}, u32[]{:S(2)}, u32[]{:S(2)}) collective-permute-start(bf16[96,512]{1,0:T(8,128)(2,1)S(1)} %get-tuple-element.37), channel_id=1, source_target_pairs={{0,4},{1,5},{2,6},{3,7},{4,8},{5,9},{6,10},{7,11},{8,12},{9,13},{1... | collective-permute-start | bytes 294920 | tf_op jit(solution)/shard_map/ppermute | solution.py:376
  80.5 0.0 collective-permute-done.2
  80.5 0.1 fusion.8.ready1_h
  80.6 1.5 %collective-permute-start.3 = (bf16[2,128,512]{2,1,0:T(8,128)(2,1)S(1)}, bf16[2,128,512]{2,1,0:T(8,128)(2,1)S(1)}, u32[]{:S(2)}, u32[]{:S(2)}) collective-permute-start(bf16[2,128,512]{2,1,0:T(8,128)(2,1)S(1)} %fusion.8.ready1_h), channel_id=1, source_target_pairs={{0,2},{1,3},{2,0},{3,1},{4,6},{5,7},{6,4},{7,5},{8,10},{9,11},{10,... | collective-permute-start | bytes 786440 | tf_op jit(solution)/shard_map/ppermute | solution.py:376
  82.1 0.0 collective-permute-done.4
  82.1 1.3 %fusion.4 = f32[2,128,512]{2,1,0:T(8,128)S(1)} fusion(f32[2,2,128,512]{3,2,1,0:T(8,128)} %bitcast.94, s32[]{:T(128)S(6)} %select_n.39, bf16[2,128,512]{2,1,0:T(8,128)(2,1)} %collective-permute-done.4, bf16[2,2,128,512]{3,2,1,0:T(8,128)(2,1)} %bitcast.9), kind=kLoop, calls=%fused_computation.17 | loop fusion | flops 524288 | bytes 1572868 | tf_op jit(solution)/shard_map/add | solution.py:397
  83.4 1.2 %all-to-all-done.1 = bf16[16,16,512]{2,1,0:T(8,128)(2,1)S(1)} async-done(((bf16[16,16,512]{2,1,0:T(8,128)(2,1)}), bf16[16,16,512]{2,1,0:T(8,128)(2,1)S(1)}, u32[]{:S(2)}, u32[]{:S(2)}) %all-to-all-start.1) | async-done | bytes 262176 | tf_op jit(solution)/shard_map/all_to_all | solution.py:540
  84.7 0.7 copy-done.1
  85.4 2.7 %halo_return.1 = f32[512,512]{1,0:T(8,128)} custom-call(s32[1,16,16]{2,1,0:T(8,128)} %rows_ref.3, bf16[256,512]{1,0:T(8,128)(2,1)} %bitcast.90, f32[512,512]{1,0:T(8,128)} %get-tuple-element.29.part_ref), custom_call_target="tpu_custom_call" | custom-call | flops 134217728 | bytes 2097152 | tf_op jit(solution)/shard_map/halo_return/pallas_call | solution.py:560
  88.1 0.0 collective-permute-done.11
  88.1 4.1 %collective-permute-done.10 = bf16[96,512]{1,0:T(8,128)(2,1)S(1)} collective-permute-done((bf16[96,512]{1,0:T(8,128)(2,1)S(1)}, bf16[96,512]{1,0:T(8,128)(2,1)S(1)}, u32[]{:S(2)}, u32[]{:S(2)}) %collective-permute-start.10) | collective-permute-done | bytes 98336 | tf_op jit(solution)/shard_map/ppermute | solution.py:376
  92.2 0.0 collective-permute-done.9
  92.2 0.7 fusion.21
  92.9 0.0 collective-permute-done.3
  92.9 1.1 %fusion.5 = f32[2,128,512]{2,1,0:T(8,128)S(1)} fusion(f32[2,2,128,512]{3,2,1,0:T(8,128)} %bitcast.92, s32[]{:T(128)S(6)} %select_n.39, bf16[2,128,512]{2,1,0:T(8,128)(2,1)S(1)} %collective-permute-done.3, bf16[2,2,128,512]{3,2,1,0:T(8,128)(2,1)S(1)} %bitcast.99), kind=kLoop, calls=%fused_computation.19 | loop fusion | flops 524288 | bytes 1572868 | tf_op jit(solution)/shard_map/add | solution.py:397
  94.1 0.1 fusion.23
  94.3 0.2 collective-permute-start.7
  94.5 0.9 collective-permute-start.6
  95.3 1.9 %collective-permute-start.5 = (bf16[128,512]{1,0:T(8,128)(2,1)S(1)}, bf16[128,512]{1,0:T(8,128)(2,1)S(1)}, u32[]{:S(2)}, u32[]{:S(2)}) collective-permute-start(bf16[128,512]{1,0:T(8,128)(2,1)S(1)} %get-tuple-element.34), channel_id=1, source_target_pairs={{0,4},{1,5},{2,6},{3,7},{4,8},{5,9},{6,10},{7,11},{8,12},{9,13},{1... | collective-permute-start | bytes 393224 | tf_op jit(solution)/shard_map/ppermute | solution.py:376
  97.3 5.1 %grad_edge.1 = bf16[2560,512]{1,0:T(8,128)(2,1)} custom-call(bf16[2560,512]{1,0:T(8,128)(2,1)} %cotan_h.5, bf16[2560,512]{1,0:T(8,128)(2,1)} %get-tuple-element.24.pre_h, bf16[1536,512]{1,0:T(8,128)(2,1)} %w1_h.7, bf16[2,128,512]{2,1,0:T(8,128)(2,1)} %copy-done.2, bf16[2,128,512]{2,1,0:T(8,128)(2,1)} %copy-done.3), custom_call_target="tpu_custom_call" | custom-call | flops 2013265920 | bytes 7864320 | tf_op jit(solution)/shard_map/grad_edge/pallas_call | solution.py:548
  102.4 0.0 collective-permute-done.7
  102.4 4.5 %collective-permute-done.6 = bf16[128,512]{1,0:T(8,128)(2,1)S(1)} collective-permute-done((bf16[128,512]{1,0:T(8,128)(2,1)S(1)}, bf16[128,512]{1,0:T(8,128)(2,1)S(1)}, u32[]{:S(2)}, u32[]{:S(2)}) %collective-permute-start.6) | collective-permute-done | bytes 131104 | tf_op jit(solution)/shard_map/ppermute | solution.py:376
  106.9 0.0 collective-permute-done.5
  106.9 0.8 fusion.15
  (14 shorter events, 0.1 us)
Async XLA Ops:
  2.7 19.2 %all-to-all-start = ((bf16[16,16,512]{2,1,0:T(8,128)(2,1)}), bf16[16,16,512]{2,1,0:T(8,128)(2,1)S(1)}, u32[]{:S(2)}, u32[]{:S(2)}) async-start(bf16[16,16,512]{2,1,0:T(8,128)(2,1)} %bitcast.91), calls=%async_computation | async-start | bytes 524288 | tf_op jit(solution)/shard_map/all_to_all | solution.py:460
  21.9 0.7 copy-start.7
  37.4 17.4 %collective-permute-start = (bf16[8,96,512]{2,1,0:T(8,128)(2,1)}, bf16[8,96,512]{2,1,0:T(8,128)(2,1)S(1)}, u32[]{:S(2)}, u32[]{:S(2)}) collective-permute-start(bf16[8,96,512]{2,1,0:T(8,128)(2,1)} %get-tuple-element.27), channel_id=1, source_target_pairs={{0,1},{1,0},{2,3},{3,2},{4,5},{5,4},{6,7},{7,6},{8,9},{9,8},{10,11... | collective-permute-start | bytes 2359304 | tf_op jit(solution)/shard_map/ppermute | solution.py:376
  37.8 16.9 %copy-start = (f32[8,96,512]{2,1,0:T(8,128)S(1)}, f32[8,96,512]{2,1,0:T(8,128)}, u32[]{:S(2)}) copy-start(f32[8,96,512]{2,1,0:T(8,128)} %get-tuple-element.26) | copy-start | bytes 4718596
  54.6 12.3 %collective-permute-start.1 = (bf16[4,128,512]{2,1,0:T(8,128)(2,1)}, bf16[4,128,512]{2,1,0:T(8,128)(2,1)}, u32[]{:S(2)}, u32[]{:S(2)}) collective-permute-start(bf16[4,128,512]{2,1,0:T(8,128)(2,1)} %get-tuple-element.31), channel_id=1, source_target_pairs={{0,1},{1,0},{2,3},{3,2},{4,5},{5,4},{6,7},{7,6},{8,9},{9,8},{10,11... | collective-permute-start | bytes 1572872 | tf_op jit(solution)/shard_map/ppermute | solution.py:376
  54.7 2.9 %copy-start.6 = (bf16[8,96,512]{2,1,0:T(8,128)(2,1)}, bf16[8,96,512]{2,1,0:T(8,128)(2,1)S(1)}, u32[]{:S(2)}) copy-start(bf16[8,96,512]{2,1,0:T(8,128)(2,1)S(1)} %collective-permute-done) | copy-start | bytes 2359300
  55.7 18.4 %collective-permute-start.8 = (bf16[4,96,512]{2,1,0:T(8,128)(2,1)}, bf16[4,96,512]{2,1,0:T(8,128)(2,1)}, u32[]{:S(2)}, u32[]{:S(2)}) collective-permute-start(bf16[4,96,512]{2,1,0:T(8,128)(2,1)} %fusion.6.order_h), channel_id=1, source_target_pairs={{0,2},{1,3},{2,0},{3,1},{4,6},{5,7},{6,4},{7,5},{8,10},{9,11},{10,... | collective-permute-start | bytes 1179656 | tf_op jit(solution)/shard_map/ppermute | solution.py:376
  57.7 9.2 %copy-start.5 = (f32[4,128,512]{2,1,0:T(8,128)S(1)}, f32[4,128,512]{2,1,0:T(8,128)}, u32[]{:S(2)}) copy-start(f32[4,128,512]{2,1,0:T(8,128)} %get-tuple-element.30) | copy-start | bytes 3145732
  66.8 13.7 %collective-permute-start.2 = (bf16[4,128,512]{2,1,0:T(8,128)(2,1)}, bf16[4,128,512]{2,1,0:T(8,128)(2,1)S(1)}, u32[]{:S(2)}, u32[]{:S(2)}) collective-permute-start(bf16[4,128,512]{2,1,0:T(8,128)(2,1)} %get-tuple-element.33), channel_id=1, source_target_pairs={{0,1},{1,0},{2,3},{3,2},{4,5},{5,4},{6,7},{7,6},{8,9},{9,8},{10,11... | collective-permute-start | bytes 1572872 | tf_op jit(solution)/shard_map/ppermute | solution.py:376
  68.0 15.5 %copy-start.2 = (bf16[2,128,512]{2,1,0:T(8,128)(2,1)}, bf16[2,128,512]{2,1,0:T(8,128)(2,1)S(1)}, u32[]{:S(2)}) copy-start(bf16[2,128,512]{2,1,0:T(8,128)(2,1)S(1)} %fusion.7.ready0_h) | copy-start | bytes 786436
  68.0 14.2 %collective-permute-start.4 = (bf16[2,128,512]{2,1,0:T(8,128)(2,1)S(1)}, bf16[2,128,512]{2,1,0:T(8,128)(2,1)}, u32[]{:S(2)}, u32[]{:S(2)}) collective-permute-start(bf16[2,128,512]{2,1,0:T(8,128)(2,1)S(1)} %fusion.7.ready0_h), channel_id=1, source_target_pairs={{0,2},{1,3},{2,0},{3,1},{4,6},{5,7},{6,4},{7,5},{8,10},{9,11},{10,... | collective-permute-start | bytes 786440 | tf_op jit(solution)/shard_map/ppermute | solution.py:376
  68.2 16.4 %all-to-all-start.1 = ((bf16[16,16,512]{2,1,0:T(8,128)(2,1)}), bf16[16,16,512]{2,1,0:T(8,128)(2,1)S(1)}, u32[]{:S(2)}, u32[]{:S(2)}) async-start(bf16[16,16,512]{2,1,0:T(8,128)(2,1)} %bitcast.100), calls=%async_computation.1 | async-start | bytes 524288 | tf_op jit(solution)/shard_map/all_to_all | solution.py:540
  74.1 6.4 %copy-start.4 = (f32[4,128,512]{2,1,0:T(8,128)S(1)}, f32[4,128,512]{2,1,0:T(8,128)}, u32[]{:S(2)}) copy-start(f32[4,128,512]{2,1,0:T(8,128)} %get-tuple-element.32) | copy-start | bytes 3145732
  75.6 12.5 %collective-permute-start.11 = (bf16[96,512]{1,0:T(8,128)(2,1)S(1)}, bf16[96,512]{1,0:T(8,128)(2,1)S(1)}, u32[]{:S(2)}, u32[]{:S(2)}) collective-permute-start(bf16[96,512]{1,0:T(8,128)(2,1)S(1)} %get-tuple-element.38), channel_id=1, source_target_pairs={{0,12},{1,13},{2,14},{3,15},{4,0},{5,1},{6,2},{7,3},{8,4},{9,5},{1... | collective-permute-start | bytes 294920 | tf_op jit(solution)/shard_map/ppermute | solution.py:376
  79.4 12.8 %collective-permute-start.10 = (bf16[96,512]{1,0:T(8,128)(2,1)S(1)}, bf16[96,512]{1,0:T(8,128)(2,1)S(1)}, u32[]{:S(2)}, u32[]{:S(2)}) collective-permute-start(bf16[96,512]{1,0:T(8,128)(2,1)S(1)} %get-tuple-element.39), channel_id=1, source_target_pairs={{0,8},{1,9},{2,10},{3,11},{4,12},{5,13},{6,14},{7,15},{8,0},{9,1},... | collective-permute-start | bytes 294920 | tf_op jit(solution)/shard_map/ppermute | solution.py:376
  79.4 12.8 %collective-permute-start.9 = (bf16[96,512]{1,0:T(8,128)(2,1)S(1)}, bf16[96,512]{1,0:T(8,128)(2,1)S(1)}, u32[]{:S(2)}, u32[]{:S(2)}) collective-permute-start(bf16[96,512]{1,0:T(8,128)(2,1)S(1)} %get-tuple-element.37), channel_id=1, source_target_pairs={{0,4},{1,5},{2,6},{3,7},{4,8},{5,9},{6,10},{7,11},{8,12},{9,13},{1... | collective-permute-start | bytes 294920 | tf_op jit(solution)/shard_map/ppermute | solution.py:376
  80.6 13.5 %copy-start.3 = (bf16[2,128,512]{2,1,0:T(8,128)(2,1)}, bf16[2,128,512]{2,1,0:T(8,128)(2,1)S(1)}, u32[]{:S(2)}) copy-start(bf16[2,128,512]{2,1,0:T(8,128)(2,1)S(1)} %fusion.8.ready1_h) | copy-start | bytes 786436
  80.6 12.4 %collective-permute-start.3 = (bf16[2,128,512]{2,1,0:T(8,128)(2,1)S(1)}, bf16[2,128,512]{2,1,0:T(8,128)(2,1)S(1)}, u32[]{:S(2)}, u32[]{:S(2)}) collective-permute-start(bf16[2,128,512]{2,1,0:T(8,128)(2,1)S(1)} %fusion.8.ready1_h), channel_id=1, source_target_pairs={{0,2},{1,3},{2,0},{3,1},{4,6},{5,7},{6,4},{7,5},{8,10},{9,11},{10,... | collective-permute-start | bytes 786440 | tf_op jit(solution)/shard_map/ppermute | solution.py:376
  84.7 0.7 copy-start.1
  94.3 8.1 %collective-permute-start.7 = (bf16[128,512]{1,0:T(8,128)(2,1)S(1)}, bf16[128,512]{1,0:T(8,128)(2,1)S(1)}, u32[]{:S(2)}, u32[]{:S(2)}) collective-permute-start(bf16[128,512]{1,0:T(8,128)(2,1)S(1)} %get-tuple-element.36), channel_id=1, source_target_pairs={{0,12},{1,13},{2,14},{3,15},{4,0},{5,1},{6,2},{7,3},{8,4},{9,5},{1... | collective-permute-start | bytes 393224 | tf_op jit(solution)/shard_map/ppermute | solution.py:376
  94.5 12.4 %collective-permute-start.6 = (bf16[128,512]{1,0:T(8,128)(2,1)S(1)}, bf16[128,512]{1,0:T(8,128)(2,1)S(1)}, u32[]{:S(2)}, u32[]{:S(2)}) collective-permute-start(bf16[128,512]{1,0:T(8,128)(2,1)S(1)} %get-tuple-element.35), channel_id=1, source_target_pairs={{0,8},{1,9},{2,10},{3,11},{4,12},{5,13},{6,14},{7,15},{8,0},{9,1},... | collective-permute-start | bytes 393224 | tf_op jit(solution)/shard_map/ppermute | solution.py:376
  95.3 11.6 %collective-permute-start.5 = (bf16[128,512]{1,0:T(8,128)(2,1)S(1)}, bf16[128,512]{1,0:T(8,128)(2,1)S(1)}, u32[]{:S(2)}, u32[]{:S(2)}) collective-permute-start(bf16[128,512]{1,0:T(8,128)(2,1)S(1)} %get-tuple-element.34), channel_id=1, source_target_pairs={{0,4},{1,5},{2,6},{3,7},{4,8},{5,9},{6,10},{7,11},{8,12},{9,13},{1... | collective-permute-start | bytes 393224 | tf_op jit(solution)/shard_map/ppermute | solution.py:376

commit v4 on v3

--- a/solution.py
+++ b/solution.py
@@ -94,9 +94,10 @@
     def start(self, turn):
         self.copy(turn).start()
 
-    def start_all(self):
-        for turn in range(self.turns):
-            self.start(turn)
+    def start_next(self, turn):
+        @pl.when(turn + 1 < self.turns)
+        def _():
+            self.start(turn + 1)
 
     def wait(self, turn):
         self.copy(turn).wait()
@@ -128,10 +129,6 @@
 
 def rows_kernel(rows_ref, latent_ref, out_ref):
     out_ref[...] = dot(pick_slots(rows_ref, latent_ref.shape[0]), latent_ref[...]).astype(BF)
-
-
-def return_kernel(rows_ref, back_ref, part_ref, out_ref):
-    out_ref[...] = part_ref[...] + dot_rows(pick_slots(rows_ref, out_ref.shape[0]), back_ref[...])
 
 
 def early_kernel(
@@ -146,7 +143,7 @@
     ]
     edges = Blocks(edge_h, edge, edge_sem, size)
     outs = Blocks(pre, pre_h, out_sem, size)
-    edges.start_all()
+    edges.start(0)
     for copy in first:
         copy.wait()
     for part in range(2):
@@ -157,6 +154,7 @@
         sender = pick(block_row(send_ref, turn, size), 0, nodes)
         receiver = pick(block_row(recv_ref, turn, size), 0, nodes)
         edges.wait(turn)
+        edges.start_next(turn)
         pre[rows, :] = dot(jnp.concatenate([sender, receiver, edge[rows, :]], 1), table[...])
         outs.start(turn)
 
@@ -186,7 +184,8 @@
         begin(w1_h.at[pl.ds(0, width), :], wsend, one_sem.at[1]),
     ]
     pres = Blocks(pre_h, pre, pre_sem, size)
-    pres.start_all()
+    for turn in range(pres.turns):
+        pres.start(turn)
     second = begin(w2_h, w2, one_sem.at[2])
     later = [
         begin(source, target, one_sem.at[3 + place])
@@ -272,11 +271,6 @@
     for block in ins[:2]:
         block.start(0)
     first.append(begin(w2_h, w2, one_sem.at[1]))
-    for block in ins[2:]:
-        block.start(0)
-    for turn in range(1, turns):
-        for block in ins:
-            block.start(turn)
     outs = Blocks(pre, pre_h, out_sem, size)
     acc[...] = jnp.zeros_like(acc)
     for copy in first:
@@ -288,10 +282,14 @@
         near = dot(pick(block_row(recv_ref, turn, size), 0, nodes), agg[...])
         for block in ins[:2]:
             block.wait(turn)
+        for block in ins[2:]:
+            block.start(turn)
         grad_msg = jnp.where(place < scalar_ref[0], cotan[rows, :].astype(F32) + near, 0.0)
         grad_mixed = norm_back(grad_msg, normed[rows, :], to_column(inverse_ref[turn])).astype(BF)
         for block in ins[2:]:
             block.wait(turn)
+        for block in ins[:2]:
+            block.start_next(turn)
         grad_pre = (dot_last(grad_mixed, w2[...]) * slope[rows, :].astype(F32)).astype(BF)
         pre[rows, :] = grad_pre
         outs.start(turn)
@@ -315,9 +313,9 @@
     nodes, width = latent.shape
     far_rows = halo.shape[0]
     ins = Blocks(pre_h, pre, in_sem, size)
-    ins.start_all()
+    ins.start(0)
     later = [
-        begin(source, target, one_sem.at[place])
+        pltpu.make_async_copy(source, target, one_sem.at[place])
         for place, (source, target) in enumerate(
             [(w1_h.at[pl.ds(0, 2 * width), :], w1), (part_h, part), (latent_h, latent), (halo_h, halo)]
         )
@@ -327,6 +325,13 @@
 
     def body(turn):
         ins.wait(turn)
+        ins.start_next(turn)
+
+        @pl.when(turn == ins.turns - 1)
+        def _():
+            for copy in later:
+                copy.start()
+
         rows = pl.ds(pl.multiple_of(turn * size, size), size)
         sent[...] += dot(pick_t(block_row(send_ref, turn, size), 0, nodes + far_rows), pre[rows, :])
         received[...] += dot(pick_t(block_row(recv_ref, turn, size), 0, nodes), pre[rows, :])
@@ -350,26 +355,35 @@
         copy.wait()
 
 
-def edge_kernel(size, cotan_h, pre_h, w1_h, ready0_h, ready1_h, out_h, cotan, pre, wedge, out, in_sem, out_sem, one_sem):
-    del ready0_h, ready1_h
+def last_kernel(
+    size, rows_ref, cotan_h, pre_h, w1_h, back_h, part_h, edge_h, node_h,
+    cotan, pre, wedge, back, part, out, in_sem, out_sem, one_sem,
+):
     width = wedge.shape[0]
     weight = begin(w1_h.at[pl.ds(2 * width, width), :], wedge, one_sem.at[0])
     ins = [Blocks(pre_h, pre, in_sem.at[0], size), Blocks(cotan_h, cotan, in_sem.at[1], size)]
-    for turn in range(ins[0].turns):
-        for block in ins:
-            block.start(turn)
-    outs = Blocks(out, out_h, out_sem, size)
+    for block in ins:
+        block.start(0)
+    node = [begin(back_h, back, one_sem.at[1]), begin(part_h, part, one_sem.at[2])]
+    outs = Blocks(out, edge_h, out_sem, size)
+    slots = pick_slots(rows_ref, part.shape[0])
     weight.wait()
 
     def body(turn):
         for block in ins:
             block.wait(turn)
+            block.start_next(turn)
         rows = pl.ds(pl.multiple_of(turn * size, size), size)
         out[rows, :] = (cotan[rows, :].astype(F32) + dot_last(pre[rows, :], wedge[...])).astype(BF)
         outs.start(turn)
 
     each_block(outs.turns, body)
+    for copy in node:
+        copy.wait()
+    part[...] += dot_rows(slots, back[...])
+    end = begin(part, node_h, one_sem.at[3])
     outs.wait_all()
+    end.wait()
 
 
 def permute(value, pairs):
@@ -381,33 +395,34 @@
         self.count = count
         self.terms = [keep, permute(away, [(i, i ^ 1) for i in range(count)])]
 
-    def prepare_side(self):
+    def side_hop(self):
         side = (lax.axis_index("dom") >> 1) & 1
         paired = [t.reshape(t.shape[0] // 2, 2, *t.shape[1:]) for t in self.terms]
         mine = [lax.dynamic_index_in_dim(t, side, 1, keepdims=False) for t in paired]
         other = [lax.dynamic_index_in_dim(t, 1 - side, 1, keepdims=False) for t in paired]
-        self.other = (other[0] + other[1].astype(F32)).astype(BF)
-        self.terms = mine
-        return self.other
-
-    def send_side(self):
-        self.terms.append(permute(self.other, [(i, i ^ 2) for i in range(self.count)]))
+        other = (other[0] + other[1].astype(F32)).astype(BF)
+        self.terms = mine + [permute(other, [(i, i ^ 2) for i in range(self.count)])]
+        return other
 
     def total(self):
-        return sum(term.astype(F32) for term in self.terms[1:]) + self.terms[0].astype(F32)
-
-
-def finish(total, count):
+        return self.terms[0] + self.terms[1].astype(F32) + self.terms[2].astype(F32)
+
+
+def start_groups(total, count):
     groups = count // 4
     group = lax.axis_index("dom") >> 2
-    result = lax.dynamic_index_in_dim(total, group, 0, keepdims=False)
+    own = lax.dynamic_index_in_dim(total, group, 0, keepdims=False)
     pieces = []
     for step in range(1, groups):
         piece = lax.dynamic_index_in_dim(total, (group + step) & (groups - 1), 0, keepdims=False)
         pieces.append(permute(piece.astype(BF), [(i, (i + 4 * step) % count) for i in range(count)]))
+    return own, pieces
+
+
+def end_groups(own, pieces):
     for piece in pieces:
-        result = result + piece.astype(F32)
-    return result
+        own = own + piece.astype(F32)
+    return own
 
 
 def local(
@@ -432,12 +447,12 @@
     size = edges // 2
     turns = edges // size
     place = lax.axis_index("dom")
-    scalars = jnp.stack([edge_count[0], (place & 1).astype(jnp.int32)])
+    scalars = jnp.stack([edge_count[0], place & 1, (place >> 1) & 1, place >> 2]).astype(jnp.int32)
     params = pltpu.CompilerParams(vmem_limit_bytes=VMEM_BYTES)
     unit = 2 * edges * width * width
 
     def cost(units, bytes_accessed):
-        return pl.CostEstimate(flops=int(units * unit), bytes_accessed=bytes_accessed, transcendentals=0)
+        return pl.CostEstimate(flops=int(units * unit), bytes_accessed=int(bytes_accessed), transcendentals=0)
 
     def shape(rows, dtype, columns=width):
         return jax.ShapeDtypeStruct((rows, columns), dtype)
@@ -520,8 +535,7 @@
         cost_estimate=cost(6, edges * width * 20),
         name="edge_backward",
     )(scalars, receivers, inverse, edge_cotan, normed, slope, hidden, edge_latent, agg_grad, edge_w2)
-    order = node_way.prepare_side()
-    node_way.send_side()
+    order = node_way.side_hop()
     outer_way = Share(outer_keep, outer_away, count)
 
     node_part, far_grad, inner_keep, inner_away = pl.pallas_call(
@@ -537,35 +551,29 @@
         name="edge_scatter",
     )(scalars, senders, receivers, grad_pre, edge_w1, grad_part, node_latent, incoming, order)
     inner_way = Share(inner_keep, inner_away, count)
+    outer_way.side_hop()
+    ready = inner_way.side_hop()
+    far_grad, _ = lax.optimization_barrier((far_grad, ready))
+    node_own, node_pieces = start_groups(node_way.total(), count)
     returned = lax.all_to_all(
         far_grad.reshape(peers, slots, width), "dom", split_axis=0, concat_axis=0, tiled=True
     ).reshape(halo, width)
-
-    ready = [outer_way.prepare_side(), inner_way.prepare_side()]
-    outer_way.send_side()
-    inner_way.send_side()
-    node_share = finish(node_way.total(), count)
-    grad_edge = pl.pallas_call(
-        functools.partial(edge_kernel, size),
-        in_specs=[ANY] * 5,
-        out_specs=ANY,
-        out_shape=pre_low,
-        scratch_shapes=buffer(edge_cotan, grad_pre, square, pre_low)
-        + [DMA((2, turns)), DMA((turns,)), DMA((1,))],
+    edge_own, edge_pieces = start_groups(jnp.concatenate([inner_way.total(), outer_way.total()], 0), count)
+
+    grad_edge, grad_node = pl.pallas_call(
+        functools.partial(last_kernel, size),
+        in_specs=[VMEM] + [ANY] * 5,
+        out_specs=[ANY] * 2,
+        out_shape=[pre_low, shape(nodes, F32)],
+        scratch_shapes=buffer(edge_cotan, grad_pre, square, far_shape, shape(nodes, F32), pre_low)
+        + [DMA((2, turns)), DMA((turns,)), DMA((4,))],
         compiler_params=params,
         cost_estimate=cost(1.5, edges * width * 6),
-        name="grad_edge",
-    )(edge_cotan, grad_pre, edge_w1, *ready)
-    edge_share = finish(jnp.concatenate([inner_way.total(), outer_way.total()], 0), count)
-    grad_node = pl.pallas_call(
-        return_kernel,
-        in_specs=[VMEM, VMEM, VMEM],
-        out_specs=VMEM,
-        out_shape=shape(nodes, F32),
-        compiler_params=params,
-        cost_estimate=cost(0.1, nodes * width * 8),
-        name="halo_return",
-    )(send_rows, returned, node_part)
+        name="last_grads",
+    )(send_rows, edge_cotan, grad_pre, edge_w1, returned, node_part)
+    node_share = end_groups(node_own, node_pieces)
+    edge_own, grad_node = lax.optimization_barrier((edge_own, grad_node))
+    edge_share = end_groups(edge_own, edge_pieces)
     return (grad_node, grad_edge, edge_share, node_share)
 
 

time: 109 us -> 105 us (0.963)
  the two profiles are of different devices: /device:TPU:0 before, /device:TPU:9 now
where the time goes in v4:
time: 105 us; the launch traced here: 104 us
  Pallas kernels  59.2 us (56%)
  starting transfers between devices  24.6 us (23%)
  waiting for transfers between devices  9 us (9%)
  other arithmetic  7.26 us (7%)
  local copies, waits for them, and re-layouts  2.16 us (2%)
  between operations  1.47 us (1%)
    pallas_call x1, Pallas kernels, local(): pl.pallas_call(functools.partial(edge_back_kernel, size), in_specs=[SMEM,...  16.5 us
    pallas_call x1, Pallas kernels, local(): pl.pallas_call(functools.partial(forward_kernel, size), in_specs=[SMEM, V...  14.7 us
    ppermute x12, starting transfers between devices, permute(): return lax.ppermute(value, 'dom', pairs)  11.4 us
    pallas_call x1, Pallas kernels, local(): pl.pallas_call(functools.partial(early_kernel, size), in_specs=[VMEM, VME...  10.2 us
    pallas_call x1, Pallas kernels, local(): pl.pallas_call(functools.partial(scatter_kernel, size), in_specs=[SMEM, V...  9.19 us
    all_to_all x1, waiting for transfers between devices, local(): lax.all_to_all(far_grad.reshape(peers, slots, width), 'dom', split_axis=0...  8.97 us
    all_to_all x1, starting transfers between devices, local(): lax.all_to_all(far_grad.reshape(peers, slots, width), 'dom', split_axis=0...  6.62 us
    all_to_all x1, starting transfers between devices, local(): lax.all_to_all(outgoing.reshape(peers, slots, width), 'dom', split_axis=0...  6.61 us
  transfers between devices with their start and end apart: 14, of which 1 were waited for; matrix products, arithmetic and copies ran while one was open for 7% of the time, Pallas kernels for 41%

profile of v4, /device:TPU:9, one launch (start us, length us, event | category | flops | bytes accessed | tf_op | source)
XLA Modules:
  0.0 103.7 jit_solution(15770005254432176085)
XLA Ops:
  0.6 2.1 %halo_rows.1 = bf16[256,512]{1,0:T(8,128)(2,1)} custom-call(s32[1,16,16]{2,1,0:T(8,128)} %rows_ref.3, bf16[512,512]{1,0:T(8,128)(2,1)} %latent_h.5), custom_call_target="tpu_custom_call" | custom-call | flops 134217728 | bytes 786432 | tf_op jit(solution)/shard_map/halo_rows/pallas_call | solution.py:466
  2.7 6.6 %all-to-all-start = ((bf16[16,16,512]{2,1,0:T(8,128)(2,1)}), bf16[16,16,512]{2,1,0:T(8,128)(2,1)S(1)}, u32[]{:S(2)}, u32[]{:S(2)}) async-start(bf16[16,16,512]{2,1,0:T(8,128)(2,1)} %bitcast.102), calls=%async_computation | async-start | bytes 524288 | tf_op jit(solution)/shard_map/all_to_all | solution.py:475
  10.0 0.6 pad_add_fusion.scalar_ref
  10.6 10.2 %edge_early.1.pre_h = f32[2560,512]{1,0:T(8,128)} custom-call(s32[2560]{0:T(1024)} %send_ref.5, s32[2560]{0:T(1024)} %recv_ref.7, bf16[2560,512]{1,0:T(8,128)(2,1)} %edge_h.3, bf16[512,512]{1,0:T(8,128)(2,1)} %latent_h.5, bf16[1536,512]{1,0:T(8,128)(2,1)} %w1_h.7), custom_call_target="tpu_custom_call" | custom-call | flops 4697620480 | bytes 7864320 | tf_op jit(solution)/shard_map/edge_early/pallas_call | solution.py:480
  20.8 0.0 all-to-all-done
  20.8 0.0 copy-start.8
  20.8 0.7 copy-done.8
  21.5 14.7 %edge_forward.1 = (bf16[2560,512]{1,0:T(8,128)(2,1)}, bf16[2560,512]{1,0:T(8,128)(2,1)}, f32[2560,512]{1,0:T(8,128)}, f32[2,1,1280]{2,1,0:T(1,128)}, bf16[512,51...) custom-call(s32[4]{0:T(128)} %pad_add_fusion.scalar_ref, ...), custom_call_target="tpu_custom_call" | custom-call | flops 8053063680 | bytes 26214400 | tf_op jit(solution)/shard_map/edge_forward/pallas_call | solution.py:503
  36.2 0.4 collective-permute-start
  36.7 16.5 %edge_backward.1 = (bf16[2560,512]{1,0:T(8,128)(2,1)}, f32[4,128,512]{2,1,0:T(8,128)}, bf16[4,128,512]{2,1,0:T(8,128)(2,1)}) custom-call(s32[4]{0:T(128)} %pad_add_fusion.scalar_ref, s32[2560]{0:T(1024)} %recv_ref.7, f32[2,1,1280]{2,1,0:T(1,128)} %get-tuple-element.24.inverse_ref, bf16[2560,512]{1,0:T(8,128)(2,1)} %cotan_h.5, ...), custom_call_target="tpu_custom_call" | custom-call | flops 8053063680 | bytes 26214400 | tf_op jit(solution)/shard_map/edge_backward/pallas_call | solution.py:525
  53.2 0.2 collective-permute-start.3
  53.4 0.0 collective-permute-done
  53.4 0.1 fusion.9.order_h
  53.6 1.2 %collective-permute-start.8 = (bf16[4,96,512]{2,1,0:T(8,128)(2,1)S(1)}, bf16[4,96,512]{2,1,0:T(8,128)(2,1)}, u32[]{:S(2)}, u32[]{:S(2)}) collective-permute-start(bf16[4,96,512]{2,1,0:T(8,128)(2,1)S(1)} %fusion.9.order_h), channel_id=1, source_target_pairs={{0,2},{1,3},{2,0},{3,1},{4,6},{5,7},{6,4},{7,5},{8,10},{9,11},{10,... | collective-permute-start | bytes 1179656 | tf_op jit(solution)/shard_map/ppermute | solution.py:390
  54.8 9.2 %edge_scatter.1 = (f32[512,512]{1,0:T(8,128)}, bf16[256,512]{1,0:T(8,128)(2,1)}, f32[4,128,512]{2,1,0:T(8,128)}, bf16[4,128,512]{2,1,0:T(8,128)(2,1)}) custom-call(s32[4]{0:T(128)} %pad_add_fusion.scalar_ref, s32[2560]{0:T(1024)} %send_ref.5, s32[2560]{0:T(1024)} %recv_ref.7, bf16[2560,512]{1,0:T(8,128)(2,1)} %get-tuple-element.29.pre_h, ...), custom_call_target="tpu_custom_call" | custom-call | flops 6710886400 | bytes 5242880 | tf_op jit(solution)/shard_map/edge_scatter/pallas_call | solution.py:541
  64.0 0.0 copy-start.2
  64.0 0.7 collective-permute-start.1
  64.7 0.0 collective-permute-done.3
  64.7 1.3 %fusion.11 = bf16[2,128,512]{2,1,0:T(8,128)(2,1)S(1)} fusion(f32[2,2,128,512]{3,2,1,0:T(8,128)} %bitcast.105, s32[]{:T(128)S(6)} %select_n.38, bf16[2,2,128,512]{3,2,1,0:T(8,128)(2,1)S(1)} %bitcast.109), kind=kLoop, calls=%fused_computation.25 | loop fusion | flops 393216 | bytes 1048580 | tf_op jit(solution)/shard_map/convert_element_type | solution.py:403
  66.1 0.6 collective-permute-start.4
  66.7 0.0 collective-permute-done.8
  66.7 1.3 %fusion.1 = f32[4,96,512]{2,1,0:T(8,128)S(1)} fusion(bf16[4,96,512]{2,1,0:T(8,128)(2,1)} %collective-permute-done.8, f32[4,2,96,512]{3,2,1,0:T(8,128)S(1)} %bitcast.100, s32[]{:T(128)S(6)} %select_n.39, bf16[4,2,96,512]{3,2,1,0:T(8,128)(2,1)} %bitcast.108), kind=kLoop, calls=%fused_computation.10 | loop fusion | flops 786432 | bytes 2359300 | tf_op jit(solution)/shard_map/add | solution.py:408
  68.0 0.7 fusion.25
  68.8 2.1 %collective-permute-start.10 = (bf16[96,512]{1,0:T(8,128)(2,1)}, bf16[96,512]{1,0:T(8,128)(2,1)S(1)}, u32[]{:S(2)}, u32[]{:S(2)}) collective-permute-start(bf16[96,512]{1,0:T(8,128)(2,1)} %get-tuple-element.49), channel_id=1, source_target_pairs={{0,8},{1,9},{2,10},{3,11},{4,12},{5,13},{6,14},{7,15},{8,0},{9,1},... | collective-permute-start | bytes 294920 | tf_op jit(solution)/shard_map/ppermute | solution.py:390
  70.8 0.3 collective-permute-start.11
  71.1 1.2 %collective-permute-start.9 = (bf16[96,512]{1,0:T(8,128)(2,1)}, bf16[96,512]{1,0:T(8,128)(2,1)S(1)}, u32[]{:S(2)}, u32[]{:S(2)}) collective-permute-start(bf16[96,512]{1,0:T(8,128)(2,1)} %get-tuple-element.47), channel_id=1, source_target_pairs={{0,4},{1,5},{2,6},{3,7},{4,8},{5,9},{6,10},{7,11},{8,12},{9,13},{1... | collective-permute-start | bytes 294920 | tf_op jit(solution)/shard_map/ppermute | solution.py:390
  72.3 0.0 collective-permute-done.1
  72.3 1.0 fusion.10
  73.3 1.0 collective-permute-start.2
  74.3 0.0 collective-permute-done.4
  74.4 0.1 fusion.5
  74.5 6.6 %all-to-all-start.1 = ((bf16[16,16,512]{2,1,0:T(8,128)(2,1)}), bf16[16,16,512]{2,1,0:T(8,128)(2,1)S(1)}, u32[]{:S(2)}, u32[]{:S(2)}) async-start(bf16[16,16,512]{2,1,0:T(8,128)(2,1)} %bitcast.111), calls=%async_computation.1 | async-start | bytes 524288 | tf_op jit(solution)/shard_map/all_to_all | solution.py:558
  81.1 0.0 collective-permute-done.10
  81.1 0.0 collective-permute-done.11
  81.1 0.0 collective-permute-done.9
  81.1 0.7 fusion.21
  81.8 1.0 %fusion.8 = f32[2,128,512]{2,1,0:T(8,128)S(1)} fusion(bf16[2,128,512]{2,1,0:T(8,128)(2,1)S(1)} %collective-permute-done.2, f32[2,2,128,512]{3,2,1,0:T(8,128)S(1)} %bitcast.104, s32[]{:T(128)S(6)} %select_n.39, bf16[2,2,128,512]{3,2,1,0:T(8,128)(2,1)} %bitcast.9), kind=kLoop, calls=%fused_computation.22 | loop fusion | flops 524288 | bytes 1572868 | tf_op jit(solution)/shard_map/add | solution.py:408
  82.9 0.1 fusion.23
  83.0 1.2 %collective-permute-start.5 = (bf16[128,512]{1,0:T(8,128)(2,1)S(1)}, bf16[128,512]{1,0:T(8,128)(2,1)S(1)}, u32[]{:S(2)}, u32[]{:S(2)}) collective-permute-start(bf16[128,512]{1,0:T(8,128)(2,1)S(1)} %get-tuple-element.44), channel_id=1, source_target_pairs={{0,4},{1,5},{2,6},{3,7},{4,8},{5,9},{6,10},{7,11},{8,12},{9,13},{1... | collective-permute-start | bytes 393224 | tf_op jit(solution)/shard_map/ppermute | solution.py:390
  84.3 1.0 collective-permute-start.6
  85.3 1.4 %collective-permute-start.7 = (bf16[128,512]{1,0:T(8,128)(2,1)S(1)}, bf16[128,512]{1,0:T(8,128)(2,1)S(1)}, u32[]{:S(2)}, u32[]{:S(2)}) collective-permute-start(bf16[128,512]{1,0:T(8,128)(2,1)S(1)} %get-tuple-element.46), channel_id=1, source_target_pairs={{0,12},{1,13},{2,14},{3,15},{4,0},{5,1},{6,2},{7,3},{8,4},{9,5},{1... | collective-permute-start | bytes 393224 | tf_op jit(solution)/shard_map/ppermute | solution.py:390
  86.6 0.1 fusion.15
  86.7 9.0 %all-to-all-done.1 = bf16[16,16,512]{2,1,0:T(8,128)(2,1)S(1)} async-done(((bf16[16,16,512]{2,1,0:T(8,128)(2,1)}), bf16[16,16,512]{2,1,0:T(8,128)(2,1)S(1)}, u32[]{:S(2)}, u32[]{:S(2)}) %all-to-all-start.1) | async-done | bytes 262176 | tf_op jit(solution)/shard_map/all_to_all | solution.py:558
  95.7 0.7 copy-done.1
  96.4 6.5 %last_grads.1 = (bf16[2560,512]{1,0:T(8,128)(2,1)}, f32[512,512]{1,0:T(8,128)}) custom-call(s32[1,16,16]{2,1,0:T(8,128)} %rows_ref.3, bf16[2560,512]{1,0:T(8,128)(2,1)} %cotan_h.5, bf16[2560,512]{1,0:T(8,128)(2,1)} %get-tuple-element.29.pre_h, bf16[1536,512]{1,0:T(8,128)(2,1)} %w1_h.7, bf16[256,512]{1,0:T(8,128)(2,1)} %bitcast.101, ...), custom_call_target="tpu_custom_call" | custom-call | flops 2013265920 | bytes 7864320 | tf_op jit(solution)/shard_map/last_grads/pallas_call | solution.py:563
  102.9 0.0 collective-permute-done.6
  102.9 0.0 collective-permute-done.7
  102.9 0.8 convert_add_fusion
  (16 shorter events, 0.0 us)
Async XLA Ops:
  2.7 18.0 %all-to-all-start = ((bf16[16,16,512]{2,1,0:T(8,128)(2,1)}), bf16[16,16,512]{2,1,0:T(8,128)(2,1)S(1)}, u32[]{:S(2)}, u32[]{:S(2)}) async-start(bf16[16,16,512]{2,1,0:T(8,128)(2,1)} %bitcast.102), calls=%async_computation | async-start | bytes 524288 | tf_op jit(solution)/shard_map/all_to_all | solution.py:475
  20.8 0.7 copy-start.8
  36.2 17.2 %collective-permute-start = (bf16[8,96,512]{2,1,0:T(8,128)(2,1)}, bf16[8,96,512]{2,1,0:T(8,128)(2,1)S(1)}, u32[]{:S(2)}, u32[]{:S(2)}) collective-permute-start(bf16[8,96,512]{2,1,0:T(8,128)(2,1)} %get-tuple-element.32), channel_id=1, source_target_pairs={{0,1},{1,0},{2,3},{3,2},{4,5},{5,4},{6,7},{7,6},{8,9},{9,8},{10,11... | collective-permute-start | bytes 2359304 | tf_op jit(solution)/shard_map/ppermute | solution.py:390
  36.7 16.7 %copy-start = (f32[8,96,512]{2,1,0:T(8,128)S(1)}, f32[8,96,512]{2,1,0:T(8,128)}, u32[]{:S(2)}) copy-start(f32[8,96,512]{2,1,0:T(8,128)} %get-tuple-element.31) | copy-start | bytes 4718596
  53.2 11.5 %collective-permute-start.3 = (bf16[4,128,512]{2,1,0:T(8,128)(2,1)}, bf16[4,128,512]{2,1,0:T(8,128)(2,1)S(1)}, u32[]{:S(2)}, u32[]{:S(2)}) collective-permute-start(bf16[4,128,512]{2,1,0:T(8,128)(2,1)} %get-tuple-element.36), channel_id=1, source_target_pairs={{0,1},{1,0},{2,3},{3,2},{4,5},{5,4},{6,7},{7,6},{8,9},{9,8},{10,11... | collective-permute-start | bytes 1572872 | tf_op jit(solution)/shard_map/ppermute | solution.py:390
  53.4 1.4 %copy-start.4 = (bf16[8,96,512]{2,1,0:T(8,128)(2,1)}, bf16[8,96,512]{2,1,0:T(8,128)(2,1)S(1)}, u32[]{:S(2)}) copy-start(bf16[8,96,512]{2,1,0:T(8,128)(2,1)S(1)} %collective-permute-done) | copy-start | bytes 2359300
  53.5 1.3 %copy-start.7 = (bf16[4,96,512]{2,1,0:T(8,128)(2,1)}, bf16[4,96,512]{2,1,0:T(8,128)(2,1)S(1)}, u32[]{:S(2)}) copy-start(bf16[4,96,512]{2,1,0:T(8,128)(2,1)S(1)} %fusion.9.order_h) | copy-start | bytes 1179652
  53.6 13.1 %collective-permute-start.8 = (bf16[4,96,512]{2,1,0:T(8,128)(2,1)S(1)}, bf16[4,96,512]{2,1,0:T(8,128)(2,1)}, u32[]{:S(2)}, u32[]{:S(2)}) collective-permute-start(bf16[4,96,512]{2,1,0:T(8,128)(2,1)S(1)} %fusion.9.order_h), channel_id=1, source_target_pairs={{0,2},{1,3},{2,0},{3,1},{4,6},{5,7},{6,4},{7,5},{8,10},{9,11},{10,... | collective-permute-start | bytes 1179656 | tf_op jit(solution)/shard_map/ppermute | solution.py:390
  64.0 8.3 %copy-start.2 = (f32[4,128,512]{2,1,0:T(8,128)S(1)}, f32[4,128,512]{2,1,0:T(8,128)}, u32[]{:S(2)}) copy-start(f32[4,128,512]{2,1,0:T(8,128)} %get-tuple-element.33) | copy-start | bytes 3145732
  64.0 8.3 %collective-permute-start.1 = (bf16[4,128,512]{2,1,0:T(8,128)(2,1)}, bf16[4,128,512]{2,1,0:T(8,128)(2,1)}, u32[]{:S(2)}, u32[]{:S(2)}) collective-permute-start(bf16[4,128,512]{2,1,0:T(8,128)(2,1)} %get-tuple-element.34), channel_id=1, source_target_pairs={{0,1},{1,0},{2,3},{3,2},{4,5},{5,4},{6,7},{7,6},{8,9},{9,8},{10,11... | collective-permute-start | bytes 1572872 | tf_op jit(solution)/shard_map/ppermute | solution.py:390
  64.7 9.6 %copy-start.3 = (f32[4,128,512]{2,1,0:T(8,128)S(1)}, f32[4,128,512]{2,1,0:T(8,128)}, u32[]{:S(2)}) copy-start(f32[4,128,512]{2,1,0:T(8,128)} %get-tuple-element.35) | copy-start | bytes 3145732
  64.7 2.0 %copy-start.5 = (bf16[4,128,512]{2,1,0:T(8,128)(2,1)}, bf16[4,128,512]{2,1,0:T(8,128)(2,1)S(1)}, u32[]{:S(2)}) copy-start(bf16[4,128,512]{2,1,0:T(8,128)(2,1)S(1)} %collective-permute-done.3) | copy-start | bytes 1572868
  66.1 8.3 %collective-permute-start.4 = (bf16[2,128,512]{2,1,0:T(8,128)(2,1)S(1)}, bf16[2,128,512]{2,1,0:T(8,128)(2,1)S(1)}, u32[]{:S(2)}, u32[]{:S(2)}) collective-permute-start(bf16[2,128,512]{2,1,0:T(8,128)(2,1)S(1)} %fusion.11), channel_id=1, source_target_pairs={{0,2},{1,3},{2,0},{3,1},{4,6},{5,7},{6,4},{7,5},{8,10},{9,11},{10,... | collective-permute-start | bytes 786440 | tf_op jit(solution)/shard_map/ppermute | solution.py:390
  66.7 7.7 %copy-start.6 = (bf16[4,128,512]{2,1,0:T(8,128)(2,1)S(1)}, bf16[4,128,512]{2,1,0:T(8,128)(2,1)}, u32[]{:S(2)}) copy-start(bf16[4,128,512]{2,1,0:T(8,128)(2,1)} %copy-done.5) | copy-start | bytes 1572868
  68.8 12.3 %collective-permute-start.10 = (bf16[96,512]{1,0:T(8,128)(2,1)}, bf16[96,512]{1,0:T(8,128)(2,1)S(1)}, u32[]{:S(2)}, u32[]{:S(2)}) collective-permute-start(bf16[96,512]{1,0:T(8,128)(2,1)} %get-tuple-element.49), channel_id=1, source_target_pairs={{0,8},{1,9},{2,10},{3,11},{4,12},{5,13},{6,14},{7,15},{8,0},{9,1},... | collective-permute-start | bytes 294920 | tf_op jit(solution)/shard_map/ppermute | solution.py:390
  70.8 10.2 %collective-permute-start.11 = (bf16[96,512]{1,0:T(8,128)(2,1)}, bf16[96,512]{1,0:T(8,128)(2,1)S(1)}, u32[]{:S(2)}, u32[]{:S(2)}) collective-permute-start(bf16[96,512]{1,0:T(8,128)(2,1)} %get-tuple-element.48), channel_id=1, source_target_pairs={{0,12},{1,13},{2,14},{3,15},{4,0},{5,1},{6,2},{7,3},{8,4},{9,5},{1... | collective-permute-start | bytes 294920 | tf_op jit(solution)/shard_map/ppermute | solution.py:390
  71.1 10.0 %collective-permute-start.9 = (bf16[96,512]{1,0:T(8,128)(2,1)}, bf16[96,512]{1,0:T(8,128)(2,1)S(1)}, u32[]{:S(2)}, u32[]{:S(2)}) collective-permute-start(bf16[96,512]{1,0:T(8,128)(2,1)} %get-tuple-element.47), channel_id=1, source_target_pairs={{0,4},{1,5},{2,6},{3,7},{4,8},{5,9},{6,10},{7,11},{8,12},{9,13},{1... | collective-permute-start | bytes 294920 | tf_op jit(solution)/shard_map/ppermute | solution.py:390
  73.3 8.5 %collective-permute-start.2 = (bf16[2,128,512]{2,1,0:T(8,128)(2,1)S(1)}, bf16[2,128,512]{2,1,0:T(8,128)(2,1)S(1)}, u32[]{:S(2)}, u32[]{:S(2)}) collective-permute-start(bf16[2,128,512]{2,1,0:T(8,128)(2,1)S(1)} %fusion.10), channel_id=1, source_target_pairs={{0,2},{1,3},{2,0},{3,1},{4,6},{5,7},{6,4},{7,5},{8,10},{9,11},{10,... | collective-permute-start | bytes 786440 | tf_op jit(solution)/shard_map/ppermute | solution.py:390
  74.5 21.2 %all-to-all-start.1 = ((bf16[16,16,512]{2,1,0:T(8,128)(2,1)}), bf16[16,16,512]{2,1,0:T(8,128)(2,1)S(1)}, u32[]{:S(2)}, u32[]{:S(2)}) async-start(bf16[16,16,512]{2,1,0:T(8,128)(2,1)} %bitcast.111), calls=%async_computation.1 | async-start | bytes 524288 | tf_op jit(solution)/shard_map/all_to_all | solution.py:558
  83.0 19.8 %collective-permute-start.5 = (bf16[128,512]{1,0:T(8,128)(2,1)S(1)}, bf16[128,512]{1,0:T(8,128)(2,1)S(1)}, u32[]{:S(2)}, u32[]{:S(2)}) collective-permute-start(bf16[128,512]{1,0:T(8,128)(2,1)S(1)} %get-tuple-element.44), channel_id=1, source_target_pairs={{0,4},{1,5},{2,6},{3,7},{4,8},{5,9},{6,10},{7,11},{8,12},{9,13},{1... | collective-permute-start | bytes 393224 | tf_op jit(solution)/shard_map/ppermute | solution.py:390
  84.3 18.6 %collective-permute-start.6 = (bf16[128,512]{1,0:T(8,128)(2,1)S(1)}, bf16[128,512]{1,0:T(8,128)(2,1)S(1)}, u32[]{:S(2)}, u32[]{:S(2)}) collective-permute-start(bf16[128,512]{1,0:T(8,128)(2,1)S(1)} %get-tuple-element.45), channel_id=1, source_target_pairs={{0,8},{1,9},{2,10},{3,11},{4,12},{5,13},{6,14},{7,15},{8,0},{9,1},... | collective-permute-start | bytes 393224 | tf_op jit(solution)/shard_map/ppermute | solution.py:390
  85.3 17.6 %collective-permute-start.7 = (bf16[128,512]{1,0:T(8,128)(2,1)S(1)}, bf16[128,512]{1,0:T(8,128)(2,1)S(1)}, u32[]{:S(2)}, u32[]{:S(2)}) collective-permute-start(bf16[128,512]{1,0:T(8,128)(2,1)S(1)} %get-tuple-element.46), channel_id=1, source_target_pairs={{0,12},{1,13},{2,14},{3,15},{4,0},{5,1},{6,2},{7,3},{8,4},{9,5},{1... | collective-permute-start | bytes 393224 | tf_op jit(solution)/shard_map/ppermute | solution.py:390
  95.7 0.7 copy-start.1

commit v5 on v4

--- a/solution.py
+++ b/solution.py
@@ -10,6 +10,7 @@
 BF = jnp.bfloat16
 F32 = jnp.float32
 VMEM_BYTES = 58 * 1024 * 1024
+SMALL_BYTES = 52 * 1024 * 1024
 ANY = pl.BlockSpec(memory_space=pl.ANY)
 VMEM = pl.BlockSpec(memory_space=pltpu.VMEM)
 SMEM = pl.BlockSpec(memory_space=pltpu.SMEM)
@@ -120,11 +121,8 @@
 
 
 def each_block(turns, body):
-    def step(turn, carry):
+    for turn in range(turns):
         body(turn)
-        return carry
-
-    lax.fori_loop(0, turns, step, 0)
 
 
 def rows_kernel(rows_ref, latent_ref, out_ref):
@@ -449,6 +447,7 @@
     place = lax.axis_index("dom")
     scalars = jnp.stack([edge_count[0], place & 1, (place >> 1) & 1, place >> 2]).astype(jnp.int32)
     params = pltpu.CompilerParams(vmem_limit_bytes=VMEM_BYTES)
+    small = pltpu.CompilerParams(vmem_limit_bytes=SMALL_BYTES)
     unit = 2 * edges * width * width
 
     def cost(units, bytes_accessed):
@@ -509,7 +508,7 @@
         + buffer(*state, *ends)
         + buffer(shape(halo, BF), shape(nodes, F32), shape(3 * width, F32))
         + [DMA((turns,)), DMA((3, turns)), DMA((7,)), DMA((4,))],
-        compiler_params=params,
+        compiler_params=small,
         cost_estimate=cost(6, edges * width * 20),
         name="edge_forward",
     )(
@@ -531,7 +530,7 @@
             edge_cotan, normed, slope, hidden, edge_latent, agg_grad, edge_w2, pre_low, *kept, two
         )
         + [DMA((5, turns)), DMA((turns,)), DMA((2,)), DMA((2,))],
-        compiler_params=params,
+        compiler_params=small,
         cost_estimate=cost(6, edges * width * 20),
         name="edge_backward",
     )(scalars, receivers, inverse, edge_cotan, normed, slope, hidden, edge_latent, agg_grad, edge_w2)
@@ -546,7 +545,7 @@
         scratch_shapes=buffer(pre_low, shape(2 * width, BF), grad_part, node_latent, incoming, far_shape, *kept)
         + buffer(shape(nodes + halo, F32), shape(nodes, F32), two)
         + [DMA((turns,)), DMA((4,)), DMA((4,))],
-        compiler_params=params,
+        compiler_params=small,
         cost_estimate=cost(5, edges * width * 4),
         name="edge_scatter",
     )(scalars, senders, receivers, grad_pre, edge_w1, grad_part, node_latent, incoming, order)
@@ -567,7 +566,7 @@
         out_shape=[pre_low, shape(nodes, F32)],
         scratch_shapes=buffer(edge_cotan, grad_pre, square, far_shape, shape(nodes, F32), pre_low)
         + [DMA((2, turns)), DMA((turns,)), DMA((4,))],
-        compiler_params=params,
+        compiler_params=small,
         cost_estimate=cost(1.5, edges * width * 6),
         name="last_grads",
     )(send_rows, edge_cotan, grad_pre, edge_w1, returned, node_part)

time: 105 us -> 98.5 us (0.938)
  the two profiles are of different devices: /device:TPU:9 before, /device:TPU:0 now
where the time goes in v5:
time: 98.5 us; the launch traced here: 97 us
  Pallas kernels  54.7 us (56%)
  starting transfers between devices  27.3 us (28%)
  other arithmetic  8.85 us (9%)
  waiting for transfers between devices  3.83 us (4%)
  between operations  1.53 us (2%)
    ppermute x12, starting transfers between devices, permute(): return lax.ppermute(value, 'dom', pairs)  15 us
    pallas_call x1, Pallas kernels, local(): pl.pallas_call(functools.partial(edge_back_kernel, size), in_specs=[SMEM,...  14.9 us
    pallas_call x1, Pallas kernels, local(): pl.pallas_call(functools.partial(forward_kernel, size), in_specs=[SMEM, V...  13.7 us
    pallas_call x1, Pallas kernels, local(): pl.pallas_call(functools.partial(early_kernel, size), in_specs=[VMEM, VME...  9.44 us
    pallas_call x1, Pallas kernels, local(): pl.pallas_call(functools.partial(scatter_kernel, size), in_specs=[SMEM, V...  8.88 us
    all_to_all x1, starting transfers between devices, local(): lax.all_to_all(outgoing.reshape(peers, slots, width), 'dom', split_axis=0...  7.39 us
    pallas_call x1, Pallas kernels, local(): pl.pallas_call(functools.partial(last_kernel, size), in_specs=[VMEM] + [A...  5.63 us
    all_to_all x1, starting transfers between devices, local(): lax.all_to_all(far_grad.reshape(peers, slots, width), 'dom', split_axis=0...  4.9 us
  transfers between devices with their start and end apart: 14, of which 2 were waited for; matrix products, arithmetic and copies ran while one was open for 9% of the time, Pallas kernels for 40%

profile of v5, /device:TPU:0, one launch (start us, length us, event | category | flops | bytes accessed | tf_op | source)
XLA Modules:
  0.0 97.0 jit_solution(10743376856150646249)
XLA Ops:
  0.6 2.1 %halo_rows.1 = bf16[256,512]{1,0:T(8,128)(2,1)} custom-call(s32[1,16,16]{2,1,0:T(8,128)} %rows_ref.3, bf16[512,512]{1,0:T(8,128)(2,1)} %latent_h.5), custom_call_target="tpu_custom_call" | custom-call | flops 134217728 | bytes 786432 | tf_op jit(solution)/shard_map/halo_rows/pallas_call | solution.py:465
  2.7 7.4 %all-to-all-start = ((bf16[16,16,512]{2,1,0:T(8,128)(2,1)}), bf16[16,16,512]{2,1,0:T(8,128)(2,1)S(1)}, u32[]{:S(2)}, u32[]{:S(2)}) async-start(bf16[16,16,512]{2,1,0:T(8,128)(2,1)} %bitcast.104), calls=%async_computation | async-start | bytes 524288 | tf_op jit(solution)/shard_map/all_to_all | solution.py:474
  10.8 0.1 pad_add_fusion.scalar_ref
  10.9 9.4 %edge_early.1.pre_h = f32[2560,512]{1,0:T(8,128)} custom-call(s32[2560]{0:T(1024)} %send_ref.5, s32[2560]{0:T(1024)} %recv_ref.7, bf16[2560,512]{1,0:T(8,128)(2,1)} %edge_h.3, bf16[512,512]{1,0:T(8,128)(2,1)} %latent_h.5, bf16[1536,512]{1,0:T(8,128)(2,1)} %w1_h.7), custom_call_target="tpu_custom_call" | custom-call | flops 4697620480 | bytes 7864320 | tf_op jit(solution)/shard_map/edge_early/pallas_call | solution.py:479
  20.3 0.0 all-to-all-done
  20.4 13.7 %edge_forward.1 = (bf16[2560,512]{1,0:T(8,128)(2,1)}, bf16[2560,512]{1,0:T(8,128)(2,1)}, f32[2560,512]{1,0:T(8,128)}, f32[2,1,1280]{2,1,0:T(1,128)S(1)}, bf16[51...) custom-call(s32[4]{0:T(128)S(1)} %pad_add_fusion.scalar_ref, ...), custom_call_target="tpu_custom_call" | custom-call | flops 8053063680 | bytes 26214400 | tf_op jit(solution)/shard_map/edge_forward/pallas_call | solution.py:502
  34.1 0.5 collective-permute-start
  34.6 14.9 %edge_backward.1 = (bf16[2560,512]{1,0:T(8,128)(2,1)}, f32[4,128,512]{2,1,0:T(8,128)}, bf16[4,128,512]{2,1,0:T(8,128)(2,1)S(1)}) custom-call(s32[4]{0:T(128)S(1)} %pad_add_fusion.scalar_ref, s32[2560]{0:T(1024)S(1)} %copy-done.4, f32[2,1,1280]{2,1,0:T(1,128)S(1)} %get-tuple-element.24.inverse_ref, bf16[2560,512]{1,0:T(8,128)(2,1)} %cotan_h.5, ...), custom_call_target="tpu_custom_call" | custom-call | flops 8053063680 | bytes 26214400 | tf_op jit(solution)/shard_map/edge_backward/pallas_call | solution.py:524
  49.5 0.2 collective-permute-start.3
  49.7 0.0 collective-permute-done
  49.7 0.1 fusion.9.order_h
  49.8 2.0 %collective-permute-start.8 = (bf16[4,96,512]{2,1,0:T(8,128)(2,1)S(1)}, bf16[4,96,512]{2,1,0:T(8,128)(2,1)}, u32[]{:S(2)}, u32[]{:S(2)}) collective-permute-start(bf16[4,96,512]{2,1,0:T(8,128)(2,1)S(1)} %fusion.9.order_h), channel_id=1, source_target_pairs={{0,2},{1,3},{2,0},{3,1},{4,6},{5,7},{6,4},{7,5},{8,10},{9,11},{10,... | collective-permute-start | bytes 1179656 | tf_op jit(solution)/shard_map/ppermute | solution.py:388
  51.8 8.9 %edge_scatter.1 = (f32[512,512]{1,0:T(8,128)}, bf16[256,512]{1,0:T(8,128)(2,1)}, f32[4,128,512]{2,1,0:T(8,128)}, bf16[4,128,512]{2,1,0:T(8,128)(2,1)S(1)}) custom-call(s32[4]{0:T(128)S(1)} %pad_add_fusion.scalar_ref, s32[2560]{0:T(1024)S(1)} %copy-done.5, s32[2560]{0:T(1024)S(1)} %copy-done.4, bf16[2560,512]{1,0:T(8,128)(2,1)} %get-tuple-element.29.pre_h, ...), custom_call_target="tpu_custom_call" | custom-call | flops 6710886400 | bytes 5242880 | tf_op jit(solution)/shard_map/edge_scatter/pallas_call | solution.py:540
  60.7 0.1 collective-permute-start.1
  60.8 0.0 collective-permute-done.3
  60.8 1.1 %fusion.11 = bf16[2,128,512]{2,1,0:T(8,128)(2,1)S(1)} fusion(f32[2,2,128,512]{3,2,1,0:T(8,128)S(1)} %bitcast.107, s32[]{:T(128)S(6)} %select_n.38, bf16[2,2,128,512]{3,2,1,0:T(8,128)(2,1)} %bitcast.13), kind=kLoop, calls=%fused_computation.25 | loop fusion | flops 393216 | bytes 1048580 | tf_op jit(solution)/shard_map/convert_element_type | solution.py:401
  61.9 0.9 collective-permute-start.4
  62.8 0.0 collective-permute-done.8
  62.8 1.5 %fusion.1 = f32[4,96,512]{2,1,0:T(8,128)S(1)} fusion(bf16[4,96,512]{2,1,0:T(8,128)(2,1)} %collective-permute-done.8, f32[4,2,96,512]{3,2,1,0:T(8,128)} %bitcast.102, s32[]{:T(128)S(6)} %select_n.39, bf16[4,2,96,512]{3,2,1,0:T(8,128)(2,1)} %bitcast.110), kind=kLoop, calls=%fused_computation.10 | loop fusion | flops 786432 | bytes 2359300 | tf_op jit(solution)/shard_map/add | solution.py:406
  64.3 0.7 fusion.25
  65.0 2.4 %collective-permute-start.10 = (bf16[96,512]{1,0:T(8,128)(2,1)}, bf16[96,512]{1,0:T(8,128)(2,1)}, u32[]{:S(2)}, u32[]{:S(2)}) collective-permute-start(bf16[96,512]{1,0:T(8,128)(2,1)} %get-tuple-element.49), channel_id=1, source_target_pairs={{0,8},{1,9},{2,10},{3,11},{4,12},{5,13},{6,14},{7,15},{8,0},{9,1},... | collective-permute-start | bytes 294920 | tf_op jit(solution)/shard_map/ppermute | solution.py:388
  67.4 1.5 %collective-permute-start.11 = (bf16[96,512]{1,0:T(8,128)(2,1)}, bf16[96,512]{1,0:T(8,128)(2,1)}, u32[]{:S(2)}, u32[]{:S(2)}) collective-permute-start(bf16[96,512]{1,0:T(8,128)(2,1)} %get-tuple-element.48), channel_id=1, source_target_pairs={{0,12},{1,13},{2,14},{3,15},{4,0},{5,1},{6,2},{7,3},{8,4},{9,5},{1... | collective-permute-start | bytes 294920 | tf_op jit(solution)/shard_map/ppermute | solution.py:388
  68.8 0.6 collective-permute-start.9
  69.4 0.0 collective-permute-done.1
  69.4 1.0 %fusion.10 = bf16[2,128,512]{2,1,0:T(8,128)(2,1)S(1)} fusion(f32[2,2,128,512]{3,2,1,0:T(8,128)S(1)} %bitcast.106, s32[]{:T(128)S(6)} %select_n.38, bf16[2,2,128,512]{3,2,1,0:T(8,128)(2,1)} %bitcast.9), kind=kLoop, calls=%fused_computation.24 | loop fusion | flops 393216 | bytes 1048580 | tf_op jit(solution)/shard_map/convert_element_type | solution.py:401
  70.4 1.3 %collective-permute-start.2 = (bf16[2,128,512]{2,1,0:T(8,128)(2,1)S(1)}, bf16[2,128,512]{2,1,0:T(8,128)(2,1)S(1)}, u32[]{:S(2)}, u32[]{:S(2)}) collective-permute-start(bf16[2,128,512]{2,1,0:T(8,128)(2,1)S(1)} %fusion.10), channel_id=1, source_target_pairs={{0,2},{1,3},{2,0},{3,1},{4,6},{5,7},{6,4},{7,5},{8,10},{9,11},{10,... | collective-permute-start | bytes 786440 | tf_op jit(solution)/shard_map/ppermute | solution.py:388
  71.7 0.0 collective-permute-done.4
  71.7 1.0 %fusion.5 = f32[2,128,512]{2,1,0:T(8,128)S(1)} fusion(bf16[2,128,512]{2,1,0:T(8,128)(2,1)S(1)} %collective-permute-done.4, f32[2,2,128,512]{3,2,1,0:T(8,128)S(1)} %bitcast.108, s32[]{:T(128)S(6)} %select_n.39, bf16[2,2,128,512]{3,2,1,0:T(8,128)(2,1)} %bitcast.13), kind=kLoop, calls=%fused_computation.17 | loop fusion | flops 524288 | bytes 1572868 | tf_op jit(solution)/shard_map/add | solution.py:406
  72.8 4.9 %all-to-all-start.1 = ((bf16[16,16,512]{2,1,0:T(8,128)(2,1)}), bf16[16,16,512]{2,1,0:T(8,128)(2,1)S(1)}, u32[]{:S(2)}, u32[]{:S(2)}) async-start(bf16[16,16,512]{2,1,0:T(8,128)(2,1)} %bitcast.17), calls=%async_computation.1 | async-start | bytes 524288 | tf_op jit(solution)/shard_map/all_to_all | solution.py:557
  77.7 0.0 copy-start
  77.7 0.0 copy-start.2
  77.7 0.0 collective-permute-done.10
  77.7 0.0 collective-permute-done.11
  77.7 0.0 collective-permute-done.9
  77.7 1.8 %fusion.21 = f32[96,512]{1,0:T(8,128)} fusion(bf16[96,512]{1,0:T(8,128)(2,1)} %collective-permute-done.11, bf16[96,512]{1,0:T(8,128)(2,1)} %collective-permute-done.10, bf16[96,512]{1,0:T(8,128)(2,1)} %collective-permute-done.9, f32[4,96,512]{2,1,0:T(8,128)S(1)} %fusion.1, s32[]{:T(128)S(6)} %select_n.40), kind=kLoop, calls=%fused_computation.37 | loop fusion | flops 294912 | bytes 688132 | tf_op jit(solution)/shard_map/add | solution.py:422
  79.5 0.0 collective-permute-done.2
  79.5 1.2 %fusion.8 = f32[2,128,512]{2,1,0:T(8,128)S(1)} fusion(bf16[2,128,512]{2,1,0:T(8,128)(2,1)S(1)} %collective-permute-done.2, f32[2,2,128,512]{3,2,1,0:T(8,128)} %bitcast.105, s32[]{:T(128)S(6)} %select_n.39, bf16[2,2,128,512]{3,2,1,0:T(8,128)(2,1)} %bitcast.9), kind=kLoop, calls=%fused_computation.22 | loop fusion | flops 524288 | bytes 1572868 | tf_op jit(solution)/shard_map/add | solution.py:406
  80.7 0.1 fusion.23
  80.9 2.0 %collective-permute-start.5 = (bf16[128,512]{1,0:T(8,128)(2,1)S(1)}, bf16[128,512]{1,0:T(8,128)(2,1)S(1)}, u32[]{:S(2)}, u32[]{:S(2)}) collective-permute-start(bf16[128,512]{1,0:T(8,128)(2,1)S(1)} %get-tuple-element.44), channel_id=1, source_target_pairs={{0,4},{1,5},{2,6},{3,7},{4,8},{5,9},{6,10},{7,11},{8,12},{9,13},{1... | collective-permute-start | bytes 393224 | tf_op jit(solution)/shard_map/ppermute | solution.py:388
  82.9 2.4 %collective-permute-start.6 = (bf16[128,512]{1,0:T(8,128)(2,1)S(1)}, bf16[128,512]{1,0:T(8,128)(2,1)S(1)}, u32[]{:S(2)}, u32[]{:S(2)}) collective-permute-start(bf16[128,512]{1,0:T(8,128)(2,1)S(1)} %get-tuple-element.45), channel_id=1, source_target_pairs={{0,8},{1,9},{2,10},{3,11},{4,12},{5,13},{6,14},{7,15},{8,0},{9,1},... | collective-permute-start | bytes 393224 | tf_op jit(solution)/shard_map/ppermute | solution.py:388
  85.2 1.5 %collective-permute-start.7 = (bf16[128,512]{1,0:T(8,128)(2,1)S(1)}, bf16[128,512]{1,0:T(8,128)(2,1)S(1)}, u32[]{:S(2)}, u32[]{:S(2)}) collective-permute-start(bf16[128,512]{1,0:T(8,128)(2,1)S(1)} %get-tuple-element.46), channel_id=1, source_target_pairs={{0,12},{1,13},{2,14},{3,15},{4,0},{5,1},{6,2},{7,3},{8,4},{9,5},{1... | collective-permute-start | bytes 393224 | tf_op jit(solution)/shard_map/ppermute | solution.py:388
  86.7 0.1 fusion.15
  86.8 1.4 %all-to-all-done.1 = bf16[16,16,512]{2,1,0:T(8,128)(2,1)S(1)} async-done(((bf16[16,16,512]{2,1,0:T(8,128)(2,1)}), bf16[16,16,512]{2,1,0:T(8,128)(2,1)S(1)}, u32[]{:S(2)}, u32[]{:S(2)}) %all-to-all-start.1) | async-done | bytes 262176 | tf_op jit(solution)/shard_map/all_to_all | solution.py:557
  88.2 5.6 %last_grads.1 = (bf16[2560,512]{1,0:T(8,128)(2,1)}, f32[512,512]{1,0:T(8,128)}) custom-call(s32[1,16,16]{2,1,0:T(8,128)S(1)} %copy-done.2, bf16[2560,512]{1,0:T(8,128)(2,1)} %cotan_h.5, bf16[2560,512]{1,0:T(8,128)(2,1)} %get-tuple-element.29.pre_h, bf16[1536,512]{1,0:T(8,128)(2,1)} %w1_h.7, bf16[256,512]{1,0:T(8,128)(2,1)S(1)} %bitcast.99, ...), custom_call_target="tpu_custom_call" | custom-call | flops 2013265920 | bytes 7864320 | tf_op jit(solution)/shard_map/last_grads/pallas_call | solution.py:562
  93.8 0.0 collective-permute-done.5
  93.9 2.4 %collective-permute-done.6 = bf16[128,512]{1,0:T(8,128)(2,1)S(1)} collective-permute-done((bf16[128,512]{1,0:T(8,128)(2,1)S(1)}, bf16[128,512]{1,0:T(8,128)(2,1)S(1)}, u32[]{:S(2)}, u32[]{:S(2)}) %collective-permute-start.6) | collective-permute-done | bytes 131104 | tf_op jit(solution)/shard_map/ppermute | solution.py:388
  96.2 0.0 collective-permute-done.7
  96.2 0.8 convert_add_fusion
  (18 shorter events, 0.0 us)
Async XLA Ops:
  2.7 17.6 %all-to-all-start = ((bf16[16,16,512]{2,1,0:T(8,128)(2,1)}), bf16[16,16,512]{2,1,0:T(8,128)(2,1)S(1)}, u32[]{:S(2)}, u32[]{:S(2)}) async-start(bf16[16,16,512]{2,1,0:T(8,128)(2,1)} %bitcast.104), calls=%async_computation | async-start | bytes 524288 | tf_op jit(solution)/shard_map/all_to_all | solution.py:474
  10.9 9.5 %copy-start.1 = (bf16[512,512]{1,0:T(8,128)(2,1)S(1)}, bf16[512,512]{1,0:T(8,128)(2,1)}, u32[]{:S(2)}) copy-start(bf16[512,512]{1,0:T(8,128)(2,1)} %latent_h.5) | copy-start | bytes 1572868
  10.9 9.5 %copy-start.3 = (bf16[512,512]{1,0:T(8,128)(2,1)S(1)}, bf16[512,512]{1,0:T(8,128)(2,1)}, u32[]{:S(2)}) copy-start(bf16[512,512]{1,0:T(8,128)(2,1)} %w2_h.3) | copy-start | bytes 1572868
  10.9 9.5 %copy-start.4 = (s32[2560]{0:T(1024)S(1)}, s32[2560]{0:T(1024)}, u32[]{:S(2)}) copy-start(s32[2560]{0:T(1024)} %recv_ref.7) | copy-start | bytes 30724
  10.9 9.5 %copy-start.5 = (s32[2560]{0:T(1024)S(1)}, s32[2560]{0:T(1024)}, u32[]{:S(2)}) copy-start(s32[2560]{0:T(1024)} %send_ref.5) | copy-start | bytes 30724
  34.1 15.6 %collective-permute-start = (bf16[8,96,512]{2,1,0:T(8,128)(2,1)}, bf16[8,96,512]{2,1,0:T(8,128)(2,1)S(1)}, u32[]{:S(2)}, u32[]{:S(2)}) collective-permute-start(bf16[8,96,512]{2,1,0:T(8,128)(2,1)} %get-tuple-element.32), channel_id=1, source_target_pairs={{0,1},{1,0},{2,3},{3,2},{4,5},{5,4},{6,7},{7,6},{8,9},{9,8},{10,11... | collective-permute-start | bytes 2359304 | tf_op jit(solution)/shard_map/ppermute | solution.py:388
  34.6 15.1 %copy-start.6 = (f32[8,96,512]{2,1,0:T(8,128)S(1)}, f32[8,96,512]{2,1,0:T(8,128)}, u32[]{:S(2)}) copy-start(f32[8,96,512]{2,1,0:T(8,128)} %get-tuple-element.31) | copy-start | bytes 4718596
  49.5 11.3 %collective-permute-start.3 = (bf16[4,128,512]{2,1,0:T(8,128)(2,1)S(1)}, bf16[4,128,512]{2,1,0:T(8,128)(2,1)}, u32[]{:S(2)}, u32[]{:S(2)}) collective-permute-start(bf16[4,128,512]{2,1,0:T(8,128)(2,1)S(1)} %get-tuple-element.36), channel_id=1, source_target_pairs={{0,1},{1,0},{2,3},{3,2},{4,5},{5,4},{6,7},{7,6},{8,9},{9,8},{10,11... | collective-permute-start | bytes 1572872 | tf_op jit(solution)/shard_map/ppermute | solution.py:388
  49.7 2.1 %copy-start.9 = (bf16[8,96,512]{2,1,0:T(8,128)(2,1)}, bf16[8,96,512]{2,1,0:T(8,128)(2,1)S(1)}, u32[]{:S(2)}) copy-start(bf16[8,96,512]{2,1,0:T(8,128)(2,1)S(1)} %collective-permute-done) | copy-start | bytes 2359300
  49.8 13.0 %collective-permute-start.8 = (bf16[4,96,512]{2,1,0:T(8,128)(2,1)S(1)}, bf16[4,96,512]{2,1,0:T(8,128)(2,1)}, u32[]{:S(2)}, u32[]{:S(2)}) collective-permute-start(bf16[4,96,512]{2,1,0:T(8,128)(2,1)S(1)} %fusion.9.order_h), channel_id=1, source_target_pairs={{0,2},{1,3},{2,0},{3,1},{4,6},{5,7},{6,4},{7,5},{8,10},{9,11},{10,... | collective-permute-start | bytes 1179656 | tf_op jit(solution)/shard_map/ppermute | solution.py:388
  51.8 9.0 %copy-start.8 = (f32[4,128,512]{2,1,0:T(8,128)S(1)}, f32[4,128,512]{2,1,0:T(8,128)}, u32[]{:S(2)}) copy-start(f32[4,128,512]{2,1,0:T(8,128)} %get-tuple-element.35) | copy-start | bytes 3145732
  60.7 8.7 %copy-start.7 = (f32[4,128,512]{2,1,0:T(8,128)S(1)}, f32[4,128,512]{2,1,0:T(8,128)}, u32[]{:S(2)}) copy-start(f32[4,128,512]{2,1,0:T(8,128)} %get-tuple-element.33) | copy-start | bytes 3145732
  60.7 8.7 %collective-permute-start.1 = (bf16[4,128,512]{2,1,0:T(8,128)(2,1)S(1)}, bf16[4,128,512]{2,1,0:T(8,128)(2,1)}, u32[]{:S(2)}, u32[]{:S(2)}) collective-permute-start(bf16[4,128,512]{2,1,0:T(8,128)(2,1)S(1)} %get-tuple-element.34), channel_id=1, source_target_pairs={{0,1},{1,0},{2,3},{3,2},{4,5},{5,4},{6,7},{7,6},{8,9},{9,8},{10,11... | collective-permute-start | bytes 1572872 | tf_op jit(solution)/shard_map/ppermute | solution.py:388
  61.9 9.8 %collective-permute-start.4 = (bf16[2,128,512]{2,1,0:T(8,128)(2,1)S(1)}, bf16[2,128,512]{2,1,0:T(8,128)(2,1)S(1)}, u32[]{:S(2)}, u32[]{:S(2)}) collective-permute-start(bf16[2,128,512]{2,1,0:T(8,128)(2,1)S(1)} %fusion.11), channel_id=1, source_target_pairs={{0,2},{1,3},{2,0},{3,1},{4,6},{5,7},{6,4},{7,5},{8,10},{9,11},{10,... | collective-permute-start | bytes 786440 | tf_op jit(solution)/shard_map/ppermute | solution.py:388
  65.0 12.7 %collective-permute-start.10 = (bf16[96,512]{1,0:T(8,128)(2,1)}, bf16[96,512]{1,0:T(8,128)(2,1)}, u32[]{:S(2)}, u32[]{:S(2)}) collective-permute-start(bf16[96,512]{1,0:T(8,128)(2,1)} %get-tuple-element.49), channel_id=1, source_target_pairs={{0,8},{1,9},{2,10},{3,11},{4,12},{5,13},{6,14},{7,15},{8,0},{9,1},... | collective-permute-start | bytes 294920 | tf_op jit(solution)/shard_map/ppermute | solution.py:388
  67.4 10.3 %collective-permute-start.11 = (bf16[96,512]{1,0:T(8,128)(2,1)}, bf16[96,512]{1,0:T(8,128)(2,1)}, u32[]{:S(2)}, u32[]{:S(2)}) collective-permute-start(bf16[96,512]{1,0:T(8,128)(2,1)} %get-tuple-element.48), channel_id=1, source_target_pairs={{0,12},{1,13},{2,14},{3,15},{4,0},{5,1},{6,2},{7,3},{8,4},{9,5},{1... | collective-permute-start | bytes 294920 | tf_op jit(solution)/shard_map/ppermute | solution.py:388
  68.8 8.9 %collective-permute-start.9 = (bf16[96,512]{1,0:T(8,128)(2,1)}, bf16[96,512]{1,0:T(8,128)(2,1)}, u32[]{:S(2)}, u32[]{:S(2)}) collective-permute-start(bf16[96,512]{1,0:T(8,128)(2,1)} %get-tuple-element.47), channel_id=1, source_target_pairs={{0,4},{1,5},{2,6},{3,7},{4,8},{5,9},{6,10},{7,11},{8,12},{9,13},{1... | collective-permute-start | bytes 294920 | tf_op jit(solution)/shard_map/ppermute | solution.py:388
  70.4 9.1 %collective-permute-start.2 = (bf16[2,128,512]{2,1,0:T(8,128)(2,1)S(1)}, bf16[2,128,512]{2,1,0:T(8,128)(2,1)S(1)}, u32[]{:S(2)}, u32[]{:S(2)}) collective-permute-start(bf16[2,128,512]{2,1,0:T(8,128)(2,1)S(1)} %fusion.10), channel_id=1, source_target_pairs={{0,2},{1,3},{2,0},{3,1},{4,6},{5,7},{6,4},{7,5},{8,10},{9,11},{10,... | collective-permute-start | bytes 786440 | tf_op jit(solution)/shard_map/ppermute | solution.py:388
  72.8 15.4 %all-to-all-start.1 = ((bf16[16,16,512]{2,1,0:T(8,128)(2,1)}), bf16[16,16,512]{2,1,0:T(8,128)(2,1)S(1)}, u32[]{:S(2)}, u32[]{:S(2)}) async-start(bf16[16,16,512]{2,1,0:T(8,128)(2,1)} %bitcast.17), calls=%async_computation.1 | async-start | bytes 524288 | tf_op jit(solution)/shard_map/all_to_all | solution.py:557
  77.7 10.5 %copy-start = (f32[512,512]{1,0:T(8,128)S(1)}, f32[512,512]{1,0:T(8,128)}, u32[]{:S(2)}) copy-start(f32[512,512]{1,0:T(8,128)} %get-tuple-element.39.part_h) | copy-start | bytes 3145732
  77.7 10.5 %copy-start.2 = (s32[1,16,16]{2,1,0:T(8,128)S(1)}, s32[1,16,16]{2,1,0:T(8,128)}, u32[]{:S(2)}) copy-start(s32[1,16,16]{2,1,0:T(8,128)} %rows_ref.3) | copy-start | bytes 3076
  80.9 12.9 %collective-permute-start.5 = (bf16[128,512]{1,0:T(8,128)(2,1)S(1)}, bf16[128,512]{1,0:T(8,128)(2,1)S(1)}, u32[]{:S(2)}, u32[]{:S(2)}) collective-permute-start(bf16[128,512]{1,0:T(8,128)(2,1)S(1)} %get-tuple-element.44), channel_id=1, source_target_pairs={{0,4},{1,5},{2,6},{3,7},{4,8},{5,9},{6,10},{7,11},{8,12},{9,13},{1... | collective-permute-start | bytes 393224 | tf_op jit(solution)/shard_map/ppermute | solution.py:388
  82.9 13.3 %collective-permute-start.6 = (bf16[128,512]{1,0:T(8,128)(2,1)S(1)}, bf16[128,512]{1,0:T(8,128)(2,1)S(1)}, u32[]{:S(2)}, u32[]{:S(2)}) collective-permute-start(bf16[128,512]{1,0:T(8,128)(2,1)S(1)} %get-tuple-element.45), channel_id=1, source_target_pairs={{0,8},{1,9},{2,10},{3,11},{4,12},{5,13},{6,14},{7,15},{8,0},{9,1},... | collective-permute-start | bytes 393224 | tf_op jit(solution)/shard_map/ppermute | solution.py:388
  85.2 11.0 %collective-permute-start.7 = (bf16[128,512]{1,0:T(8,128)(2,1)S(1)}, bf16[128,512]{1,0:T(8,128)(2,1)S(1)}, u32[]{:S(2)}, u32[]{:S(2)}) collective-permute-start(bf16[128,512]{1,0:T(8,128)(2,1)S(1)} %get-tuple-element.46), channel_id=1, source_target_pairs={{0,12},{1,13},{2,14},{3,15},{4,0},{5,1},{6,2},{7,3},{8,4},{9,5},{1... | collective-permute-start | bytes 393224 | tf_op jit(solution)/shard_map/ppermute | solution.py:388

commit v6 on v5

--- a/solution.py
+++ b/solution.py
@@ -120,6 +120,10 @@
     return ref[pl.ds(pl.multiple_of(turn * size, size), size)].reshape(1, size)
 
 
+def add_block(ref, value, turn):
+    ref[...] = value if turn == 0 else ref[...] + value
+
+
 def each_block(turns, body):
     for turn in range(turns):
         body(turn)
@@ -196,7 +200,6 @@
         Blocks(slope, slope_h, out_sem.at[1], size),
         Blocks(normed, normed_h, out_sem.at[2], size),
     ]
-    gathered[...] = jnp.zeros_like(gathered)
     for copy in first:
         copy.wait()
     table[...] = dot(halo[...], wsend[...]).astype(BF)
@@ -217,7 +220,7 @@
             out.start(turn)
         place = turn * size + lax.broadcasted_iota(jnp.int32, (size, 1), 0)
         message = jnp.where(place < scalar_ref[0], unit, 0.0).astype(BF)
-        gathered[...] += dot(pick_t(block_row(recv_ref, turn, size), 0, nodes), message)
+        add_block(gathered, dot(pick_t(block_row(recv_ref, turn, size), 0, nodes), message), turn)
 
     each_block(pres.turns, body)
     for copy in later:
@@ -270,7 +273,6 @@
         block.start(0)
     first.append(begin(w2_h, w2, one_sem.at[1]))
     outs = Blocks(pre, pre_h, out_sem, size)
-    acc[...] = jnp.zeros_like(acc)
     for copy in first:
         copy.wait()
 
@@ -291,8 +293,8 @@
         grad_pre = (dot_last(grad_mixed, w2[...]) * slope[rows, :].astype(F32)).astype(BF)
         pre[rows, :] = grad_pre
         outs.start(turn)
-        acc[pl.ds(width, width), :] += dot_rows(hidden[rows, :], grad_mixed)
-        acc[pl.ds(0, width), :] += dot_rows(edge[rows, :], grad_pre)
+        add_block(acc.at[pl.ds(width, width), :], dot_rows(hidden[rows, :], grad_mixed), turn)
+        add_block(acc.at[pl.ds(0, width), :], dot_rows(edge[rows, :], grad_pre), turn)
 
     each_block(turns, body)
     stash(acc, keep, away, scalar_ref[1])
@@ -305,7 +307,7 @@
 def scatter_kernel(
     size, scalar_ref, send_ref, recv_ref, pre_h, w1_h, part_h, latent_h, halo_h, order_h,
     node_h, far_h, keep_h, away_h,
-    pre, w1, part, latent, halo, far_grad, keep, away, sent, received, acc, in_sem, one_sem, end_sem,
+    pre, w1, part, latent, halo, far_grad, keep, away, sums, acc, in_sem, one_sem, end_sem,
 ):
     del order_h
     nodes, width = latent.shape
@@ -318,8 +320,6 @@
             [(w1_h.at[pl.ds(0, 2 * width), :], w1), (part_h, part), (latent_h, latent), (halo_h, halo)]
         )
     ]
-    sent[...] = jnp.zeros_like(sent)
-    received[...] = jnp.zeros_like(received)
 
     def body(turn):
         ins.wait(turn)
@@ -331,16 +331,22 @@
                 copy.start()
 
         rows = pl.ds(pl.multiple_of(turn * size, size), size)
-        sent[...] += dot(pick_t(block_row(send_ref, turn, size), 0, nodes + far_rows), pre[rows, :])
-        received[...] += dot(pick_t(block_row(recv_ref, turn, size), 0, nodes), pre[rows, :])
+        both = jnp.concatenate(
+            [
+                pick_t(block_row(send_ref, turn, size), 0, nodes + far_rows),
+                pick_t(block_row(recv_ref, turn, size), 0, nodes),
+            ],
+            0,
+        )
+        add_block(sums, dot(both, pre[rows, :]), turn)
 
     each_block(ins.turns, body)
     for copy in later:
         copy.wait()
     w_send = w1[pl.ds(0, width), :]
-    near = sent[pl.ds(0, nodes), :].astype(BF)
-    far = sent[pl.ds(nodes, far_rows), :].astype(BF)
-    into = received[...].astype(BF)
+    near = sums[pl.ds(0, nodes), :].astype(BF)
+    far = sums[pl.ds(nodes, far_rows), :].astype(BF)
+    into = sums[pl.ds(nodes + far_rows, nodes), :].astype(BF)
     acc[pl.ds(0, width), :] = dot_rows(latent[...], near) + dot_rows(halo[...], far)
     acc[pl.ds(width, width), :] = dot_rows(latent[...], into)
     stash(acc, keep, away, scalar_ref[1])
@@ -543,9 +549,9 @@
         out_specs=[ANY] * 4,
         out_shape=[shape(nodes, F32), far_shape] + kept,
         scratch_shapes=buffer(pre_low, shape(2 * width, BF), grad_part, node_latent, incoming, far_shape, *kept)
-        + buffer(shape(nodes + halo, F32), shape(nodes, F32), two)
+        + buffer(shape(2 * nodes + halo, F32), two)
         + [DMA((turns,)), DMA((4,)), DMA((4,))],
-        compiler_params=small,
+        compiler_params=pltpu.CompilerParams(vmem_limit_bytes=50 * 1024 * 1024),
         cost_estimate=cost(5, edges * width * 4),
         name="edge_scatter",
     )(scalars, senders, receivers, grad_pre, edge_w1, grad_part, node_latent, incoming, order)

time: 98.5 us -> 97.7 us (level)
  no operation moved by 1% of the time
where the time goes in v6:
time: 97.7 us; the launch traced here: 96.1 us
  Pallas kernels  53.8 us (55%)
  starting transfers between devices  27.2 us (28%)
  other arithmetic  8.67 us (9%)
  waiting for transfers between devices  4.04 us (4%)
  between operations  1.52 us (2%)
    pallas_call x1, Pallas kernels, local(): pl.pallas_call(functools.partial(edge_back_kernel, size), in_specs=[SMEM,...  15 us
    ppermute x12, starting transfers between devices, permute(): return lax.ppermute(value, 'dom', pairs)  15 us
    pallas_call x1, Pallas kernels, local(): pl.pallas_call(functools.partial(forward_kernel, size), in_specs=[SMEM, V...  13.7 us
    pallas_call x1, Pallas kernels, local(): pl.pallas_call(functools.partial(early_kernel, size), in_specs=[VMEM, VME...  9.44 us
    pallas_call x1, Pallas kernels, local(): pl.pallas_call(functools.partial(scatter_kernel, size), in_specs=[SMEM, V...  7.92 us
    all_to_all x1, starting transfers between devices, local(): lax.all_to_all(outgoing.reshape(peers, slots, width), 'dom', split_axis=0...  7.39 us
    pallas_call x1, Pallas kernels, local(): pl.pallas_call(functools.partial(last_kernel, size), in_specs=[VMEM] + [A...  5.63 us
    all_to_all x1, starting transfers between devices, local(): lax.all_to_all(far_grad.reshape(peers, slots, width), 'dom', split_axis=0...  4.88 us
  transfers between devices with their start and end apart: 14, of which 2 were waited for; matrix products, arithmetic and copies ran while one was open for 9% of the time, Pallas kernels for 40%

profile of v6, /device:TPU:0, one launch (start us, length us, event | category | flops | bytes accessed | tf_op | source)
XLA Modules:
  0.0 96.1 jit_solution(4781898239271709282)
XLA Ops:
  0.6 2.1 %halo_rows.1 = bf16[256,512]{1,0:T(8,128)(2,1)} custom-call(s32[1,16,16]{2,1,0:T(8,128)} %rows_ref.3, bf16[512,512]{1,0:T(8,128)(2,1)} %latent_h.5), custom_call_target="tpu_custom_call" | custom-call | flops 134217728 | bytes 786432 | tf_op jit(solution)/shard_map/halo_rows/pallas_call | solution.py:471
  2.7 7.4 %all-to-all-start = ((bf16[16,16,512]{2,1,0:T(8,128)(2,1)}), bf16[16,16,512]{2,1,0:T(8,128)(2,1)S(1)}, u32[]{:S(2)}, u32[]{:S(2)}) async-start(bf16[16,16,512]{2,1,0:T(8,128)(2,1)} %bitcast.106), calls=%async_computation | async-start | bytes 524288 | tf_op jit(solution)/shard_map/all_to_all | solution.py:480
  10.8 0.1 pad_add_fusion.scalar_ref
  10.9 9.4 %edge_early.1.pre_h = f32[2560,512]{1,0:T(8,128)} custom-call(s32[2560]{0:T(1024)} %send_ref.5, s32[2560]{0:T(1024)} %recv_ref.7, bf16[2560,512]{1,0:T(8,128)(2,1)} %edge_h.3, bf16[512,512]{1,0:T(8,128)(2,1)} %latent_h.5, bf16[1536,512]{1,0:T(8,128)(2,1)} %w1_h.7), custom_call_target="tpu_custom_call" | custom-call | flops 4697620480 | bytes 7864320 | tf_op jit(solution)/shard_map/edge_early/pallas_call | solution.py:485
  20.3 0.0 all-to-all-done
  20.4 13.7 %edge_forward.1 = (bf16[2560,512]{1,0:T(8,128)(2,1)}, bf16[2560,512]{1,0:T(8,128)(2,1)}, f32[2560,512]{1,0:T(8,128)}, f32[2,1,1280]{2,1,0:T(1,128)S(1)}, bf16[51...) custom-call(s32[4]{0:T(128)S(1)} %pad_add_fusion.scalar_ref, ...), custom_call_target="tpu_custom_call" | custom-call | flops 8053063680 | bytes 26214400 | tf_op jit(solution)/shard_map/edge_forward/pallas_call | solution.py:508
  34.1 0.5 collective-permute-start
  34.6 15.0 %edge_backward.1 = (bf16[2560,512]{1,0:T(8,128)(2,1)}, f32[4,128,512]{2,1,0:T(8,128)}, bf16[4,128,512]{2,1,0:T(8,128)(2,1)}) custom-call(s32[4]{0:T(128)S(1)} %pad_add_fusion.scalar_ref, s32[2560]{0:T(1024)S(1)} %copy-done.3, f32[2,1,1280]{2,1,0:T(1,128)S(1)} %get-tuple-element.24.inverse_ref, bf16[2560,512]{1,0:T(8,128)(2,1)} %cotan_h.5, ...), custom_call_target="tpu_custom_call" | custom-call | flops 8053063680 | bytes 26214400 | tf_op jit(solution)/shard_map/edge_backward/pallas_call | solution.py:530
  49.6 0.2 collective-permute-start.3
  49.8 0.0 collective-permute-done
  49.8 0.1 fusion.9.order_h
  49.9 2.0 %collective-permute-start.8 = (bf16[4,96,512]{2,1,0:T(8,128)(2,1)S(1)}, bf16[4,96,512]{2,1,0:T(8,128)(2,1)}, u32[]{:S(2)}, u32[]{:S(2)}) collective-permute-start(bf16[4,96,512]{2,1,0:T(8,128)(2,1)S(1)} %fusion.9.order_h), channel_id=1, source_target_pairs={{0,2},{1,3},{2,0},{3,1},{4,6},{5,7},{6,4},{7,5},{8,10},{9,11},{10,... | collective-permute-start | bytes 1179656 | tf_op jit(solution)/shard_map/ppermute | solution.py:394
  51.9 7.9 %edge_scatter.1 = (f32[512,512]{1,0:T(8,128)S(1)}, bf16[256,512]{1,0:T(8,128)(2,1)}, f32[4,128,512]{2,1,0:T(8,128)S(1)}, bf16[4,128,512]{2,1,0:T(8,128)(2,1)}) custom-call(s32[4]{0:T(128)S(1)} %pad_add_fusion.scalar_ref, s32[2560]{0:T(1024)S(1)} %copy-done.4, s32[2560]{0:T(1024)S(1)} %copy-done.3, bf16[2560,512]{1,0:T(8,128)(2,1)} %get-tuple-element.29.pre_h, ...), custom_call_target="tpu_custom_call" | custom-call | flops 6710886400 | bytes 5242880 | tf_op jit(solution)/shard_map/edge_scatter/pallas_call | solution.py:546
  59.8 0.1 collective-permute-start.1
  59.9 0.0 collective-permute-done.3
  59.9 1.2 %fusion.11 = bf16[2,128,512]{2,1,0:T(8,128)(2,1)S(1)} fusion(f32[2,2,128,512]{3,2,1,0:T(8,128)} %bitcast.107, s32[]{:T(128)S(6)} %select_n.38, bf16[2,2,128,512]{3,2,1,0:T(8,128)(2,1)} %bitcast.13), kind=kLoop, calls=%fused_computation.25 | loop fusion | flops 393216 | bytes 1048580 | tf_op jit(solution)/shard_map/convert_element_type | solution.py:407
  61.1 0.9 collective-permute-start.4
  62.0 0.0 collective-permute-done.8
  62.0 1.5 %fusion.1 = f32[4,96,512]{2,1,0:T(8,128)S(1)} fusion(bf16[4,96,512]{2,1,0:T(8,128)(2,1)} %collective-permute-done.8, f32[4,2,96,512]{3,2,1,0:T(8,128)} %bitcast.104, s32[]{:T(128)S(6)} %select_n.39, bf16[4,2,96,512]{3,2,1,0:T(8,128)(2,1)} %bitcast.110), kind=kLoop, calls=%fused_computation.10 | loop fusion | flops 786432 | bytes 2359300 | tf_op jit(solution)/shard_map/add | solution.py:412
  63.5 0.0 copy-start.5
  63.5 0.8 fusion.25
  64.3 2.4 %collective-permute-start.10 = (bf16[96,512]{1,0:T(8,128)(2,1)}, bf16[96,512]{1,0:T(8,128)(2,1)S(1)}, u32[]{:S(2)}, u32[]{:S(2)}) collective-permute-start(bf16[96,512]{1,0:T(8,128)(2,1)} %get-tuple-element.49), channel_id=1, source_target_pairs={{0,8},{1,9},{2,10},{3,11},{4,12},{5,13},{6,14},{7,15},{8,0},{9,1},... | collective-permute-start | bytes 294920 | tf_op jit(solution)/shard_map/ppermute | solution.py:394
  66.7 1.5 %collective-permute-start.11 = (bf16[96,512]{1,0:T(8,128)(2,1)}, bf16[96,512]{1,0:T(8,128)(2,1)}, u32[]{:S(2)}, u32[]{:S(2)}) collective-permute-start(bf16[96,512]{1,0:T(8,128)(2,1)} %get-tuple-element.48), channel_id=1, source_target_pairs={{0,12},{1,13},{2,14},{3,15},{4,0},{5,1},{6,2},{7,3},{8,4},{9,5},{1... | collective-permute-start | bytes 294920 | tf_op jit(solution)/shard_map/ppermute | solution.py:394
  68.1 0.6 collective-permute-start.9
  68.7 0.0 collective-permute-done.1
  68.7 0.8 fusion.10
  69.5 1.2 %collective-permute-start.2 = (bf16[2,128,512]{2,1,0:T(8,128)(2,1)}, bf16[2,128,512]{2,1,0:T(8,128)(2,1)}, u32[]{:S(2)}, u32[]{:S(2)}) collective-permute-start(bf16[2,128,512]{2,1,0:T(8,128)(2,1)} %fusion.10), channel_id=1, source_target_pairs={{0,2},{1,3},{2,0},{3,1},{4,6},{5,7},{6,4},{7,5},{8,10},{9,11},{10,... | collective-permute-start | bytes 786440 | tf_op jit(solution)/shard_map/ppermute | solution.py:394
  70.7 0.0 collective-permute-done.4
  70.7 1.2 %fusion.5 = f32[2,128,512]{2,1,0:T(8,128)S(1)} fusion(bf16[2,128,512]{2,1,0:T(8,128)(2,1)S(1)} %collective-permute-done.4, f32[2,2,128,512]{3,2,1,0:T(8,128)} %bitcast.108, s32[]{:T(128)S(6)} %select_n.39, bf16[2,2,128,512]{3,2,1,0:T(8,128)(2,1)} %bitcast.13), kind=kLoop, calls=%fused_computation.17 | loop fusion | flops 524288 | bytes 1572868 | tf_op jit(solution)/shard_map/add | solution.py:412
  71.9 4.9 %all-to-all-start.1 = ((bf16[16,16,512]{2,1,0:T(8,128)(2,1)}), bf16[16,16,512]{2,1,0:T(8,128)(2,1)S(1)}, u32[]{:S(2)}, u32[]{:S(2)}) async-start(bf16[16,16,512]{2,1,0:T(8,128)(2,1)} %bitcast.17), calls=%async_computation.1 | async-start | bytes 524288 | tf_op jit(solution)/shard_map/all_to_all | solution.py:563
  76.8 0.0 copy-start.1
  76.8 0.0 collective-permute-done.10
  76.8 0.0 collective-permute-done.11
  76.9 0.0 collective-permute-done.9
  76.9 1.8 %fusion.21 = f32[96,512]{1,0:T(8,128)} fusion(bf16[96,512]{1,0:T(8,128)(2,1)} %collective-permute-done.11, bf16[96,512]{1,0:T(8,128)(2,1)S(1)} %collective-permute-done.10, bf16[96,512]{1,0:T(8,128)(2,1)} %collective-permute-done.9, f32[4,96,512]{2,1,0:T(8,128)} %copy-done.5, s32[]{:T(128)S(6)} %select_n.40), kind=kLoop, calls=%fused_computation.37 | loop fusion | flops 294912 | bytes 688132 | tf_op jit(solution)/shard_map/add | solution.py:428
  78.6 0.0 collective-permute-done.2
  78.6 1.1 %fusion.8 = f32[2,128,512]{2,1,0:T(8,128)S(1)} fusion(bf16[2,128,512]{2,1,0:T(8,128)(2,1)} %collective-permute-done.2, f32[2,2,128,512]{3,2,1,0:T(8,128)S(1)} %bitcast.101, s32[]{:T(128)S(6)} %select_n.39, bf16[2,2,128,512]{3,2,1,0:T(8,128)(2,1)S(1)} %bitcast.112), kind=kLoop, calls=%fused_computation.22 | loop fusion | flops 524288 | bytes 1572868 | tf_op jit(solution)/shard_map/add | solution.py:412
  79.7 0.1 fusion.23
  79.8 2.0 %collective-permute-start.5 = (bf16[128,512]{1,0:T(8,128)(2,1)S(1)}, bf16[128,512]{1,0:T(8,128)(2,1)S(1)}, u32[]{:S(2)}, u32[]{:S(2)}) collective-permute-start(bf16[128,512]{1,0:T(8,128)(2,1)S(1)} %get-tuple-element.44), channel_id=1, source_target_pairs={{0,4},{1,5},{2,6},{3,7},{4,8},{5,9},{6,10},{7,11},{8,12},{9,13},{1... | collective-permute-start | bytes 393224 | tf_op jit(solution)/shard_map/ppermute | solution.py:394
  81.8 2.4 %collective-permute-start.6 = (bf16[128,512]{1,0:T(8,128)(2,1)S(1)}, bf16[128,512]{1,0:T(8,128)(2,1)S(1)}, u32[]{:S(2)}, u32[]{:S(2)}) collective-permute-start(bf16[128,512]{1,0:T(8,128)(2,1)S(1)} %get-tuple-element.45), channel_id=1, source_target_pairs={{0,8},{1,9},{2,10},{3,11},{4,12},{5,13},{6,14},{7,15},{8,0},{9,1},... | collective-permute-start | bytes 393224 | tf_op jit(solution)/shard_map/ppermute | solution.py:394
  84.2 1.5 %collective-permute-start.7 = (bf16[128,512]{1,0:T(8,128)(2,1)S(1)}, bf16[128,512]{1,0:T(8,128)(2,1)S(1)}, u32[]{:S(2)}, u32[]{:S(2)}) collective-permute-start(bf16[128,512]{1,0:T(8,128)(2,1)S(1)} %get-tuple-element.46), channel_id=1, source_target_pairs={{0,12},{1,13},{2,14},{3,15},{4,0},{5,1},{6,2},{7,3},{8,4},{9,5},{1... | collective-permute-start | bytes 393224 | tf_op jit(solution)/shard_map/ppermute | solution.py:394
  85.6 0.1 fusion.15
  85.7 1.6 %all-to-all-done.1 = bf16[16,16,512]{2,1,0:T(8,128)(2,1)S(1)} async-done(((bf16[16,16,512]{2,1,0:T(8,128)(2,1)}), bf16[16,16,512]{2,1,0:T(8,128)(2,1)S(1)}, u32[]{:S(2)}, u32[]{:S(2)}) %all-to-all-start.1) | async-done | bytes 262176 | tf_op jit(solution)/shard_map/all_to_all | solution.py:563
  87.3 5.6 %last_grads.1 = (bf16[2560,512]{1,0:T(8,128)(2,1)}, f32[512,512]{1,0:T(8,128)}) custom-call(s32[1,16,16]{2,1,0:T(8,128)S(1)} %copy-done.1, bf16[2560,512]{1,0:T(8,128)(2,1)} %cotan_h.5, bf16[2560,512]{1,0:T(8,128)(2,1)} %get-tuple-element.29.pre_h, bf16[1536,512]{1,0:T(8,128)(2,1)} %w1_h.7, bf16[256,512]{1,0:T(8,128)(2,1)S(1)} %bitcast.99, ...), custom_call_target="tpu_custom_call" | custom-call | flops 2013265920 | bytes 7864320 | tf_op jit(solution)/shard_map/last_grads/pallas_call | solution.py:568
  93.0 0.0 collective-permute-done.5
  93.0 2.4 %collective-permute-done.6 = bf16[128,512]{1,0:T(8,128)(2,1)S(1)} collective-permute-done((bf16[128,512]{1,0:T(8,128)(2,1)S(1)}, bf16[128,512]{1,0:T(8,128)(2,1)S(1)}, u32[]{:S(2)}, u32[]{:S(2)}) %collective-permute-start.6) | collective-permute-done | bytes 131104 | tf_op jit(solution)/shard_map/ppermute | solution.py:394
  95.4 0.0 collective-permute-done.7
  95.4 0.8 convert_add_fusion
  (14 shorter events, 0.0 us)
Async XLA Ops:
  2.7 17.6 %all-to-all-start = ((bf16[16,16,512]{2,1,0:T(8,128)(2,1)}), bf16[16,16,512]{2,1,0:T(8,128)(2,1)S(1)}, u32[]{:S(2)}, u32[]{:S(2)}) async-start(bf16[16,16,512]{2,1,0:T(8,128)(2,1)} %bitcast.106), calls=%async_computation | async-start | bytes 524288 | tf_op jit(solution)/shard_map/all_to_all | solution.py:480
  10.9 9.5 %copy-start = (bf16[512,512]{1,0:T(8,128)(2,1)S(1)}, bf16[512,512]{1,0:T(8,128)(2,1)}, u32[]{:S(2)}) copy-start(bf16[512,512]{1,0:T(8,128)(2,1)} %latent_h.5) | copy-start | bytes 1572868
  10.9 9.5 %copy-start.2 = (bf16[512,512]{1,0:T(8,128)(2,1)S(1)}, bf16[512,512]{1,0:T(8,128)(2,1)}, u32[]{:S(2)}) copy-start(bf16[512,512]{1,0:T(8,128)(2,1)} %w2_h.3) | copy-start | bytes 1572868
  10.9 9.5 %copy-start.3 = (s32[2560]{0:T(1024)S(1)}, s32[2560]{0:T(1024)}, u32[]{:S(2)}) copy-start(s32[2560]{0:T(1024)} %recv_ref.7) | copy-start | bytes 30724
  10.9 9.5 %copy-start.4 = (s32[2560]{0:T(1024)S(1)}, s32[2560]{0:T(1024)}, u32[]{:S(2)}) copy-start(s32[2560]{0:T(1024)} %send_ref.5) | copy-start | bytes 30724
  34.1 15.6 %collective-permute-start = (bf16[8,96,512]{2,1,0:T(8,128)(2,1)}, bf16[8,96,512]{2,1,0:T(8,128)(2,1)S(1)}, u32[]{:S(2)}, u32[]{:S(2)}) collective-permute-start(bf16[8,96,512]{2,1,0:T(8,128)(2,1)} %get-tuple-element.32), channel_id=1, source_target_pairs={{0,1},{1,0},{2,3},{3,2},{4,5},{5,4},{6,7},{7,6},{8,9},{9,8},{10,11... | collective-permute-start | bytes 2359304 | tf_op jit(solution)/shard_map/ppermute | solution.py:394
  34.6 15.2 %copy-start.6 = (f32[8,96,512]{2,1,0:T(8,128)S(1)}, f32[8,96,512]{2,1,0:T(8,128)}, u32[]{:S(2)}) copy-start(f32[8,96,512]{2,1,0:T(8,128)} %get-tuple-element.31) | copy-start | bytes 4718596
  49.6 10.3 %collective-permute-start.3 = (bf16[4,128,512]{2,1,0:T(8,128)(2,1)}, bf16[4,128,512]{2,1,0:T(8,128)(2,1)}, u32[]{:S(2)}, u32[]{:S(2)}) collective-permute-start(bf16[4,128,512]{2,1,0:T(8,128)(2,1)} %get-tuple-element.36), channel_id=1, source_target_pairs={{0,1},{1,0},{2,3},{3,2},{4,5},{5,4},{6,7},{7,6},{8,9},{9,8},{10,11... | collective-permute-start | bytes 1572872 | tf_op jit(solution)/shard_map/ppermute | solution.py:394
  49.8 2.1 %copy-start.7 = (bf16[8,96,512]{2,1,0:T(8,128)(2,1)}, bf16[8,96,512]{2,1,0:T(8,128)(2,1)S(1)}, u32[]{:S(2)}) copy-start(bf16[8,96,512]{2,1,0:T(8,128)(2,1)S(1)} %collective-permute-done) | copy-start | bytes 2359300
  49.9 12.1 %collective-permute-start.8 = (bf16[4,96,512]{2,1,0:T(8,128)(2,1)S(1)}, bf16[4,96,512]{2,1,0:T(8,128)(2,1)}, u32[]{:S(2)}, u32[]{:S(2)}) collective-permute-start(bf16[4,96,512]{2,1,0:T(8,128)(2,1)S(1)} %fusion.9.order_h), channel_id=1, source_target_pairs={{0,2},{1,3},{2,0},{3,1},{4,6},{5,7},{6,4},{7,5},{8,10},{9,11},{10,... | collective-permute-start | bytes 1179656 | tf_op jit(solution)/shard_map/ppermute | solution.py:394
  59.8 8.9 %collective-permute-start.1 = (bf16[4,128,512]{2,1,0:T(8,128)(2,1)}, bf16[4,128,512]{2,1,0:T(8,128)(2,1)S(1)}, u32[]{:S(2)}, u32[]{:S(2)}) collective-permute-start(bf16[4,128,512]{2,1,0:T(8,128)(2,1)} %get-tuple-element.34), channel_id=1, source_target_pairs={{0,1},{1,0},{2,3},{3,2},{4,5},{5,4},{6,7},{7,6},{8,9},{9,8},{10,11... | collective-permute-start | bytes 1572872 | tf_op jit(solution)/shard_map/ppermute | solution.py:394
  61.1 9.6 %collective-permute-start.4 = (bf16[2,128,512]{2,1,0:T(8,128)(2,1)S(1)}, bf16[2,128,512]{2,1,0:T(8,128)(2,1)S(1)}, u32[]{:S(2)}, u32[]{:S(2)}) collective-permute-start(bf16[2,128,512]{2,1,0:T(8,128)(2,1)S(1)} %fusion.11), channel_id=1, source_target_pairs={{0,2},{1,3},{2,0},{3,1},{4,6},{5,7},{6,4},{7,5},{8,10},{9,11},{10,... | collective-permute-start | bytes 786440 | tf_op jit(solution)/shard_map/ppermute | solution.py:394
  63.5 7.2 %copy-start.5 = (f32[4,96,512]{2,1,0:T(8,128)}, f32[4,96,512]{2,1,0:T(8,128)S(1)}, u32[]{:S(2)}) copy-start(f32[4,96,512]{2,1,0:T(8,128)S(1)} %fusion.1) | copy-start | bytes 2359300
  64.3 12.5 %collective-permute-start.10 = (bf16[96,512]{1,0:T(8,128)(2,1)}, bf16[96,512]{1,0:T(8,128)(2,1)S(1)}, u32[]{:S(2)}, u32[]{:S(2)}) collective-permute-start(bf16[96,512]{1,0:T(8,128)(2,1)} %get-tuple-element.49), channel_id=1, source_target_pairs={{0,8},{1,9},{2,10},{3,11},{4,12},{5,13},{6,14},{7,15},{8,0},{9,1},... | collective-permute-start | bytes 294920 | tf_op jit(solution)/shard_map/ppermute | solution.py:394
  66.7 10.2 %collective-permute-start.11 = (bf16[96,512]{1,0:T(8,128)(2,1)}, bf16[96,512]{1,0:T(8,128)(2,1)}, u32[]{:S(2)}, u32[]{:S(2)}) collective-permute-start(bf16[96,512]{1,0:T(8,128)(2,1)} %get-tuple-element.48), channel_id=1, source_target_pairs={{0,12},{1,13},{2,14},{3,15},{4,0},{5,1},{6,2},{7,3},{8,4},{9,5},{1... | collective-permute-start | bytes 294920 | tf_op jit(solution)/shard_map/ppermute | solution.py:394
  68.1 8.7 %collective-permute-start.9 = (bf16[96,512]{1,0:T(8,128)(2,1)}, bf16[96,512]{1,0:T(8,128)(2,1)}, u32[]{:S(2)}, u32[]{:S(2)}) collective-permute-start(bf16[96,512]{1,0:T(8,128)(2,1)} %get-tuple-element.47), channel_id=1, source_target_pairs={{0,4},{1,5},{2,6},{3,7},{4,8},{5,9},{6,10},{7,11},{8,12},{9,13},{1... | collective-permute-start | bytes 294920 | tf_op jit(solution)/shard_map/ppermute | solution.py:394
  69.5 9.1 %collective-permute-start.2 = (bf16[2,128,512]{2,1,0:T(8,128)(2,1)}, bf16[2,128,512]{2,1,0:T(8,128)(2,1)}, u32[]{:S(2)}, u32[]{:S(2)}) collective-permute-start(bf16[2,128,512]{2,1,0:T(8,128)(2,1)} %fusion.10), channel_id=1, source_target_pairs={{0,2},{1,3},{2,0},{3,1},{4,6},{5,7},{6,4},{7,5},{8,10},{9,11},{10,... | collective-permute-start | bytes 786440 | tf_op jit(solution)/shard_map/ppermute | solution.py:394
  71.9 15.4 %all-to-all-start.1 = ((bf16[16,16,512]{2,1,0:T(8,128)(2,1)}), bf16[16,16,512]{2,1,0:T(8,128)(2,1)S(1)}, u32[]{:S(2)}, u32[]{:S(2)}) async-start(bf16[16,16,512]{2,1,0:T(8,128)(2,1)} %bitcast.17), calls=%async_computation.1 | async-start | bytes 524288 | tf_op jit(solution)/shard_map/all_to_all | solution.py:563
  76.8 10.5 %copy-start.1 = (s32[1,16,16]{2,1,0:T(8,128)S(1)}, s32[1,16,16]{2,1,0:T(8,128)}, u32[]{:S(2)}) copy-start(s32[1,16,16]{2,1,0:T(8,128)} %rows_ref.3) | copy-start | bytes 3076
  79.8 13.1 %collective-permute-start.5 = (bf16[128,512]{1,0:T(8,128)(2,1)S(1)}, bf16[128,512]{1,0:T(8,128)(2,1)S(1)}, u32[]{:S(2)}, u32[]{:S(2)}) collective-permute-start(bf16[128,512]{1,0:T(8,128)(2,1)S(1)} %get-tuple-element.44), channel_id=1, source_target_pairs={{0,4},{1,5},{2,6},{3,7},{4,8},{5,9},{6,10},{7,11},{8,12},{9,13},{1... | collective-permute-start | bytes 393224 | tf_op jit(solution)/shard_map/ppermute | solution.py:394
  81.8 13.5 %collective-permute-start.6 = (bf16[128,512]{1,0:T(8,128)(2,1)S(1)}, bf16[128,512]{1,0:T(8,128)(2,1)S(1)}, u32[]{:S(2)}, u32[]{:S(2)}) collective-permute-start(bf16[128,512]{1,0:T(8,128)(2,1)S(1)} %get-tuple-element.45), channel_id=1, source_target_pairs={{0,8},{1,9},{2,10},{3,11},{4,12},{5,13},{6,14},{7,15},{8,0},{9,1},... | collective-permute-start | bytes 393224 | tf_op jit(solution)/shard_map/ppermute | solution.py:394
  84.2 11.2 %collective-permute-start.7 = (bf16[128,512]{1,0:T(8,128)(2,1)S(1)}, bf16[128,512]{1,0:T(8,128)(2,1)S(1)}, u32[]{:S(2)}, u32[]{:S(2)}) collective-permute-start(bf16[128,512]{1,0:T(8,128)(2,1)S(1)} %get-tuple-element.46), channel_id=1, source_target_pairs={{0,12},{1,13},{2,14},{3,15},{4,0},{5,1},{6,2},{7,3},{8,4},{9,5},{1... | collective-permute-start | bytes 393224 | tf_op jit(solution)/shard_map/ppermute | solution.py:394
